TPU v7x, 256 devices: a whole 4x4x8 slice. The times are simulated.
256 devices in a mesh: leaf: 64 (over z, x, core), sub: 4 (over y).
Axes of the slice: x: 4, y: 4, z: 8, core: 2. Of those that a mesh axis runs over, the one named last changes fastest.
Arguments:
- vectors: bfloat16 [32, 262144], P(None, ('leaf', 'sub')), may hold values from -6 to 6
- right_side: bfloat16 [32, 262144], P(None, ('leaf', 'sub')), may hold values from -6 to 6
- tree_order: int32 [256, 1024], P(('leaf', 'sub')), may hold values from 0 to 1023, each once within a row
- live_counts: int32 [256], P(('leaf', 'sub')), may hold values from 1 to 1024, 196608 in all
- leaf_block: bfloat16 [262144, 1024], P(('leaf', 'sub')), may hold values from -0.1875 to 0.1875
- left_basis: bfloat16 [8, 262144, 128], P(None, ('leaf', 'sub')), may hold values from -0.5 to 0.5
- right_level_bases: bfloat16 [8, 262144, 128], P(None, ('leaf', 'sub')), may hold values from -0.1875 to 0.1875
- coupling: bfloat16 [256, 8, 256, 128], P(('leaf', 'sub')), may hold values from -0.375 to 0.375
Outputs:
- product: float32 [32, 262144], P(None, ('leaf', 'sub'))
- solution: float32 [32, 262144], P(None, ('leaf', 'sub'))
Inputs may be any that keep to these rules, and one draw needn't show every extreme that they name: `tree_order`: each row is a permutation of 0 to 1023. `live_counts`: the counts sum to 196608, the largest is exactly 1024.
All inputs are finite; a program needn't handle non-finite values. No bound on the sum of `live_counts` on one device may be relied on, other than what follows from the above.
Results may differ from a plain program's by a relative error of at most 0.028.
Values may be sent and summed in bfloat16 or wider, within the bound.
No kernel may reach another device: no remote copies, remote signals or barrier semaphores. Data moves between devices by JAX's collectives and lax.ppermute only.
A program may use at most 64 MiB of HBM per device.

v0:
```python
import jax
import jax.numpy as jnp
from jax import lax
from jax.sharding import PartitionSpec as P


def partner_2(block, axis, apart):
    count = lax.axis_size(axis)
    route = []
    for low in range(count):
        high = low | 1 << apart
        if high != low and high < count:
            route += [(low, high), (high, low)]
    return lax.ppermute(block, axis, route)


def product_swap(values_in, tree_bit, sub_bits):
    if tree_bit < sub_bits:
        return partner_2(values_in.astype(jnp.bfloat16), "sub", tree_bit).astype(values_in.dtype)
    return partner_2(values_in.astype(jnp.bfloat16), "leaf", tree_bit - sub_bits).astype(
        values_in.dtype
    )


def solve_swap(values_in, tree_bit, sub_bits):
    if tree_bit < sub_bits:
        return partner_2(values_in, "sub", tree_bit)
    return partner_2(values_in, "leaf", tree_bit - sub_bits)


def pair_swap(values_in, tree_bit, sub_bits):
    if tree_bit < sub_bits:
        return partner_2(values_in, "sub", tree_bit)
    return partner_2(values_in, "leaf", tree_bit - sub_bits)


def twofold_partner(mine_sum, tree_height, sub_bits):
    for tree_bit in range(tree_height):
        mine_sum = mine_sum + solve_swap(mine_sum, tree_bit, sub_bits)
    mine_round = mine_sum.astype(jnp.bfloat16)
    return (mine_round, pair_swap(mine_round, tree_height, sub_bits))


def per_device(
    vectors,
    right_side,
    tree_order,
    live_counts,
    leaf_block,
    left_basis,
    right_level_bases,
    coupling,
):
    levels = left_basis.shape[0]
    sub_bits = lax.axis_size("sub").bit_length() - 1
    leaf_order = tree_order[0]
    inverse = jnp.argsort(leaf_order)
    live_mask = lax.broadcasted_iota(jnp.int32, (1, leaf_order.shape[0]), 1) < live_counts[0]
    tree_x = jnp.where(
        live_mask, jnp.take(vectors, leaf_order, axis=1), jnp.zeros((), jnp.bfloat16)
    )
    level_scale = jnp.asarray(
        [2.0 ** (-0.5 * level_now) for level_now in range(levels)], jnp.float32
    )
    carried = jnp.einsum(
        "vp,lpr->lvr", tree_x, right_level_bases, preferred_element_type=jnp.float32
    )
    carried = carried * level_scale[:, None, None]
    siblings = []
    for tree_height in range(levels - 1):
        partner = product_swap(carried, tree_height, sub_bits)
        siblings.append(partner[0].astype(jnp.bfloat16))
        carried = carried[1:] + partner[1:]
    top_round = carried[0].astype(jnp.bfloat16)
    siblings.append(partner_2(top_round, "leaf", levels - 1 - sub_bits))
    stacked = jnp.stack(siblings)
    total = jnp.einsum("vq,pq->vp", tree_x, leaf_block, preferred_element_type=jnp.float32)
    total = total + jnp.einsum(
        "lvr,lpr->vp", stacked, left_basis, preferred_element_type=jnp.float32
    )
    total = jnp.where(live_mask, total, jnp.float32(0.0))
    product = jnp.take(total, inverse, axis=1)
    state = jnp.where(
        live_mask, jnp.take(right_side, leaf_order, axis=1).astype(jnp.float32), jnp.float32(0.0)
    )
    for tree_height in range(levels):
        factor = 2.0 ** (-0.5 * tree_height)
        mine_sum = (
            jnp.dot(
                state.astype(jnp.bfloat16),
                right_level_bases[tree_height],
                preferred_element_type=jnp.float32,
            )
            * factor
        )
        mine_round, other_round = twofold_partner(mine_sum, tree_height, sub_bits)
        merged_result = jnp.concatenate([mine_round, other_round], axis=1)
        linked_result = jnp.dot(
            merged_result, coupling[0, tree_height], preferred_element_type=jnp.float32
        ).astype(jnp.bfloat16)
        update = jnp.einsum(
            "vr,pr->vp", linked_result, left_basis[tree_height], preferred_element_type=jnp.float32
        )
        state = jnp.where(live_mask, state - update, jnp.float32(0.0))
    solution = jnp.take(state, inverse, axis=1)
    return (product, solution)


def solution(mesh):
    placed = (
        P(None, ("leaf", "sub")),
        P(None, ("leaf", "sub")),
        P(("leaf", "sub"), None),
        P(("leaf", "sub")),
        P(("leaf", "sub"), None),
        P(None, ("leaf", "sub"), None),
        P(None, ("leaf", "sub"), None),
        P(("leaf", "sub"), None, None, None),
    )
    return jax.shard_map(
        per_device,
        mesh=mesh,
        in_specs=placed,
        out_specs=(P(None, ("leaf", "sub")), P(None, ("leaf", "sub"))),
        check_vma=False,
    )
```

profile of v0, /device:TPU:32, one launch (start us, length us, event | category | flops | bytes accessed | tf_op | source)
XLA Modules:
  0.0 187.6 jit_solution(10530092155322117190)
XLA Ops:
  3.9 3.2 %gather_fusion.2 = bf16[1024,32]{1,0:T(8,128)(2,1)S(1)} fusion(bf16[32,1024]{0,1:T(8,128)(2,1)S(1)} %copy.14, s32[1024]{0:T(1024)S(1)} %fusion.144), kind=kCustom, calls=%fused_computation.2.clone | custom fusion | bytes 135168 | tf_op jit(solution)/shard_map/jit(_take)/gather | solution.py:84
  18.3 3.3 %collective-permute-start.10 = (bf16[32,128]{1,0:T(8,128)(2,1)S(1)}, bf16[32,128]{1,0:T(8,128)(2,1)S(1)}, u32[]{:S(2)}, u32[]{:S(2)}) collective-permute-start(bf16[32,128]{1,0:T(8,128)(2,1)S(1)} %add_convert_fusion.6), channel_id=1, source_target_pairs={{0,2},{2,0},{1,3},{3,1},{4,6},{6,4},{5,7},{7,5},{8,10},{10,8},{9,1... | collective-permute-start | bytes 24584 | tf_op jit(solution)/shard_map/ppermute | solution.py:14
  27.5 2.2 %collective-permute-done.11 = f32[32,128]{1,0:T(8,128)S(1)} collective-permute-done((f32[32,128]{1,0:T(8,128)S(1)}, f32[32,128]{1,0:T(8,128)S(1)}, u32[]{:S(2)}, u32[]{:S(2)}) %collective-permute-start.11) | collective-permute-done | bytes 16416 | tf_op jit(solution)/shard_map/ppermute | solution.py:14
  29.7 3.2 %collective-permute-start.12 = (f32[32,128]{1,0:T(8,128)S(1)}, f32[32,128]{1,0:T(8,128)S(1)}, u32[]{:S(2)}, u32[]{:S(2)}) collective-permute-start(f32[32,128]{1,0:T(8,128)S(1)} %add.129), channel_id=1, source_target_pairs={{0,2},{2,0},{1,3},{3,1},{4,6},{6,4},{5,7},{7,5},{8,10},{10,8},{9,1... | collective-permute-start | bytes 49160 | tf_op jit(solution)/shard_map/ppermute | solution.py:14
  42.4 3.2 %collective-permute-start.15 = (f32[32,128]{1,0:T(8,128)S(1)}, f32[32,128]{1,0:T(8,128)S(1)}, u32[]{:S(2)}, u32[]{:S(2)}) collective-permute-start(f32[32,128]{1,0:T(8,128)S(1)} %add.131), channel_id=1, source_target_pairs={{0,2},{2,0},{1,3},{3,1},{4,6},{6,4},{5,7},{7,5},{8,10},{10,8},{9,1... | collective-permute-start | bytes 49160 | tf_op jit(solution)/shard_map/ppermute | solution.py:14
  58.7 3.2 %collective-permute-start.19 = (f32[32,128]{1,0:T(8,128)S(1)}, f32[32,128]{1,0:T(8,128)S(1)}, u32[]{:S(2)}, u32[]{:S(2)}) collective-permute-start(f32[32,128]{1,0:T(8,128)S(1)} %add.134), channel_id=1, source_target_pairs={{0,2},{2,0},{1,3},{3,1},{4,6},{6,4},{5,7},{7,5},{8,10},{10,8},{9,1... | collective-permute-start | bytes 49160 | tf_op jit(solution)/shard_map/ppermute | solution.py:14
  66.6 2.2 %collective-permute-done.21 = f32[32,128]{1,0:T(8,128)S(1)} collective-permute-done((f32[32,128]{1,0:T(8,128)S(1)}, f32[32,128]{1,0:T(8,128)S(1)}, u32[]{:S(2)}, u32[]{:S(2)}) %collective-permute-start.21) | collective-permute-done | bytes 16416 | tf_op jit(solution)/shard_map/ppermute | solution.py:14
  68.8 3.0 %collective-permute-start.22 = (bf16[32,128]{1,0:T(8,128)(2,1)S(1)}, bf16[32,128]{1,0:T(8,128)(2,1)S(1)}, u32[]{:S(2)}, u32[]{:S(2)}) collective-permute-start(bf16[32,128]{1,0:T(8,128)(2,1)S(1)} %add_convert_fusion.3), channel_id=1, source_target_pairs={{0,16},{16,0},{4,20},{20,4},{8,24},{24,8},{12,28},{28,12},{32,48},... | collective-permute-start | bytes 24584 | tf_op jit(solution)/shard_map/ppermute | solution.py:14
  78.2 3.2 %gather_fusion = bf16[1024,32]{1,0:T(8,128)(2,1)S(1)} fusion(bf16[32,1024]{0,1:T(8,128)(2,1)S(1)} %copy.11, s32[1024]{0:T(1024)S(1)} %fusion.144), kind=kCustom, calls=%fused_computation.clone | custom fusion | bytes 135168 | tf_op jit(solution)/shard_map/jit(_take)/gather | solution.py:60
  81.5 3.0 %collective-permute-start.24 = (f32[32,128]{1,0:T(8,128)S(1)}, f32[32,128]{1,0:T(8,128)S(1)}, u32[]{:S(2)}, u32[]{:S(2)}) collective-permute-start(f32[32,128]{1,0:T(8,128)S(1)} %add.138), channel_id=1, source_target_pairs={{0,2},{2,0},{1,3},{3,1},{4,6},{6,4},{5,7},{7,5},{8,10},{10,8},{9,1... | collective-permute-start | bytes 49160 | tf_op jit(solution)/shard_map/ppermute | solution.py:14
  87.8 4.4 %sort.17 = (s32[1024]{0:T(1024)}, s32[1024]{0:T(1024)S(1)}) sort(s32[1024]{0:T(1024)S(1)} %bitcast.124, s32[1024]{0:T(1024)S(1)} %iota.11), dimensions={0}, to_apply=%region_0.2 | sort | flops 10240 | bytes 16384 | tf_op jit(solution)/shard_map/jit(argsort)/sort | solution.py:57
  93.8 2.2 %collective-permute-done.26 = f32[32,128]{1,0:T(8,128)S(1)} collective-permute-done((f32[32,128]{1,0:T(8,128)S(1)}, f32[32,128]{1,0:T(8,128)S(1)}, u32[]{:S(2)}, u32[]{:S(2)}) %collective-permute-start.26) | collective-permute-done | bytes 16416 | tf_op jit(solution)/shard_map/ppermute | solution.py:14
  96.0 3.0 %collective-permute-start.27 = (f32[32,128]{1,0:T(8,128)S(1)}, f32[32,128]{1,0:T(8,128)S(1)}, u32[]{:S(2)}, u32[]{:S(2)}) collective-permute-start(f32[32,128]{1,0:T(8,128)S(1)} %add.141), channel_id=1, source_target_pairs={{0,16},{16,0},{4,20},{20,4},{8,24},{24,8},{12,28},{28,12},{32,48},... | collective-permute-start | bytes 49160 | tf_op jit(solution)/shard_map/ppermute | solution.py:14
  99.0 2.2 %collective-permute-done.27 = f32[32,128]{1,0:T(8,128)S(1)} collective-permute-done((f32[32,128]{1,0:T(8,128)S(1)}, f32[32,128]{1,0:T(8,128)S(1)}, u32[]{:S(2)}, u32[]{:S(2)}) %collective-permute-start.27) | collective-permute-done | bytes 16416 | tf_op jit(solution)/shard_map/ppermute | solution.py:14
  101.5 3.3 %collective-permute-start.1 = (bf16[7,32,128]{2,1,0:T(8,128)(2,1)S(1)}, bf16[7,32,128]{2,1,0:T(8,128)(2,1)S(1)}, u32[]{:S(2)}, u32[]{:S(2)}) collective-permute-start(bf16[7,32,128]{2,1,0:T(8,128)(2,1)S(1)} %get-tuple-element.18), channel_id=1, source_target_pairs={{0,2},{2,0},{1,3},{3,1},{4,6},{6,4},{5,7},{7,5},{8,10},{10,8},{9,1... | collective-permute-start | bytes 172040 | tf_op jit(solution)/shard_map/ppermute | solution.py:14
  111.1 2.7 %collective-permute-start.30 = (f32[32,128]{1,0:T(8,128)S(1)}, f32[32,128]{1,0:T(8,128)S(1)}, u32[]{:S(2)}, u32[]{:S(2)}) collective-permute-start(f32[32,128]{1,0:T(8,128)S(1)} %add.143), channel_id=1, source_target_pairs={{0,2},{2,0},{1,3},{3,1},{4,6},{6,4},{5,7},{7,5},{8,10},{10,8},{9,1... | collective-permute-start | bytes 49160 | tf_op jit(solution)/shard_map/ppermute | solution.py:14
  113.9 2.4 %collective-permute-done.30 = f32[32,128]{1,0:T(8,128)S(1)} collective-permute-done((f32[32,128]{1,0:T(8,128)S(1)}, f32[32,128]{1,0:T(8,128)S(1)}, u32[]{:S(2)}, u32[]{:S(2)}) %collective-permute-start.30) | collective-permute-done | bytes 16416 | tf_op jit(solution)/shard_map/ppermute | solution.py:14
  121.3 3.0 %collective-permute-start.33 = (f32[32,128]{1,0:T(8,128)S(1)}, f32[32,128]{1,0:T(8,128)S(1)}, u32[]{:S(2)}, u32[]{:S(2)}) collective-permute-start(f32[32,128]{1,0:T(8,128)S(1)} %add.146), channel_id=1, source_target_pairs={{0,16},{16,0},{4,20},{20,4},{8,24},{24,8},{12,28},{28,12},{32,48},... | collective-permute-start | bytes 49160 | tf_op jit(solution)/shard_map/ppermute | solution.py:14
  124.3 2.2 %collective-permute-done.33 = f32[32,128]{1,0:T(8,128)S(1)} collective-permute-done((f32[32,128]{1,0:T(8,128)S(1)}, f32[32,128]{1,0:T(8,128)S(1)}, u32[]{:S(2)}, u32[]{:S(2)}) %collective-permute-start.33) | collective-permute-done | bytes 16416 | tf_op jit(solution)/shard_map/ppermute | solution.py:14
  127.8 3.1 %collective-permute-start.4 = (bf16[4,32,128]{2,1,0:T(8,128)(2,1)S(1)}, bf16[4,32,128]{2,1,0:T(8,128)(2,1)S(1)}, u32[]{:S(2)}, u32[]{:S(2)}) collective-permute-start(bf16[4,32,128]{2,1,0:T(8,128)(2,1)S(1)} %get-tuple-element.12), channel_id=1, source_target_pairs={{0,16},{16,0},{4,20},{20,4},{8,24},{24,8},{12,28},{28,12},{32,48},... | collective-permute-start | bytes 98312 | tf_op jit(solution)/shard_map/ppermute | solution.py:14
  130.9 3.4 %collective-permute-start.35 = (bf16[32,128]{1,0:T(8,128)(2,1)S(1)}, bf16[32,128]{1,0:T(8,128)(2,1)S(1)}, u32[]{:S(2)}, u32[]{:S(2)}) collective-permute-start(bf16[32,128]{1,0:T(8,128)(2,1)S(1)} %add_convert_fusion.1), channel_id=1, source_target_pairs={{0,64},{64,0},{4,68},{68,4},{8,72},{72,8},{12,76},{76,12},{16,80},... | collective-permute-start | bytes 24584 | tf_op jit(solution)/shard_map/ppermute | solution.py:14
  144.1 3.2 %collective-permute-done.37 = f32[32,128]{1,0:T(8,128)S(1)} collective-permute-done((f32[32,128]{1,0:T(8,128)S(1)}, f32[32,128]{1,0:T(8,128)S(1)}, u32[]{:S(2)}, u32[]{:S(2)}) %collective-permute-start.37) | collective-permute-done | bytes 16416 | tf_op jit(solution)/shard_map/ppermute | solution.py:14
  147.3 3.0 %collective-permute-start.6 = (bf16[2,32,128]{2,1,0:T(8,128)(2,1)S(1)}, bf16[2,32,128]{2,1,0:T(8,128)(2,1)S(1)}, u32[]{:S(2)}, u32[]{:S(2)}) collective-permute-start(bf16[2,32,128]{2,1,0:T(8,128)(2,1)S(1)} %get-tuple-element.8), channel_id=1, source_target_pairs={{0,64},{64,0},{4,68},{68,4},{8,72},{72,8},{12,76},{76,12},{16,80},... | collective-permute-start | bytes 49160 | tf_op jit(solution)/shard_map/ppermute | solution.py:14
  151.5 2.9 %collective-permute-done.39 = f32[32,128]{1,0:T(8,128)S(1)} collective-permute-done((f32[32,128]{1,0:T(8,128)S(1)}, f32[32,128]{1,0:T(8,128)S(1)}, u32[]{:S(2)}, u32[]{:S(2)}) %collective-permute-start.39) | collective-permute-done | bytes 16416 | tf_op jit(solution)/shard_map/ppermute | solution.py:14
  154.4 2.3 %collective-permute-start.40 = (f32[32,128]{1,0:T(8,128)S(1)}, f32[32,128]{1,0:T(8,128)S(1)}, u32[]{:S(2)}, u32[]{:S(2)}) collective-permute-start(f32[32,128]{1,0:T(8,128)S(1)} %add.152), channel_id=1, source_target_pairs={{0,16},{16,0},{4,20},{20,4},{8,24},{24,8},{12,28},{28,12},{32,48},... | collective-permute-start | bytes 49160 | tf_op jit(solution)/shard_map/ppermute | solution.py:14
  156.7 4.8 %collective-permute-start.7 = (bf16[32,128]{1,0:T(8,128)(2,1)S(1)}, bf16[32,128]{1,0:T(8,128)(2,1)S(1)}, u32[]{:S(2)}, u32[]{:S(2)}) collective-permute-start(bf16[32,128]{1,0:T(8,128)(2,1)S(1)} %fusion.143), channel_id=1, source_target_pairs={{0,128},{128,0},{4,132},{132,4},{8,136},{136,8},{12,140},{140,12},... | collective-permute-start | bytes 24584 | tf_op jit(solution)/shard_map/ppermute | solution.py:14
  162.7 2.7 %collective-permute-done.41 = f32[32,128]{1,0:T(8,128)S(1)} collective-permute-done((f32[32,128]{1,0:T(8,128)S(1)}, f32[32,128]{1,0:T(8,128)S(1)}, u32[]{:S(2)}, u32[]{:S(2)}) %collective-permute-start.41) | collective-permute-done | bytes 16416 | tf_op jit(solution)/shard_map/ppermute | solution.py:14
  166.8 3.1 %collective-permute-done.42 = f32[32,128]{1,0:T(8,128)S(1)} collective-permute-done((f32[32,128]{1,0:T(8,128)S(1)}, f32[32,128]{1,0:T(8,128)S(1)}, u32[]{:S(2)}, u32[]{:S(2)}) %collective-permute-start.42) | collective-permute-done | bytes 16416 | tf_op jit(solution)/shard_map/ppermute | solution.py:14
  170.0 2.5 %collective-permute-start.43 = (bf16[32,128]{1,0:T(8,128)(2,1)S(1)}, bf16[32,128]{1,0:T(8,128)(2,1)S(1)}, u32[]{:S(2)}, u32[]{:S(2)}) collective-permute-start(bf16[32,128]{1,0:T(8,128)(2,1)S(1)} %add_convert_fusion), channel_id=1, source_target_pairs={{0,128},{128,0},{4,132},{132,4},{8,136},{136,8},{12,140},{140,12},... | collective-permute-start | bytes 24584 | tf_op jit(solution)/shard_map/ppermute | solution.py:14
  172.5 2.3 %fusion.1 = f32[32,1024]{1,0:T(8,128)S(1)} fusion(f32[32,1024]{1,0:T(8,128)S(1)} %fusion.88, bf16[8,32,128]{2,1,0:T(8,128)(2,1)S(1)} %constant_dynamic-update-slice_fusion, bf16[8,1024,128]{2,1,0:T(8,128)(2,1)} %param.18, pred[1024]{0:T(1024)(128)(4,1)S(1)} %get-tuple-element.24), kind=kOutput, calls=%fused_computation.6 | convolution fusion | flops 67174400 | bytes 2425856 | tf_op jit(solution)/shard_map/lvr,lpr->vp/dot_general | solution.py:78
  175.0 4.0 %gather_fusion.1 = f32[1024,32]{1,0:T(8,128)} fusion(f32[32,1024]{0,1:T(8,128)S(1)} %copy.13, s32[1024]{0:T(1024)S(1)} %fusion.145), kind=kCustom, calls=%fused_computation.1.clone | custom fusion | bytes 266240 | tf_op jit(solution)/shard_map/jit(_take)/gather | solution.py:82
  180.5 4.0 %gather_fusion.3 = f32[1024,32]{1,0:T(8,128)} fusion(f32[32,1024]{0,1:T(8,128)S(1)} %copy.16, s32[1024]{0:T(1024)S(1)} %fusion.145), kind=kCustom, calls=%fused_computation.3.clone | custom fusion | bytes 266240 | tf_op jit(solution)/shard_map/jit(_take)/gather | solution.py:105
  (147 shorter events, 89.2 us)
Async XLA Ops:
  14.4 3.8 %collective-permute-start.9 = (f32[32,128]{1,0:T(8,128)S(1)}, f32[32,128]{1,0:T(8,128)S(1)}, u32[]{:S(2)}, u32[]{:S(2)}) collective-permute-start(f32[32,128]{1,0:T(8,128)S(1)} %convolution_multiply_fusion.7), channel_id=1, source_target_pairs={{0,1},{1,0},{2,3},{3,2},{4,5},{5,4},{6,7},{7,6},{8,9},{9,8},{10,11... | collective-permute-start | bytes 49160 | tf_op jit(solution)/shard_map/ppermute | solution.py:14
  18.3 5.2 %collective-permute-start.10 = (bf16[32,128]{1,0:T(8,128)(2,1)S(1)}, bf16[32,128]{1,0:T(8,128)(2,1)S(1)}, u32[]{:S(2)}, u32[]{:S(2)}) collective-permute-start(bf16[32,128]{1,0:T(8,128)(2,1)S(1)} %add_convert_fusion.6), channel_id=1, source_target_pairs={{0,2},{2,0},{1,3},{3,1},{4,6},{6,4},{5,7},{7,5},{8,10},{10,8},{9,1... | collective-permute-start | bytes 24584 | tf_op jit(solution)/shard_map/ppermute | solution.py:14
  25.9 3.9 %collective-permute-start.11 = (f32[32,128]{1,0:T(8,128)S(1)}, f32[32,128]{1,0:T(8,128)S(1)}, u32[]{:S(2)}, u32[]{:S(2)}) collective-permute-start(f32[32,128]{1,0:T(8,128)S(1)} %convolution_multiply_fusion.6), channel_id=1, source_target_pairs={{0,1},{1,0},{2,3},{3,2},{4,5},{5,4},{6,7},{7,6},{8,9},{9,8},{10,11... | collective-permute-start | bytes 49160 | tf_op jit(solution)/shard_map/ppermute | solution.py:14
  29.7 5.2 %collective-permute-start.12 = (f32[32,128]{1,0:T(8,128)S(1)}, f32[32,128]{1,0:T(8,128)S(1)}, u32[]{:S(2)}, u32[]{:S(2)}) collective-permute-start(f32[32,128]{1,0:T(8,128)S(1)} %add.129), channel_id=1, source_target_pairs={{0,2},{2,0},{1,3},{3,1},{4,6},{6,4},{5,7},{7,5},{8,10},{10,8},{9,1... | collective-permute-start | bytes 49160 | tf_op jit(solution)/shard_map/ppermute | solution.py:14
  38.5 3.8 %collective-permute-start.14 = (f32[32,128]{1,0:T(8,128)S(1)}, f32[32,128]{1,0:T(8,128)S(1)}, u32[]{:S(2)}, u32[]{:S(2)}) collective-permute-start(f32[32,128]{1,0:T(8,128)S(1)} %convolution_multiply_fusion.5), channel_id=1, source_target_pairs={{0,1},{1,0},{2,3},{3,2},{4,5},{5,4},{6,7},{7,6},{8,9},{9,8},{10,11... | collective-permute-start | bytes 49160 | tf_op jit(solution)/shard_map/ppermute | solution.py:14
  42.4 5.2 %collective-permute-start.15 = (f32[32,128]{1,0:T(8,128)S(1)}, f32[32,128]{1,0:T(8,128)S(1)}, u32[]{:S(2)}, u32[]{:S(2)}) collective-permute-start(f32[32,128]{1,0:T(8,128)S(1)} %add.131), channel_id=1, source_target_pairs={{0,2},{2,0},{1,3},{3,1},{4,6},{6,4},{5,7},{7,5},{8,10},{10,8},{9,1... | collective-permute-start | bytes 49160 | tf_op jit(solution)/shard_map/ppermute | solution.py:14
  54.8 3.8 %collective-permute-start.18 = (f32[32,128]{1,0:T(8,128)S(1)}, f32[32,128]{1,0:T(8,128)S(1)}, u32[]{:S(2)}, u32[]{:S(2)}) collective-permute-start(f32[32,128]{1,0:T(8,128)S(1)} %convolution_multiply_fusion.4), channel_id=1, source_target_pairs={{0,1},{1,0},{2,3},{3,2},{4,5},{5,4},{6,7},{7,6},{8,9},{9,8},{10,11... | collective-permute-start | bytes 49160 | tf_op jit(solution)/shard_map/ppermute | solution.py:14
  58.7 5.2 %collective-permute-start.19 = (f32[32,128]{1,0:T(8,128)S(1)}, f32[32,128]{1,0:T(8,128)S(1)}, u32[]{:S(2)}, u32[]{:S(2)}) collective-permute-start(f32[32,128]{1,0:T(8,128)S(1)} %add.134), channel_id=1, source_target_pairs={{0,2},{2,0},{1,3},{3,1},{4,6},{6,4},{5,7},{7,5},{8,10},{10,8},{9,1... | collective-permute-start | bytes 49160 | tf_op jit(solution)/shard_map/ppermute | solution.py:14
  68.8 5.2 %collective-permute-start.22 = (bf16[32,128]{1,0:T(8,128)(2,1)S(1)}, bf16[32,128]{1,0:T(8,128)(2,1)S(1)}, u32[]{:S(2)}, u32[]{:S(2)}) collective-permute-start(bf16[32,128]{1,0:T(8,128)(2,1)S(1)} %add_convert_fusion.3), channel_id=1, source_target_pairs={{0,16},{16,0},{4,20},{20,4},{8,24},{24,8},{12,28},{28,12},{32,48},... | collective-permute-start | bytes 24584 | tf_op jit(solution)/shard_map/ppermute | solution.py:14
  76.3 5.1 %collective-permute-start.23 = (f32[32,128]{1,0:T(8,128)S(1)}, f32[32,128]{1,0:T(8,128)S(1)}, u32[]{:S(2)}, u32[]{:S(2)}) collective-permute-start(f32[32,128]{1,0:T(8,128)S(1)} %convolution_multiply_fusion.3), channel_id=1, source_target_pairs={{0,1},{1,0},{2,3},{3,2},{4,5},{5,4},{6,7},{7,6},{8,9},{9,8},{10,11... | collective-permute-start | bytes 49160 | tf_op jit(solution)/shard_map/ppermute | solution.py:14
  81.5 5.4 %collective-permute-start.24 = (f32[32,128]{1,0:T(8,128)S(1)}, f32[32,128]{1,0:T(8,128)S(1)}, u32[]{:S(2)}, u32[]{:S(2)}) collective-permute-start(f32[32,128]{1,0:T(8,128)S(1)} %add.138), channel_id=1, source_target_pairs={{0,2},{2,0},{1,3},{3,1},{4,6},{6,4},{5,7},{7,5},{8,10},{10,8},{9,1... | collective-permute-start | bytes 49160 | tf_op jit(solution)/shard_map/ppermute | solution.py:14
  86.6 14.9 %collective-permute-start = (bf16[8,32,128]{2,1,0:T(8,128)(2,1)S(1)}, bf16[8,32,128]{2,1,0:T(8,128)(2,1)S(1)}, u32[]{:S(2)}, u32[]{:S(2)}) collective-permute-start(bf16[8,32,128]{2,1,0:T(8,128)(2,1)S(1)} %get-tuple-element.22), channel_id=1, source_target_pairs={{0,1},{1,0},{2,3},{3,2},{4,5},{5,4},{6,7},{7,6},{8,9},{9,8},{10,11... | collective-permute-start | bytes 196616 | tf_op jit(solution)/shard_map/ppermute | solution.py:14
  87.0 5.2 %collective-permute-start.25 = (f32[32,128]{1,0:T(8,128)S(1)}, f32[32,128]{1,0:T(8,128)S(1)}, u32[]{:S(2)}, u32[]{:S(2)}) collective-permute-start(f32[32,128]{1,0:T(8,128)S(1)} %add.139), channel_id=1, source_target_pairs={{0,4},{4,0},{8,12},{12,8},{16,20},{20,16},{24,28},{28,24},{32,36},... | collective-permute-start | bytes 49160 | tf_op jit(solution)/shard_map/ppermute | solution.py:14
  96.0 5.2 %collective-permute-start.27 = (f32[32,128]{1,0:T(8,128)S(1)}, f32[32,128]{1,0:T(8,128)S(1)}, u32[]{:S(2)}, u32[]{:S(2)}) collective-permute-start(f32[32,128]{1,0:T(8,128)S(1)} %add.141), channel_id=1, source_target_pairs={{0,16},{16,0},{4,20},{20,4},{8,24},{24,8},{12,28},{28,12},{32,48},... | collective-permute-start | bytes 49160 | tf_op jit(solution)/shard_map/ppermute | solution.py:14
  101.5 12.3 %collective-permute-start.1 = (bf16[7,32,128]{2,1,0:T(8,128)(2,1)S(1)}, bf16[7,32,128]{2,1,0:T(8,128)(2,1)S(1)}, u32[]{:S(2)}, u32[]{:S(2)}) collective-permute-start(bf16[7,32,128]{2,1,0:T(8,128)(2,1)S(1)} %get-tuple-element.18), channel_id=1, source_target_pairs={{0,2},{2,0},{1,3},{3,1},{4,6},{6,4},{5,7},{7,5},{8,10},{10,8},{9,1... | collective-permute-start | bytes 172040 | tf_op jit(solution)/shard_map/ppermute | solution.py:14
  107.3 3.8 %collective-permute-start.29 = (f32[32,128]{1,0:T(8,128)S(1)}, f32[32,128]{1,0:T(8,128)S(1)}, u32[]{:S(2)}, u32[]{:S(2)}) collective-permute-start(f32[32,128]{1,0:T(8,128)S(1)} %convolution_multiply_fusion.2), channel_id=1, source_target_pairs={{0,1},{1,0},{2,3},{3,2},{4,5},{5,4},{6,7},{7,6},{8,9},{9,8},{10,11... | collective-permute-start | bytes 49160 | tf_op jit(solution)/shard_map/ppermute | solution.py:14
  111.1 5.2 %collective-permute-start.30 = (f32[32,128]{1,0:T(8,128)S(1)}, f32[32,128]{1,0:T(8,128)S(1)}, u32[]{:S(2)}, u32[]{:S(2)}) collective-permute-start(f32[32,128]{1,0:T(8,128)S(1)} %add.143), channel_id=1, source_target_pairs={{0,2},{2,0},{1,3},{3,1},{4,6},{6,4},{5,7},{7,5},{8,10},{10,8},{9,1... | collective-permute-start | bytes 49160 | tf_op jit(solution)/shard_map/ppermute | solution.py:14
  113.8 5.2 %collective-permute-start.2 = (bf16[6,32,128]{2,1,0:T(8,128)(2,1)S(1)}, bf16[6,32,128]{2,1,0:T(8,128)(2,1)S(1)}, u32[]{:S(2)}, u32[]{:S(2)}) collective-permute-start(bf16[6,32,128]{2,1,0:T(8,128)(2,1)S(1)} %get-tuple-element.16), channel_id=1, source_target_pairs={{0,4},{4,0},{8,12},{12,8},{16,20},{20,16},{24,28},{28,24},{32,36},... | collective-permute-start | bytes 147464 | tf_op jit(solution)/shard_map/ppermute | solution.py:14
  119.1 8.7 %collective-permute-start.3 = (bf16[5,32,128]{2,1,0:T(8,128)(2,1)S(1)}, bf16[5,32,128]{2,1,0:T(8,128)(2,1)S(1)}, u32[]{:S(2)}, u32[]{:S(2)}) collective-permute-start(bf16[5,32,128]{2,1,0:T(8,128)(2,1)S(1)} %get-tuple-element.14), channel_id=1, source_target_pairs={{0,8},{8,0},{4,12},{12,4},{16,24},{24,16},{20,28},{28,20},{32,40},... | collective-permute-start | bytes 122888 | tf_op jit(solution)/shard_map/ppermute | solution.py:14
  121.3 5.2 %collective-permute-start.33 = (f32[32,128]{1,0:T(8,128)S(1)}, f32[32,128]{1,0:T(8,128)S(1)}, u32[]{:S(2)}, u32[]{:S(2)}) collective-permute-start(f32[32,128]{1,0:T(8,128)S(1)} %add.146), channel_id=1, source_target_pairs={{0,16},{16,0},{4,20},{20,4},{8,24},{24,8},{12,28},{28,12},{32,48},... | collective-permute-start | bytes 49160 | tf_op jit(solution)/shard_map/ppermute | solution.py:14
  126.5 4.3 %collective-permute-start.34 = (f32[32,128]{1,0:T(8,128)S(1)}, f32[32,128]{1,0:T(8,128)S(1)}, u32[]{:S(2)}, u32[]{:S(2)}) collective-permute-start(f32[32,128]{1,0:T(8,128)S(1)} %add.147), channel_id=1, source_target_pairs={{0,32},{32,0},{4,36},{36,4},{8,40},{40,8},{12,44},{44,12},{16,48},... | collective-permute-start | bytes 49160 | tf_op jit(solution)/shard_map/ppermute | solution.py:14
  127.8 11.7 %collective-permute-start.4 = (bf16[4,32,128]{2,1,0:T(8,128)(2,1)S(1)}, bf16[4,32,128]{2,1,0:T(8,128)(2,1)S(1)}, u32[]{:S(2)}, u32[]{:S(2)}) collective-permute-start(bf16[4,32,128]{2,1,0:T(8,128)(2,1)S(1)} %get-tuple-element.12), channel_id=1, source_target_pairs={{0,16},{16,0},{4,20},{20,4},{8,24},{24,8},{12,28},{28,12},{32,48},... | collective-permute-start | bytes 98312 | tf_op jit(solution)/shard_map/ppermute | solution.py:14
  130.9 5.0 %collective-permute-start.35 = (bf16[32,128]{1,0:T(8,128)(2,1)S(1)}, bf16[32,128]{1,0:T(8,128)(2,1)S(1)}, u32[]{:S(2)}, u32[]{:S(2)}) collective-permute-start(bf16[32,128]{1,0:T(8,128)(2,1)S(1)} %add_convert_fusion.1), channel_id=1, source_target_pairs={{0,64},{64,0},{4,68},{68,4},{8,72},{72,8},{12,76},{76,12},{16,80},... | collective-permute-start | bytes 24584 | tf_op jit(solution)/shard_map/ppermute | solution.py:14
  138.2 3.8 %collective-permute-start.36 = (f32[32,128]{1,0:T(8,128)S(1)}, f32[32,128]{1,0:T(8,128)S(1)}, u32[]{:S(2)}, u32[]{:S(2)}) collective-permute-start(f32[32,128]{1,0:T(8,128)S(1)} %convolution_multiply_fusion.1), channel_id=1, source_target_pairs={{0,1},{1,0},{2,3},{3,2},{4,5},{5,4},{6,7},{7,6},{8,9},{9,8},{10,11... | collective-permute-start | bytes 49160 | tf_op jit(solution)/shard_map/ppermute | solution.py:14
  139.5 7.8 %collective-permute-start.5 = (bf16[3,32,128]{2,1,0:T(8,128)(2,1)S(1)}, bf16[3,32,128]{2,1,0:T(8,128)(2,1)S(1)}, u32[]{:S(2)}, u32[]{:S(2)}) collective-permute-start(bf16[3,32,128]{2,1,0:T(8,128)(2,1)S(1)} %get-tuple-element.10), channel_id=1, source_target_pairs={{0,32},{32,0},{4,36},{36,4},{8,40},{40,8},{12,44},{44,12},{16,48},... | collective-permute-start | bytes 73736 | tf_op jit(solution)/shard_map/ppermute | solution.py:14
  142.1 5.2 %collective-permute-start.37 = (f32[32,128]{1,0:T(8,128)S(1)}, f32[32,128]{1,0:T(8,128)S(1)}, u32[]{:S(2)}, u32[]{:S(2)}) collective-permute-start(f32[32,128]{1,0:T(8,128)S(1)} %add.149), channel_id=1, source_target_pairs={{0,2},{2,0},{1,3},{3,1},{4,6},{6,4},{5,7},{7,5},{8,10},{10,8},{9,1... | collective-permute-start | bytes 49160 | tf_op jit(solution)/shard_map/ppermute | solution.py:14
  147.3 9.4 %collective-permute-start.6 = (bf16[2,32,128]{2,1,0:T(8,128)(2,1)S(1)}, bf16[2,32,128]{2,1,0:T(8,128)(2,1)S(1)}, u32[]{:S(2)}, u32[]{:S(2)}) collective-permute-start(bf16[2,32,128]{2,1,0:T(8,128)(2,1)S(1)} %get-tuple-element.8), channel_id=1, source_target_pairs={{0,64},{64,0},{4,68},{68,4},{8,72},{72,8},{12,76},{76,12},{16,80},... | collective-permute-start | bytes 49160 | tf_op jit(solution)/shard_map/ppermute | solution.py:14
  150.3 4.0 %collective-permute-start.39 = (f32[32,128]{1,0:T(8,128)S(1)}, f32[32,128]{1,0:T(8,128)S(1)}, u32[]{:S(2)}, u32[]{:S(2)}) collective-permute-start(f32[32,128]{1,0:T(8,128)S(1)} %add.151), channel_id=1, source_target_pairs={{0,8},{8,0},{4,12},{12,4},{16,24},{24,16},{20,28},{28,20},{32,40},... | collective-permute-start | bytes 49160 | tf_op jit(solution)/shard_map/ppermute | solution.py:14
  154.4 7.1 %collective-permute-start.40 = (f32[32,128]{1,0:T(8,128)S(1)}, f32[32,128]{1,0:T(8,128)S(1)}, u32[]{:S(2)}, u32[]{:S(2)}) collective-permute-start(f32[32,128]{1,0:T(8,128)S(1)} %add.152), channel_id=1, source_target_pairs={{0,16},{16,0},{4,20},{20,4},{8,24},{24,8},{12,28},{28,12},{32,48},... | collective-permute-start | bytes 49160 | tf_op jit(solution)/shard_map/ppermute | solution.py:14
  156.7 10.1 %collective-permute-start.7 = (bf16[32,128]{1,0:T(8,128)(2,1)S(1)}, bf16[32,128]{1,0:T(8,128)(2,1)S(1)}, u32[]{:S(2)}, u32[]{:S(2)}) collective-permute-start(bf16[32,128]{1,0:T(8,128)(2,1)S(1)} %fusion.143), channel_id=1, source_target_pairs={{0,128},{128,0},{4,132},{132,4},{8,136},{136,8},{12,140},{140,12},... | collective-permute-start | bytes 24584 | tf_op jit(solution)/shard_map/ppermute | solution.py:14
  165.4 4.6 %collective-permute-start.42 = (f32[32,128]{1,0:T(8,128)S(1)}, f32[32,128]{1,0:T(8,128)S(1)}, u32[]{:S(2)}, u32[]{:S(2)}) collective-permute-start(f32[32,128]{1,0:T(8,128)S(1)} %add.154), channel_id=1, source_target_pairs={{0,64},{64,0},{4,68},{68,4},{8,72},{72,8},{12,76},{76,12},{16,80},... | collective-permute-start | bytes 49160 | tf_op jit(solution)/shard_map/ppermute | solution.py:14
  170.0 9.1 %collective-permute-start.43 = (bf16[32,128]{1,0:T(8,128)(2,1)S(1)}, bf16[32,128]{1,0:T(8,128)(2,1)S(1)}, u32[]{:S(2)}, u32[]{:S(2)}) collective-permute-start(bf16[32,128]{1,0:T(8,128)(2,1)S(1)} %add_convert_fusion), channel_id=1, source_target_pairs={{0,128},{128,0},{4,132},{132,4},{8,136},{136,8},{12,140},{140,12},... | collective-permute-start | bytes 24584 | tf_op jit(solution)/shard_map/ppermute | solution.py:14
  (17 other events, 256.4 us)
where the time goes:
time: 189 us; the launch traced here: 188 us
  starting transfers between devices  78.9 us (42%)
  waiting for transfers between devices  57.6 us (30%)
  matrix products  23.8 us (13%)
  local copies, waits for them, and re-layouts  18.1 us (10%)
  other arithmetic  7.39 us (4%)
    ppermute x44, starting transfers between devices, partner_2(): return lax.ppermute(block, axis, route)  78.9 us
    ppermute x44, waiting for transfers between devices, partner_2(): return lax.ppermute(block, axis, route)  57.6 us
    dot_general x8, matrix products, per_device(): jnp.einsum('vr,pr->vp', linked_result, left_basis[tree_height], preferred...  9.76 us
    dot_general x8, matrix products, per_device(): jnp.dot(state.astype(jnp.bfloat16), right_level_bases[tree_height], prefe...  8.97 us
    sort x1, other arithmetic, per_device(): inverse = jnp.argsort(leaf_order)  4.37 us
    gather x1, local copies, waits for them, and re-layouts, per_device(): product = jnp.take(total, inverse, axis=1)  4.04 us
    gather x1, local copies, waits for them, and re-layouts, per_device(): solution = jnp.take(state, inverse, axis=1)  4.02 us
  transfers between devices with their start and end apart: 44, of which 30 were waited for; matrix products, arithmetic and copies ran while one was open for 12% of the time, Pallas kernels for 0%

commit v1 on v0

v1 whole, which is shorter than its diff:
```python
import functools

import jax
import jax.numpy as jnp
from jax import lax
from jax.experimental import pallas as pl
from jax.experimental.pallas import tpu as pltpu
from jax.sharding import PartitionSpec as P

BF = jnp.bfloat16
F32 = jnp.float32
LANE = 128
VMEM = pl.BlockSpec(memory_space=pltpu.VMEM)
SMEM = pl.BlockSpec(memory_space=pltpu.SMEM)
HBM = pl.BlockSpec(memory_space=pl.ANY)
NT = (((1,), (1,)), ((), ()))
LEVELS = 8
SUMMED = 3


def scale(level):
    return 2.0 ** (-0.5 * level)


def dot(a, b):
    return jnp.dot(a, b, preferred_element_type=F32)


def dot_t(a, b):
    return lax.dot_general(a, b, NT, preferred_element_type=F32)


def one_hot(order, low, width):
    rows = lax.broadcasted_iota(jnp.int32, (order.shape[1], width), 0)
    return jnp.where(rows == order[:, low : low + width], 1.0, 0.0).astype(BF)


def columns(ref, level):
    return ref.at[:, pl.ds(level * LANE, LANE)]


def coefficient_kernel(live, order, vec, rhs, right, first_out, solve_out, tree_out, right_cat, tree, sems):
    copies = [
        pltpu.make_async_copy(right.at[level], columns(right_cat, level), sems.at[level])
        for level in range(LEVELS)
    ]
    for copy in copies:
        copy.start()
    points = vec.shape[1]
    nvec = vec.shape[0]
    fields = jnp.concatenate([vec[...], rhs[...]], axis=0)
    chunk = 256
    for low in range(0, points, chunk):
        moved = dot(fields, one_hot(order[...], low, chunk))
        slot = lax.broadcasted_iota(jnp.int32, moved.shape, 1) + low
        tree[:, low : low + chunk] = jnp.where(slot < live[0], moved, 0.0).astype(BF)
    tree_out[...] = tree[:nvec, :]
    for copy in copies:
        copy.wait()
    for level in range(0, LEVELS, 2):
        pair = dot(tree[...], right_cat[:, level * LANE : (level + 2) * LANE])
        for now in (level, level + 1):
            part = pair[:, (now - level) * LANE : (now - level + 1) * LANE] * scale(now)
            first_out[:, (now + 1) * LANE : (now + 2) * LANE] = part[:nvec].astype(BF)
            if now == 0:
                first_out[:, :LANE] = part[nvec:].astype(BF)
            else:
                solve_out[:, (now - 1) * LANE : now * LANE] = part[nvec:]


def update_kernel(live, index, coupling, left, right, *rest):
    outs, (right_cat, left_cat, sems) = rest[:-3], rest[-3:]
    rights = [
        pltpu.make_async_copy(right.at[level], columns(right_cat, level - 1), sems.at[0, level])
        for level in range(1, LEVELS)
    ]
    lefts = [
        pltpu.make_async_copy(left.at[level], columns(left_cat, level), sems.at[1, level])
        for level in range(LEVELS - 1)
    ]
    for copy in rights + lefts:
        copy.start()
    for copy in rights:
        copy.wait()
    at = 0
    for level in range(LEVELS - 1):
        lefts[level].wait()
        block = left_cat[:, level * LANE : (level + 1) * LANE]
        rows = lax.broadcasted_iota(jnp.int32, block.shape, 0)
        block = jnp.where(rows < live[0], block.astype(F32), 0.0)
        turned = block.T.astype(BF)
        gram = dot(turned, right_cat[:, level * LANE :])
        gram = jnp.concatenate(
            [
                (gram[:, (now - level - 1) * LANE : (now - level) * LANE] * scale(now)).astype(BF)
                for now in range(level + 1, LEVELS)
            ],
            axis=1,
        )
        update = dot(canonical(coupling, index, level), gram).astype(BF)
        if level < SUMMED:
            outs[level][...] = update
        else:
            width = update.shape[1]
            outs[SUMMED][:, at : at + width] = update
            at += width


def canonical(coupling, index, level):
    held = coupling[level]
    swapped = jnp.concatenate([held[LANE:], held[:LANE]], axis=0)
    second = (lax.shift_right_logical(index[0], level) & 1) == 1
    return jnp.where(second, swapped, held)


def local_kernel(live, order, tree_x, rhs, block, left, prod_out, sol_out, moved_out, block_in, left_cat, hot, sems):
    copies = [
        pltpu.make_async_copy(left.at[level], columns(left_cat, level), sems.at[level])
        for level in range(LEVELS)
    ]
    block_copy = pltpu.make_async_copy(block, block_in, sems.at[LEVELS])
    block_copy.start()
    for copy in copies:
        copy.start()
    points = order.shape[1]
    chunk = 256
    for low in range(0, points, chunk):
        hot[:, low : low + chunk] = one_hot(order[...], low, chunk)
    slot = lax.broadcasted_iota(jnp.int32, (8, points), 1)
    alive = jnp.where(slot < live[0], 1.0, 0.0).astype(BF)
    kept = dot_t(alive, hot[...])
    sol_out[...] = rhs[...].astype(F32) * kept[:1]
    block_copy.wait()
    direct = dot_t(tree_x[...], block_in[...])
    slot = lax.broadcasted_iota(jnp.int32, direct.shape, 1)
    direct = jnp.where(slot < live[0], direct, 0.0)
    high = direct.astype(BF)
    low_part = (direct - high.astype(F32)).astype(BF)
    prod_out[...] = dot_t(high, hot[...]) + dot_t(low_part, hot[...])
    for copy in copies:
        copy.wait()
    for low in range(0, LEVELS * LANE, chunk):
        part = left_cat[:, low : low + chunk]
        rows = lax.broadcasted_iota(jnp.int32, part.shape, 0)
        part = jnp.where(rows < live[0], part.astype(F32), 0.0).astype(BF)
        moved_out[:, low : low + chunk] = dot(hot[...], part).astype(BF)


def partial_kernel(index, coupling, moved, prod, sol, siblings, joined, prod_out, sol_out):
    count = LEVELS - 1
    moved_now = moved[:, : count * LANE]
    prod_out[...] = prod[...] + dot_t(siblings[...], moved_now)
    coupled = [
        dot(joined[:, 2 * level * LANE : 2 * (level + 1) * LANE], canonical(coupling, index, level)).astype(BF)
        for level in range(count)
    ]
    sol_out[...] = sol[...] - dot_t(jnp.concatenate(coupled, axis=1), moved_now)


def last_kernel(index, coupling, moved, prod, sol, sibling, joined, prod_out, sol_out):
    prod_out[...] = prod[...] + dot_t(sibling[...], moved[...])
    held = coupling[...]
    swapped = jnp.concatenate([held[LANE:], held[:LANE]], axis=0)
    second = (lax.shift_right_logical(index[0], LEVELS - 1) & 1) == 1
    coupled = dot(joined[...], jnp.where(second, swapped, held)).astype(BF)
    sol_out[...] = sol[...] - dot_t(coupled, moved[...])


def params(mib):
    return pltpu.CompilerParams(vmem_limit_bytes=mib << 20)


def shape(rows, lanes, dtype=BF):
    return jax.ShapeDtypeStruct((rows, lanes), dtype)


def swap(block, mask):
    count = lax.axis_size("leaf") * lax.axis_size("sub")
    return lax.ppermute(block, ("leaf", "sub"), [(i, i ^ mask) for i in range(count)])


def cols(block, low, high=None):
    return block[:, low * LANE : None if high is None else high * LANE]


def cat(*blocks):
    return jnp.concatenate([block.astype(BF) for block in blocks], axis=1)


def per_device(vectors, right_side, tree_order, live_counts, leaf_block, left_basis, right_bases, coupling):
    nvec, points = vectors.shape
    index = lax.axis_index("leaf") * lax.axis_size("sub") + lax.axis_index("sub")
    index_1 = index.astype(jnp.int32).reshape(1)
    sub, core = index & 3, (index >> 2) & 1
    coupling = coupling[0]

    def join(mine, other, level):
        second = ((index >> level) & 1) == 1
        return cat(jnp.where(second, other, mine), jnp.where(second, mine, other))

    first, coef, tree_x = pl.pallas_call(
        coefficient_kernel,
        out_shape=(shape(nvec, 9 * LANE), shape(nvec, 7 * LANE, F32), shape(nvec, points)),
        in_specs=[SMEM, VMEM, VMEM, VMEM, HBM],
        out_specs=(VMEM, VMEM, VMEM),
        scratch_shapes=[
            pltpu.VMEM((points, LEVELS * LANE), BF),
            pltpu.VMEM((2 * nvec, points), BF),
            pltpu.SemaphoreType.DMA((LEVELS,)),
        ],
        compiler_params=params(24),
        cost_estimate=pl.CostEstimate(flops=300_000_000, bytes_accessed=2_500_000, transcendentals=0),
        name="coefficients",
    )(live_counts, tree_order, vectors, right_side, right_bases)

    widths = [LEVELS - 1 - level for level in range(SUMMED)]
    summed = sum(LEVELS - 1 - level for level in range(SUMMED, LEVELS - 1))
    update_0, update_1, update_2, update_up = pl.pallas_call(
        update_kernel,
        out_shape=tuple(shape(2 * LANE, width * LANE) for width in widths + [summed]),
        in_specs=[SMEM, SMEM, VMEM, HBM, HBM],
        out_specs=(VMEM,) * 4,
        scratch_shapes=[
            pltpu.VMEM((points, 7 * LANE), BF),
            pltpu.VMEM((points, 7 * LANE), BF),
            pltpu.SemaphoreType.DMA((2, LEVELS)),
        ],
        compiler_params=params(24),
        cost_estimate=pl.CostEstimate(flops=1_300_000_000, bytes_accessed=5_000_000, transcendentals=0),
        name="updates",
    )(live_counts, index_1, coupling, left_basis, right_bases)

    base_prod, base_sol, moved = pl.pallas_call(
        local_kernel,
        out_shape=(shape(nvec, points, F32), shape(nvec, points, F32), shape(points, LEVELS * LANE)),
        in_specs=[SMEM, VMEM, VMEM, VMEM, HBM, HBM],
        out_specs=(VMEM, VMEM, VMEM),
        scratch_shapes=[
            pltpu.VMEM((points, points), BF),
            pltpu.VMEM((points, LEVELS * LANE), BF),
            pltpu.VMEM((points, points), BF),
            pltpu.SemaphoreType.DMA((LEVELS + 1,)),
        ],
        compiler_params=params(32),
        cost_estimate=pl.CostEstimate(flops=2_500_000_000, bytes_accessed=7_000_000, transcendentals=0),
        name="local",
    )(live_counts, tree_order, tree_x, right_side, leaf_block, left_basis)

    siblings, joined = [], []

    got = swap(first, 1)
    joined.append(join(cols(first, 0, 1), cols(got, 0, 1), 0))
    siblings.append(cols(got, 1, 2))
    prod = cols(first, 2).astype(F32) + cols(got, 2).astype(F32)
    coef = coef - dot(joined[0], update_0)

    half = update_up.shape[0] // 2
    away = lax.dynamic_slice_in_dim(update_up, (1 - core) * half, half, 0)
    home = lax.dynamic_slice_in_dim(update_up, core * half, half, 0)
    halves = (home.astype(F32) + swap(away, 4).astype(F32)).astype(BF)
    piece = half // 4

    def rows_of(mask):
        return lax.dynamic_slice_in_dim(halves, (sub ^ mask) * piece, piece, 0)

    mine = cols(coef, 0, 1)
    got = {
        1: swap(cat(mine, rows_of(1)), 1),
        2: swap(cat(mine, rows_of(2)), 2),
        3: swap(cat(mine, rows_of(3), prod), 3),
    }
    parts = {mask: cols(block, 0, 1).astype(F32) for mask, block in got.items()}
    joined.append(join((mine + parts[1]).astype(BF), (parts[2] + parts[3]).astype(BF), 1))
    pieces = rows_of(0).astype(F32)
    for mask in (1, 2, 3):
        pieces = pieces + cols(got[mask], 1, 1 + summed).astype(F32)
    got_prod = cols(got[3], 1 + summed)
    siblings.append(cols(got_prod, 0, 1))
    prod = cols(prod, 1) + cols(got_prod, 1).astype(F32)
    coef = cols(coef, 1) - dot(joined[1], update_1)

    sent = coef.astype(BF)
    pieces_3 = pieces + swap(pieces.astype(BF), 8).astype(F32)
    total = coef
    for mask in (1, 2, 3):
        total = total + swap(sent, mask).astype(F32)
    pieces_4 = cols(pieces_3, 4) + swap(cols(pieces_3, 4).astype(BF), 24).astype(F32)
    got = swap(cat(total, prod), 4)
    got_total, got_prod = cols(got, 0, 6), cols(got, 6)
    joined.append(join(cols(total, 0, 1).astype(BF), cols(got_total, 0, 1), 2))
    siblings.append(cols(got_prod, 0, 1))
    total = cols(total, 1) + cols(got_total, 1).astype(F32)
    prod = cols(prod, 1) + cols(got_prod, 1).astype(F32)
    change = dot(joined[2], update_2)

    def gather_rows(block, extra):
        sent = cat(extra, block) if extra is not None else block.astype(BF)
        lead = extra.shape[1] if extra is not None else 0
        got = {mask: swap(sent, mask) for mask in (1, 2, 3)}
        blocks = {0: block.astype(BF)}
        for mask in (1, 2, 3):
            blocks[mask] = got[mask][:, lead:]
            if extra is not None:
                extra = extra + got[mask][:, :lead].astype(F32)
        odd, high = (sub & 1) == 1, (sub >> 1) == 1
        low_pair = [jnp.where(odd, blocks[1], blocks[0]), jnp.where(odd, blocks[0], blocks[1])]
        high_pair = [jnp.where(odd, blocks[3], blocks[2]), jnp.where(odd, blocks[2], blocks[3])]
        ordered = [jnp.where(high, b, a) for a, b in zip(low_pair, high_pair)]
        ordered += [jnp.where(high, a, b) for a, b in zip(low_pair, high_pair)]
        return ordered, extra

    def gather_cores(ordered, extra):
        width = ordered[0].shape[1]
        lead = extra.shape[1] if extra is not None else 0
        got = swap(cat(*([extra] if extra is not None else []), *ordered), 4)
        theirs = [got[:, lead + i * width : lead + (i + 1) * width] for i in range(4)]
        mine, theirs = jnp.concatenate(ordered, axis=0), jnp.concatenate(theirs, axis=0)
        second = core == 1
        whole = jnp.concatenate([jnp.where(second, theirs, mine), jnp.where(second, mine, theirs)], axis=0)
        if extra is not None:
            extra = extra + got[:, :lead].astype(F32)
        return whole, extra

    ordered, change = gather_rows(cat(cols(pieces_3, 0, 4), cols(pieces_4, 0, 3)), change)
    whole, change = gather_cores(ordered, change)
    total = total - change
    summed_updates = {3: cols(whole, 0, 4), 4: cols(whole, 4)}
    pieces_5 = cols(pieces_4, 3) + swap(cols(pieces_4, 3).astype(BF), 32).astype(F32)
    pieces_6 = cols(pieces_5, 2) + swap(cols(pieces_5, 2).astype(BF), 64).astype(F32)
    ordered, _ = gather_rows(cat(cols(pieces_5, 0, 2), pieces_6), None)
    whole, _ = gather_cores(ordered, None)
    summed_updates[5], summed_updates[6] = cols(whole, 0, 2), cols(whole, 2)

    for level, mask in ((3, 8), (4, 24), (5, 32), (6, 64)):
        left_over = LEVELS - level
        got = swap(cat(total, prod), mask)
        got_total, got_prod = cols(got, 0, left_over), cols(got, left_over)
        joined.append(join(cols(total, 0, 1).astype(BF), cols(got_total, 0, 1), level))
        siblings.append(cols(got_prod, 0, 1))
        total = cols(total, 1) + cols(got_total, 1).astype(F32) - dot(joined[level], summed_updates[level])
        prod = cols(prod, 1) + cols(got_prod, 1).astype(F32)
    sent = cat(total, prod)
    got = swap(sent, 224)
    part_prod, part_sol = pl.pallas_call(
        partial_kernel,
        out_shape=(shape(nvec, points, F32),) * 2,
        in_specs=[SMEM] + [VMEM] * 6,
        out_specs=(VMEM, VMEM),
        compiler_params=params(16),
        cost_estimate=pl.CostEstimate(flops=150_000_000, bytes_accessed=3_000_000, transcendentals=0),
        name="partial",
    )(index_1, coupling, moved, base_prod, base_sol, cat(*siblings), cat(*joined))
    last_joined = join(cols(sent, 0, 1), cols(got, 0, 1), LEVELS - 1)
    return pl.pallas_call(
        last_kernel,
        out_shape=(shape(nvec, points, F32),) * 2,
        in_specs=[SMEM] + [VMEM] * 6,
        out_specs=(VMEM, VMEM),
        compiler_params=params(8),
        cost_estimate=pl.CostEstimate(flops=30_000_000, bytes_accessed=1_000_000, transcendentals=0),
        name="last",
    )(
        index_1,
        coupling[LEVELS - 1],
        cols(moved, LEVELS - 1),
        part_prod,
        part_sol,
        cols(got, 1),
        last_joined,
    )


def solution(mesh):
    placed = (
        P(None, ("leaf", "sub")),
        P(None, ("leaf", "sub")),
        P(("leaf", "sub"), None),
        P(("leaf", "sub")),
        P(("leaf", "sub"), None),
        P(None, ("leaf", "sub"), None),
        P(None, ("leaf", "sub"), None),
        P(("leaf", "sub"), None, None, None),
    )
    return jax.shard_map(
        per_device,
        mesh=mesh,
        in_specs=placed,
        out_specs=(P(None, ("leaf", "sub")), P(None, ("leaf", "sub"))),
        check_vma=False,
    )
```

time: 189 us -> 97.5 us (0.52)
  starting transfers between devices: 78.9 us -> 37 us
  waiting for transfers between devices: 57.6 us -> 28.2 us
  matrix products: 23.8 us -> 2.03 us
  Pallas kernels: 0 us -> 15.2 us
  local copies, waits for them, and re-layouts: 18.1 us -> 9.26 us
  other arithmetic: 7.39 us -> 3.37 us
    ppermute x44 -> x26, starting transfers between devices: 78.9 us -> 37 us  [swap(): lax.ppermute(block, ('leaf', 'sub'), [(i, i ^ mask) for i in range(count)])]
    ppermute x44 -> x26, waiting for transfers between devices: 57.6 us -> 28.2 us  [swap(): lax.ppermute(block, ('leaf', 'sub'), [(i, i ^ mask) for i in range(count)])]
    dot_general x19 -> x7, matrix products: 23.8 us -> 2.03 us  [dot(): return jnp.dot(a, b, preferred_element_type=F32)]
    pallas_call x0 -> x5, Pallas kernels: none -> 15.2 us  [the longest x1 5.78 us: per_device(): pl.pallas_call(local_kernel, out_shape=(shape(nvec, points, F32), shape(n...]
    gather x6 -> x0, local copies, waits for them, and re-layouts: 14.7 us -> none  [the longest x1 4.04 us: per_device(): product = jnp.take(total, inverse, axis=1)]
    unnamed x21 -> x42, local copies, waits for them, and re-layouts: 2.94 us -> 9.06 us
    sort x1 -> x0, other arithmetic: 4.37 us -> none  [per_device(): inverse = jnp.argsort(leaf_order)]
  transfers between devices with their start and end apart: 44 -> 26, of which waited for: 30 -> 12; matrix products, arithmetic and copies ran while one was open for 12% -> 5% of each run, Pallas kernels for 0% -> 12%
where the time goes in v1:
time: 97.5 us; the launch traced here: 97 us
  starting transfers between devices  37 us (38%)
  waiting for transfers between devices  28.2 us (29%)
  Pallas kernels  15.2 us (16%)
  local copies, waits for them, and re-layouts  9.26 us (9%)
  other arithmetic  3.37 us (3%)
  matrix products  2.03 us (2%)
  between operations  1.85 us (2%)
    ppermute x26, starting transfers between devices, swap(): lax.ppermute(block, ('leaf', 'sub'), [(i, i ^ mask) for i in range(count)])  37 us
    ppermute x26, waiting for transfers between devices, swap(): lax.ppermute(block, ('leaf', 'sub'), [(i, i ^ mask) for i in range(count)])  28.2 us
    unnamed x42, local copies, waits for them, and re-layouts  9.06 us
    pallas_call x1, Pallas kernels, per_device(): pl.pallas_call(local_kernel, out_shape=(shape(nvec, points, F32), shape(n...  5.78 us
    pallas_call x1, Pallas kernels, per_device(): pl.pallas_call(update_kernel, out_shape=tuple((shape(2 * LANE, width * LA...  4.9 us
    pallas_call x1, Pallas kernels, per_device(): pl.pallas_call(coefficient_kernel, out_shape=(shape(nvec, 9 * LANE), shap...  2.28 us
    dot_general x7, matrix products, dot(): return jnp.dot(a, b, preferred_element_type=F32)  2.03 us
  transfers between devices with their start and end apart: 26, of which 12 were waited for; matrix products, arithmetic and copies ran while one was open for 5% of the time, Pallas kernels for 12%

profile of v1, /device:TPU:32, one launch (start us, length us, event | category | flops | bytes accessed | tf_op | source)
XLA Modules:
  0.0 97.0 jit_solution(11769059893989516072)
XLA Ops:
  1.3 1.6 %copy-done = bf16[8,1024,128]{2,1,0:T(8,128)(2,1)S(1)} copy-done((bf16[8,1024,128]{2,1,0:T(8,128)(2,1)S(1)}, bf16[8,1024,128]{2,1,0:T(8,128)(2,1)}, u32[]{:S(2)}) %copy-start) | copy-done | bytes 2097176
  5.2 2.3 %coefficients.1 = (bf16[32,1152]{1,0:T(8,128)(2,1)}, f32[32,896]{1,0:T(8,128)S(1)}, bf16[32,1024]{1,0:T(8,128)(2,1)S(1)}) custom-call(s32[1]{0:T(128)S(6)} %copy.33.live, s32[1,1024]{1,0:T(1,128)S(1)} %copy-done.14, bf16[32,1024]{1,0:T(8,128)(2,1)S(1)} %copy-done.11, bf16[32,1024]{1,0:T(8,128)(2,1)S(1)} %copy-done.12, bf16[8,1024,128]{2,1,0:T(8,128)(2,1)S(1)} %copy-done), custom_call_target="tpu_custom_call" | custom-call | flops 300000000 | bytes 2500000 | tf_op jit(solution)/shard_map/coefficients/pallas_call | solution.py:201
  8.8 1.6 %collective-permute-start = (bf16[32,1152]{1,0:T(8,128)(2,1)}, bf16[32,1152]{1,0:T(8,128)(2,1)}, u32[]{:S(2)}, u32[]{:S(2)}) collective-permute-start(bf16[32,1152]{1,0:T(8,128)(2,1)} %get-tuple-element.18), channel_id=1, source_target_pairs={{0,1},{1,0},{2,3},{3,2},{4,5},{5,4},{6,7},{7,6},{8,9},{9,8},{10,11... | collective-permute-start | bytes 221192 | tf_op jit(solution)/shard_map/ppermute | solution.py:179
  10.4 1.0 %copy-done.2 = bf16[1,8,256,128]{3,2,1,0:T(8,128)(2,1)S(1)} copy-done((bf16[1,8,256,128]{3,2,1,0:T(8,128)(2,1)S(1)}, bf16[1,8,256,128]{3,2,1,0:T(8,128)(2,1)}, u32[]{:S(2)}) %copy-start.2) | copy-done | bytes 524312
  11.4 1.6 %copy-done.17 = bf16[8,1024,128]{2,1,0:T(8,128)(2,1)S(1)} copy-done((bf16[8,1024,128]{2,1,0:T(8,128)(2,1)S(1)}, bf16[8,1024,128]{2,1,0:T(8,128)(2,1)}, u32[]{:S(2)}) %copy-start.17) | copy-done | bytes 2097176
  13.0 4.9 %updates.1 = (bf16[256,896]{1,0:T(8,128)(2,1)S(1)}, bf16[256,768]{1,0:T(8,128)(2,1)S(1)}, bf16[256,640]{1,0:T(8,128)(2,1)S(1)}, bf16[256,1280]{1,0:T(8,128)(2,1)S(1)}) custom-call(s32[1]{0:T(128)S(6)} %copy.33.live, s32[1]{0:T(128)} %bitcast.index, bf16[8,256,128]{2,1,0:T(8,128)(2,1)S(1)} %bitcast.7, bf16[8,1024,128]{2,1,0:T(8,128)(2,1)S(1)} %copy-done.17, ...), custom_call_target="tpu_custom_call" | custom-call | flops 1300000000 | bytes 5000000 | tf_op jit(solution)/shard_map/updates/pallas_call | solution.py:218
  20.3 1.1 %convolution_subtract_fusion = f32[32,896]{1,0:T(8,128)S(1)} fusion(f32[32,896]{1,0:T(8,128)} %copy-done.8, bf16[256,896]{1,0:T(8,128)(2,1)S(1)} %get-tuple-element.20, bf16[32,128]{1,0:T(8,128)(2,1)S(1)} %get-tuple-element.51, bf16[32,128]{1,0:T(8,128)(2,1)S(1)} %get-tuple-element.53), kind=kOutput, calls=%fused_computation | convolution fusion | flops 14741504 | bytes 704512 | tf_op jit(solution)/shard_map/dot_general | solution.py:26
  21.4 0.9 convert_add_fusion.2
  22.4 2.3 %collective-permute-start.2 = (bf16[32,2304]{1,0:T(8,128)(2,1)S(1)}, bf16[32,2304]{1,0:T(8,128)(2,1)S(1)}, u32[]{:S(2)}, u32[]{:S(2)}) collective-permute-start(bf16[32,2304]{1,0:T(8,128)(2,1)S(1)} %pad_maximum_fusion.4), channel_id=1, source_target_pairs={{0,3},{1,2},{2,1},{3,0},{4,7},{5,6},{6,5},{7,4},{8,11},{9,10},{10,... | collective-permute-start | bytes 442376 | tf_op jit(solution)/shard_map/ppermute | solution.py:179
  25.6 1.2 %collective-permute-start.4 = (bf16[32,1408]{1,0:T(8,128)(2,1)S(1)}, bf16[32,1408]{1,0:T(8,128)(2,1)S(1)}, u32[]{:S(2)}, u32[]{:S(2)}) collective-permute-start(bf16[32,1408]{1,0:T(8,128)(2,1)S(1)} %get-tuple-element.112), channel_id=1, source_target_pairs={{0,1},{1,0},{2,3},{3,2},{4,5},{5,4},{6,7},{7,6},{8,9},{9,8},{10,11... | collective-permute-start | bytes 270344 | tf_op jit(solution)/shard_map/ppermute | solution.py:179
  26.7 5.1 %collective-permute-done.3 = bf16[32,1408]{1,0:T(8,128)(2,1)S(1)} collective-permute-done((bf16[32,1408]{1,0:T(8,128)(2,1)S(1)}, bf16[32,1408]{1,0:T(8,128)(2,1)S(1)}, u32[]{:S(2)}, u32[]{:S(2)}) %collective-permute-start.3) | collective-permute-done | bytes 90144 | tf_op jit(solution)/shard_map/ppermute | solution.py:179
  32.8 3.0 %collective-permute-start.6 = (bf16[32,768]{1,0:T(8,128)(2,1)S(1)}, bf16[32,768]{1,0:T(8,128)(2,1)S(1)}, u32[]{:S(2)}, u32[]{:S(2)}) collective-permute-start(bf16[32,768]{1,0:T(8,128)(2,1)S(1)} %get-tuple-element.113), channel_id=1, source_target_pairs={{0,2},{1,3},{2,0},{3,1},{4,6},{5,7},{6,4},{7,5},{8,10},{9,11},{10,... | collective-permute-start | bytes 147464 | tf_op jit(solution)/shard_map/ppermute | solution.py:179
  35.9 1.0 %collective-permute-start.7 = (bf16[32,768]{1,0:T(8,128)(2,1)S(1)}, bf16[32,768]{1,0:T(8,128)(2,1)S(1)}, u32[]{:S(2)}, u32[]{:S(2)}) collective-permute-start(bf16[32,768]{1,0:T(8,128)(2,1)S(1)} %get-tuple-element.113), channel_id=1, source_target_pairs={{0,3},{1,2},{2,1},{3,0},{4,7},{5,6},{6,5},{7,4},{8,11},{9,10},{10,... | collective-permute-start | bytes 147464 | tf_op jit(solution)/shard_map/ppermute | solution.py:179
  37.0 1.6 %collective-permute-start.9 = (bf16[32,1280]{1,0:T(8,128)(2,1)S(1)}, bf16[32,1280]{1,0:T(8,128)(2,1)S(1)}, u32[]{:S(2)}, u32[]{:S(2)}) collective-permute-start(bf16[32,1280]{1,0:T(8,128)(2,1)S(1)} %fusion.51), channel_id=1, source_target_pairs={{0,8},{1,9},{2,10},{3,11},{4,12},{5,13},{6,14},{7,15},{8,0},{9,1},... | collective-permute-start | bytes 245768 | tf_op jit(solution)/shard_map/ppermute | solution.py:179
  38.6 2.6 %collective-permute-done.7 = bf16[32,768]{1,0:T(8,128)(2,1)S(1)} collective-permute-done((bf16[32,768]{1,0:T(8,128)(2,1)S(1)}, bf16[32,768]{1,0:T(8,128)(2,1)S(1)}, u32[]{:S(2)}, u32[]{:S(2)}) %collective-permute-start.7) | collective-permute-done | bytes 49184 | tf_op jit(solution)/shard_map/ppermute | solution.py:179
  41.6 2.8 %collective-permute-start.10 = (bf16[32,768]{1,0:T(8,128)(2,1)S(1)}, bf16[32,768]{1,0:T(8,128)(2,1)S(1)}, u32[]{:S(2)}, u32[]{:S(2)}) collective-permute-start(bf16[32,768]{1,0:T(8,128)(2,1)S(1)} %slice.633), channel_id=1, source_target_pairs={{0,24},{1,25},{2,26},{3,27},{4,28},{5,29},{6,30},{7,31},{8,16},{9,... | collective-permute-start | bytes 147464 | tf_op jit(solution)/shard_map/ppermute | solution.py:179
  44.5 2.4 %collective-permute-done.10 = bf16[32,768]{1,0:T(8,128)(2,1)S(1)} collective-permute-done((bf16[32,768]{1,0:T(8,128)(2,1)S(1)}, bf16[32,768]{1,0:T(8,128)(2,1)S(1)}, u32[]{:S(2)}, u32[]{:S(2)}) %collective-permute-start.10) | collective-permute-done | bytes 49184 | tf_op jit(solution)/shard_map/ppermute | solution.py:179
  47.7 3.3 %collective-permute-done.18 = bf16[32,384]{1,0:T(8,128)(2,1)S(1)} collective-permute-done((bf16[32,384]{1,0:T(8,128)(2,1)S(1)}, bf16[32,384]{1,0:T(8,128)(2,1)S(1)}, u32[]{:S(2)}, u32[]{:S(2)}) %collective-permute-start.18) | collective-permute-done | bytes 24608 | tf_op jit(solution)/shard_map/ppermute | solution.py:179
  51.1 3.4 %collective-permute-start.19 = (bf16[32,128]{1,0:T(8,128)(2,1)S(1)}, bf16[32,128]{1,0:T(8,128)(2,1)S(1)}, u32[]{:S(2)}, u32[]{:S(2)}) collective-permute-start(bf16[32,128]{1,0:T(8,128)(2,1)S(1)} %slice.638), channel_id=1, source_target_pairs={{0,64},{1,65},{2,66},{3,67},{4,68},{5,69},{6,70},{7,71},{8,72},{9,... | collective-permute-start | bytes 24584 | tf_op jit(solution)/shard_map/ppermute | solution.py:179
  54.6 3.6 %collective-permute-start.12 = (bf16[32,1536]{1,0:T(8,128)(2,1)S(1)}, bf16[32,1536]{1,0:T(8,128)(2,1)S(1)}, u32[]{:S(2)}, u32[]{:S(2)}) collective-permute-start(bf16[32,1536]{1,0:T(8,128)(2,1)S(1)} %pad_maximum_fusion.8), channel_id=1, source_target_pairs={{0,2},{1,3},{2,0},{3,1},{4,6},{5,7},{6,4},{7,5},{8,10},{9,11},{10,... | collective-permute-start | bytes 294920 | tf_op jit(solution)/shard_map/ppermute | solution.py:179
  58.2 1.1 %collective-permute-start.13 = (bf16[32,1536]{1,0:T(8,128)(2,1)S(1)}, bf16[32,1536]{1,0:T(8,128)(2,1)S(1)}, u32[]{:S(2)}, u32[]{:S(2)}) collective-permute-start(bf16[32,1536]{1,0:T(8,128)(2,1)S(1)} %pad_maximum_fusion.8), channel_id=1, source_target_pairs={{0,3},{1,2},{2,1},{3,0},{4,7},{5,6},{6,5},{7,4},{8,11},{9,10},{10,... | collective-permute-start | bytes 294920 | tf_op jit(solution)/shard_map/ppermute | solution.py:179
  59.3 2.3 %collective-permute-start.20 = (bf16[32,384]{1,0:T(8,128)(2,1)S(1)}, bf16[32,384]{1,0:T(8,128)(2,1)S(1)}, u32[]{:S(2)}, u32[]{:S(2)}) collective-permute-start(bf16[32,384]{1,0:T(8,128)(2,1)S(1)} %pad_maximum_fusion.19), channel_id=1, source_target_pairs={{0,3},{1,2},{2,1},{3,0},{4,7},{5,6},{6,5},{7,4},{8,11},{9,10},{10,... | collective-permute-start | bytes 73736 | tf_op jit(solution)/shard_map/ppermute | solution.py:179
  61.6 1.9 %collective-permute-start.22 = (bf16[32,384]{1,0:T(8,128)(2,1)S(1)}, bf16[32,384]{1,0:T(8,128)(2,1)S(1)}, u32[]{:S(2)}, u32[]{:S(2)}) collective-permute-start(bf16[32,384]{1,0:T(8,128)(2,1)S(1)} %pad_maximum_fusion.19), channel_id=1, source_target_pairs={{0,1},{1,0},{2,3},{3,2},{4,5},{5,4},{6,7},{7,6},{8,9},{9,8},{10,11... | collective-permute-start | bytes 73736 | tf_op jit(solution)/shard_map/ppermute | solution.py:179
  64.4 2.5 %collective-permute-done.21 = bf16[32,384]{1,0:T(8,128)(2,1)S(1)} collective-permute-done((bf16[32,384]{1,0:T(8,128)(2,1)S(1)}, bf16[32,384]{1,0:T(8,128)(2,1)S(1)}, u32[]{:S(2)}, u32[]{:S(2)}) %collective-permute-start.21) | collective-permute-done | bytes 24608 | tf_op jit(solution)/shard_map/ppermute | solution.py:179
  67.7 4.4 %collective-permute-done.15 = bf16[32,1280]{1,0:T(8,128)(2,1)S(1)} collective-permute-done((bf16[32,1280]{1,0:T(8,128)(2,1)S(1)}, bf16[32,1280]{1,0:T(8,128)(2,1)S(1)}, u32[]{:S(2)}, u32[]{:S(2)}) %collective-permute-start.15) | collective-permute-done | bytes 81952 | tf_op jit(solution)/shard_map/ppermute | solution.py:179
  72.3 2.8 %collective-permute-start.16 = (bf16[32,1024]{1,0:T(8,128)(2,1)S(1)}, bf16[32,1024]{1,0:T(8,128)(2,1)S(1)}, u32[]{:S(2)}, u32[]{:S(2)}) collective-permute-start(bf16[32,1024]{1,0:T(8,128)(2,1)S(1)} %pad_maximum_fusion.15), channel_id=1, source_target_pairs={{0,24},{1,25},{2,26},{3,27},{4,28},{5,29},{6,30},{7,31},{8,16},{9,... | collective-permute-start | bytes 196616 | tf_op jit(solution)/shard_map/ppermute | solution.py:179
  75.1 2.7 %collective-permute-done.16 = bf16[32,1024]{1,0:T(8,128)(2,1)S(1)} collective-permute-done((bf16[32,1024]{1,0:T(8,128)(2,1)S(1)}, bf16[32,1024]{1,0:T(8,128)(2,1)S(1)}, u32[]{:S(2)}, u32[]{:S(2)}) %collective-permute-start.16) | collective-permute-done | bytes 65568 | tf_op jit(solution)/shard_map/ppermute | solution.py:179
  78.4 3.8 %collective-permute-done.17 = bf16[32,768]{1,0:T(8,128)(2,1)S(1)} collective-permute-done((bf16[32,768]{1,0:T(8,128)(2,1)S(1)}, bf16[32,768]{1,0:T(8,128)(2,1)S(1)}, u32[]{:S(2)}, u32[]{:S(2)}) %collective-permute-start.17) | collective-permute-done | bytes 49184 | tf_op jit(solution)/shard_map/ppermute | solution.py:179
  83.0 5.8 %local.1 = (f32[32,1024]{1,0:T(8,128)S(1)}, f32[32,1024]{1,0:T(8,128)S(1)}, bf16[1024,1024]{1,0:T(8,128)(2,1)S(1)}) custom-call(s32[1]{0:T(128)S(6)} %copy.33.live, s32[1,1024]{1,0:T(1,128)S(1)} %copy-done.15, bf16[32,1024]{1,0:T(8,128)(2,1)S(1)} %copy-done.20, bf16[32,1024]{1,0:T(8,128)(2,1)S(1)} %copy-done.13, bf16[1024,1024]{1,0:T(8,128)(2,1)S(1)} %copy-done.16, ...), custom_call_target="tpu_custom_call" | custom-call | flops 2500000000 | bytes 7000000 | tf_op jit(solution)/shard_map/local/pallas_call | solution.py:233
  89.0 5.2 %collective-permute-start.25 = (bf16[32,256]{1,0:T(8,128)(2,1)S(1)}, bf16[32,256]{1,0:T(8,128)(2,1)S(1)}, u32[]{:S(2)}, u32[]{:S(2)}) collective-permute-start(bf16[32,256]{1,0:T(8,128)(2,1)S(1)} %pad_maximum_fusion.24), channel_id=1, source_target_pairs={{0,224},{1,225},{2,226},{3,227},{4,228},{5,229},{6,230},{7,231},{8... | collective-permute-start | bytes 49160 | tf_op jit(solution)/shard_map/ppermute | solution.py:179
  94.3 1.3 %partial.1 = (f32[32,1024]{1,0:T(8,128)S(1)}, f32[32,1024]{1,0:T(8,128)S(1)}) custom-call(s32[1]{0:T(128)} %bitcast.index, bf16[8,256,128]{2,1,0:T(8,128)(2,1)S(1)} %bitcast.8, bf16[1024,1024]{1,0:T(8,128)(2,1)S(1)} %get-tuple-element.15.moved, f32[32,1024]{1,0:T(8,128)S(1)} %get-tuple-element.16.prod, f32[32,1024]{1,0:T(8,128)S(1)} %get-tuple-element.17.sol, ...), custom_call_target="tpu_custom_call" | custom-call | flops 150000000 | bytes 3000000 | tf_op jit(solution)/shard_map/partial/pallas_call | solution.py:344
  95.9 1.0 %last.1 = (f32[32,1024]{1,0:T(8,128)}, f32[32,1024]{1,0:T(8,128)}) custom-call(s32[1]{0:T(128)} %bitcast.index, bf16[256,128]{1,0:T(8,128)(2,1)S(1)} %slice_bitcast_fusion.coupling, bf16[1024,128]{1,0:T(8,128)(2,1)S(1)} %slice.286.moved, f32[32,1024]{1,0:T(8,128)S(1)} %get-tuple-element.24.prod, f32[32,1024]{1,0:T(8,128)S(1)} %get-tuple-element.25.sol, ...), custom_call_target="tpu_custom_call" | custom-call | flops 30000000 | bytes 1000000 | tf_op jit(solution)/shard_map/last/pallas_call | solution.py:354
  (135 shorter events, 13.1 us)
Async XLA Ops:
  8.8 10.0 %collective-permute-start = (bf16[32,1152]{1,0:T(8,128)(2,1)}, bf16[32,1152]{1,0:T(8,128)(2,1)}, u32[]{:S(2)}, u32[]{:S(2)}) collective-permute-start(bf16[32,1152]{1,0:T(8,128)(2,1)} %get-tuple-element.18), channel_id=1, source_target_pairs={{0,1},{1,0},{2,3},{3,2},{4,5},{5,4},{6,7},{7,6},{8,9},{9,8},{10,11... | collective-permute-start | bytes 221192 | tf_op jit(solution)/shard_map/ppermute | solution.py:179
  18.7 13.3 %copy-start.5 = (bf16[256,768]{1,0:T(8,128)(2,1)S(1)}, bf16[256,768]{1,0:T(8,128)(2,1)}, u32[]{:S(2)}) copy-start(bf16[256,768]{1,0:T(8,128)(2,1)} %copy-done.4) | copy-start | bytes 1179652
  18.7 3.6 %collective-permute-start.1 = (bf16[128,1280]{1,0:T(8,128)(2,1)S(1)}, bf16[128,1280]{1,0:T(8,128)(2,1)S(1)}, u32[]{:S(2)}, u32[]{:S(2)}) collective-permute-start(bf16[128,1280]{1,0:T(8,128)(2,1)S(1)} %constant_dynamic-slice_fusion.3), channel_id=1, source_target_pairs={{0,4},{1,5},{2,6},{3,7},{4,0},{5,1},{6,2},{7,3},{8,12},{9,13},{10,... | collective-permute-start | bytes 983048 | tf_op jit(solution)/shard_map/ppermute | solution.py:179
  22.4 9.4 %collective-permute-start.2 = (bf16[32,2304]{1,0:T(8,128)(2,1)S(1)}, bf16[32,2304]{1,0:T(8,128)(2,1)S(1)}, u32[]{:S(2)}, u32[]{:S(2)}) collective-permute-start(bf16[32,2304]{1,0:T(8,128)(2,1)S(1)} %pad_maximum_fusion.4), channel_id=1, source_target_pairs={{0,3},{1,2},{2,1},{3,0},{4,7},{5,6},{6,5},{7,4},{8,11},{9,10},{10,... | collective-permute-start | bytes 442376 | tf_op jit(solution)/shard_map/ppermute | solution.py:179
  24.7 7.1 %collective-permute-start.3 = (bf16[32,1408]{1,0:T(8,128)(2,1)S(1)}, bf16[32,1408]{1,0:T(8,128)(2,1)S(1)}, u32[]{:S(2)}, u32[]{:S(2)}) collective-permute-start(bf16[32,1408]{1,0:T(8,128)(2,1)S(1)} %get-tuple-element.111), channel_id=1, source_target_pairs={{0,2},{1,3},{2,0},{3,1},{4,6},{5,7},{6,4},{7,5},{8,10},{9,11},{10,... | collective-permute-start | bytes 270344 | tf_op jit(solution)/shard_map/ppermute | solution.py:179
  25.6 6.3 %collective-permute-start.4 = (bf16[32,1408]{1,0:T(8,128)(2,1)S(1)}, bf16[32,1408]{1,0:T(8,128)(2,1)S(1)}, u32[]{:S(2)}, u32[]{:S(2)}) collective-permute-start(bf16[32,1408]{1,0:T(8,128)(2,1)S(1)} %get-tuple-element.112), channel_id=1, source_target_pairs={{0,1},{1,0},{2,3},{3,2},{4,5},{5,4},{6,7},{7,6},{8,9},{9,8},{10,11... | collective-permute-start | bytes 270344 | tf_op jit(solution)/shard_map/ppermute | solution.py:179
  32.1 6.4 %collective-permute-start.5 = (bf16[32,768]{1,0:T(8,128)(2,1)S(1)}, bf16[32,768]{1,0:T(8,128)(2,1)S(1)}, u32[]{:S(2)}, u32[]{:S(2)}) collective-permute-start(bf16[32,768]{1,0:T(8,128)(2,1)S(1)} %get-tuple-element.113), channel_id=1, source_target_pairs={{0,1},{1,0},{2,3},{3,2},{4,5},{5,4},{6,7},{7,6},{8,9},{9,8},{10,11... | collective-permute-start | bytes 147464 | tf_op jit(solution)/shard_map/ppermute | solution.py:179
  32.8 5.7 %collective-permute-start.6 = (bf16[32,768]{1,0:T(8,128)(2,1)S(1)}, bf16[32,768]{1,0:T(8,128)(2,1)S(1)}, u32[]{:S(2)}, u32[]{:S(2)}) collective-permute-start(bf16[32,768]{1,0:T(8,128)(2,1)S(1)} %get-tuple-element.113), channel_id=1, source_target_pairs={{0,2},{1,3},{2,0},{3,1},{4,6},{5,7},{6,4},{7,5},{8,10},{9,11},{10,... | collective-permute-start | bytes 147464 | tf_op jit(solution)/shard_map/ppermute | solution.py:179
  35.9 5.3 %collective-permute-start.7 = (bf16[32,768]{1,0:T(8,128)(2,1)S(1)}, bf16[32,768]{1,0:T(8,128)(2,1)S(1)}, u32[]{:S(2)}, u32[]{:S(2)}) collective-permute-start(bf16[32,768]{1,0:T(8,128)(2,1)S(1)} %get-tuple-element.113), channel_id=1, source_target_pairs={{0,3},{1,2},{2,1},{3,0},{4,7},{5,6},{6,5},{7,4},{8,11},{9,10},{10,... | collective-permute-start | bytes 147464 | tf_op jit(solution)/shard_map/ppermute | solution.py:179
  37.0 4.5 %collective-permute-start.9 = (bf16[32,1280]{1,0:T(8,128)(2,1)S(1)}, bf16[32,1280]{1,0:T(8,128)(2,1)S(1)}, u32[]{:S(2)}, u32[]{:S(2)}) collective-permute-start(bf16[32,1280]{1,0:T(8,128)(2,1)S(1)} %fusion.51), channel_id=1, source_target_pairs={{0,8},{1,9},{2,10},{3,11},{4,12},{5,13},{6,14},{7,15},{8,0},{9,1},... | collective-permute-start | bytes 245768 | tf_op jit(solution)/shard_map/ppermute | solution.py:179
  41.6 5.4 %collective-permute-start.10 = (bf16[32,768]{1,0:T(8,128)(2,1)S(1)}, bf16[32,768]{1,0:T(8,128)(2,1)S(1)}, u32[]{:S(2)}, u32[]{:S(2)}) collective-permute-start(bf16[32,768]{1,0:T(8,128)(2,1)S(1)} %slice.633), channel_id=1, source_target_pairs={{0,24},{1,25},{2,26},{3,27},{4,28},{5,29},{6,30},{7,31},{8,16},{9,... | collective-permute-start | bytes 147464 | tf_op jit(solution)/shard_map/ppermute | solution.py:179
  44.4 3.1 %collective-permute-start.8 = (bf16[32,1536]{1,0:T(8,128)(2,1)S(1)}, bf16[32,1536]{1,0:T(8,128)(2,1)S(1)}, u32[]{:S(2)}, u32[]{:S(2)}) collective-permute-start(bf16[32,1536]{1,0:T(8,128)(2,1)S(1)} %pad_maximum_fusion.7), channel_id=1, source_target_pairs={{0,4},{1,5},{2,6},{3,7},{4,0},{5,1},{6,2},{7,3},{8,12},{9,13},{10,... | collective-permute-start | bytes 294920 | tf_op jit(solution)/shard_map/ppermute | solution.py:179
  47.0 4.1 %collective-permute-start.18 = (bf16[32,384]{1,0:T(8,128)(2,1)S(1)}, bf16[32,384]{1,0:T(8,128)(2,1)S(1)}, u32[]{:S(2)}, u32[]{:S(2)}) collective-permute-start(bf16[32,384]{1,0:T(8,128)(2,1)S(1)} %get-tuple-element.98), channel_id=1, source_target_pairs={{0,32},{1,33},{2,34},{3,35},{4,36},{5,37},{6,38},{7,39},{8,40},{9,... | collective-permute-start | bytes 73736 | tf_op jit(solution)/shard_map/ppermute | solution.py:179
  51.1 8.2 %collective-permute-start.19 = (bf16[32,128]{1,0:T(8,128)(2,1)S(1)}, bf16[32,128]{1,0:T(8,128)(2,1)S(1)}, u32[]{:S(2)}, u32[]{:S(2)}) collective-permute-start(bf16[32,128]{1,0:T(8,128)(2,1)S(1)} %slice.638), channel_id=1, source_target_pairs={{0,64},{1,65},{2,66},{3,67},{4,68},{5,69},{6,70},{7,71},{8,72},{9,... | collective-permute-start | bytes 24584 | tf_op jit(solution)/shard_map/ppermute | solution.py:179
  54.5 7.1 %collective-permute-start.11 = (bf16[32,1536]{1,0:T(8,128)(2,1)S(1)}, bf16[32,1536]{1,0:T(8,128)(2,1)S(1)}, u32[]{:S(2)}, u32[]{:S(2)}) collective-permute-start(bf16[32,1536]{1,0:T(8,128)(2,1)S(1)} %pad_maximum_fusion.8), channel_id=1, source_target_pairs={{0,1},{1,0},{2,3},{3,2},{4,5},{5,4},{6,7},{7,6},{8,9},{9,8},{10,11... | collective-permute-start | bytes 294920 | tf_op jit(solution)/shard_map/ppermute | solution.py:179
  54.6 8.9 %collective-permute-start.12 = (bf16[32,1536]{1,0:T(8,128)(2,1)S(1)}, bf16[32,1536]{1,0:T(8,128)(2,1)S(1)}, u32[]{:S(2)}, u32[]{:S(2)}) collective-permute-start(bf16[32,1536]{1,0:T(8,128)(2,1)S(1)} %pad_maximum_fusion.8), channel_id=1, source_target_pairs={{0,2},{1,3},{2,0},{3,1},{4,6},{5,7},{6,4},{7,5},{8,10},{9,11},{10,... | collective-permute-start | bytes 294920 | tf_op jit(solution)/shard_map/ppermute | solution.py:179
  58.2 5.8 %collective-permute-start.13 = (bf16[32,1536]{1,0:T(8,128)(2,1)S(1)}, bf16[32,1536]{1,0:T(8,128)(2,1)S(1)}, u32[]{:S(2)}, u32[]{:S(2)}) collective-permute-start(bf16[32,1536]{1,0:T(8,128)(2,1)S(1)} %pad_maximum_fusion.8), channel_id=1, source_target_pairs={{0,3},{1,2},{2,1},{3,0},{4,7},{5,6},{6,5},{7,4},{8,11},{9,10},{10,... | collective-permute-start | bytes 294920 | tf_op jit(solution)/shard_map/ppermute | solution.py:179
  59.3 5.1 %collective-permute-start.20 = (bf16[32,384]{1,0:T(8,128)(2,1)S(1)}, bf16[32,384]{1,0:T(8,128)(2,1)S(1)}, u32[]{:S(2)}, u32[]{:S(2)}) collective-permute-start(bf16[32,384]{1,0:T(8,128)(2,1)S(1)} %pad_maximum_fusion.19), channel_id=1, source_target_pairs={{0,3},{1,2},{2,1},{3,0},{4,7},{5,6},{6,5},{7,4},{8,11},{9,10},{10,... | collective-permute-start | bytes 73736 | tf_op jit(solution)/shard_map/ppermute | solution.py:179
  61.5 5.3 %collective-permute-start.21 = (bf16[32,384]{1,0:T(8,128)(2,1)S(1)}, bf16[32,384]{1,0:T(8,128)(2,1)S(1)}, u32[]{:S(2)}, u32[]{:S(2)}) collective-permute-start(bf16[32,384]{1,0:T(8,128)(2,1)S(1)} %pad_maximum_fusion.19), channel_id=1, source_target_pairs={{0,2},{1,3},{2,0},{3,1},{4,6},{5,7},{6,4},{7,5},{8,10},{9,11},{10,... | collective-permute-start | bytes 73736 | tf_op jit(solution)/shard_map/ppermute | solution.py:179
  61.6 5.3 %collective-permute-start.22 = (bf16[32,384]{1,0:T(8,128)(2,1)S(1)}, bf16[32,384]{1,0:T(8,128)(2,1)S(1)}, u32[]{:S(2)}, u32[]{:S(2)}) collective-permute-start(bf16[32,384]{1,0:T(8,128)(2,1)S(1)} %pad_maximum_fusion.19), channel_id=1, source_target_pairs={{0,1},{1,0},{2,3},{3,2},{4,5},{5,4},{6,7},{7,6},{8,9},{9,8},{10,11... | collective-permute-start | bytes 73736 | tf_op jit(solution)/shard_map/ppermute | solution.py:179
  64.2 2.8 %collective-permute-start.14 = (bf16[32,4224]{1,0:T(8,128)(2,1)S(1)}, bf16[32,4224]{1,0:T(8,128)(2,1)S(1)}, u32[]{:S(2)}, u32[]{:S(2)}) collective-permute-start(bf16[32,4224]{1,0:T(8,128)(2,1)S(1)} %get-tuple-element.62), channel_id=1, source_target_pairs={{0,4},{1,5},{2,6},{3,7},{4,0},{5,1},{6,2},{7,3},{8,12},{9,13},{10,... | collective-permute-start | bytes 811016 | tf_op jit(solution)/shard_map/ppermute | solution.py:179
  66.9 8.2 %collective-permute-start.23 = (bf16[32,1536]{1,0:T(8,128)(2,1)S(1)}, bf16[32,1536]{1,0:T(8,128)(2,1)S(1)}, u32[]{:S(2)}, u32[]{:S(2)}) collective-permute-start(bf16[32,1536]{1,0:T(8,128)(2,1)S(1)} %pad_maximum_fusion.9), channel_id=1, source_target_pairs={{0,4},{1,5},{2,6},{3,7},{4,0},{5,1},{6,2},{7,3},{8,12},{9,13},{10,... | collective-permute-start | bytes 294920 | tf_op jit(solution)/shard_map/ppermute | solution.py:179
  67.1 4.9 %collective-permute-start.15 = (bf16[32,1280]{1,0:T(8,128)(2,1)S(1)}, bf16[32,1280]{1,0:T(8,128)(2,1)S(1)}, u32[]{:S(2)}, u32[]{:S(2)}) collective-permute-start(bf16[32,1280]{1,0:T(8,128)(2,1)S(1)} %pad_maximum_fusion.12), channel_id=1, source_target_pairs={{0,8},{1,9},{2,10},{3,11},{4,12},{5,13},{6,14},{7,15},{8,0},{9,1},... | collective-permute-start | bytes 245768 | tf_op jit(solution)/shard_map/ppermute | solution.py:179
  67.5 15.4 %copy-start.20 = (bf16[32,1024]{1,0:T(8,128)(2,1)S(1)}, bf16[32,1024]{1,0:T(8,128)(2,1)}, u32[]{:S(2)}) copy-start(bf16[32,1024]{1,0:T(8,128)(2,1)} %copy-done.19) | copy-start | bytes 196612
  67.5 15.4 %copy-start.13 = (bf16[32,1024]{1,0:T(8,128)(2,1)S(1)}, bf16[32,1024]{1,0:T(8,128)(2,1)}, u32[]{:S(2)}) copy-start(bf16[32,1024]{1,0:T(8,128)(2,1)} %rhs.3) | copy-start | bytes 196612
  67.5 15.4 %copy-start.15 = (s32[1,1024]{1,0:T(1,128)S(1)}, s32[1,1024]{1,0:T(1,128)}, u32[]{:S(2)}) copy-start(s32[1,1024]{1,0:T(1,128)} %order.3) | copy-start | bytes 12292
  67.6 15.4 %copy-start.16 = (bf16[1024,1024]{1,0:T(8,128)(2,1)S(1)}, bf16[1024,1024]{1,0:T(8,128)(2,1)}, u32[]{:S(2)}) copy-start(bf16[1024,1024]{1,0:T(8,128)(2,1)} %block.1) | copy-start | bytes 6291460
  67.6 15.4 %copy-start.18 = (bf16[8,1024,128]{2,1,0:T(8,128)(2,1)S(1)}, bf16[8,1024,128]{2,1,0:T(8,128)(2,1)}, u32[]{:S(2)}) copy-start(bf16[8,1024,128]{2,1,0:T(8,128)(2,1)} %left.3) | copy-start | bytes 6291460
  72.3 5.6 %collective-permute-start.16 = (bf16[32,1024]{1,0:T(8,128)(2,1)S(1)}, bf16[32,1024]{1,0:T(8,128)(2,1)S(1)}, u32[]{:S(2)}, u32[]{:S(2)}) collective-permute-start(bf16[32,1024]{1,0:T(8,128)(2,1)S(1)} %pad_maximum_fusion.15), channel_id=1, source_target_pairs={{0,24},{1,25},{2,26},{3,27},{4,28},{5,29},{6,30},{7,31},{8,16},{9,... | collective-permute-start | bytes 196616 | tf_op jit(solution)/shard_map/ppermute | solution.py:179
  78.1 4.2 %collective-permute-start.17 = (bf16[32,768]{1,0:T(8,128)(2,1)S(1)}, bf16[32,768]{1,0:T(8,128)(2,1)S(1)}, u32[]{:S(2)}, u32[]{:S(2)}) collective-permute-start(bf16[32,768]{1,0:T(8,128)(2,1)S(1)} %pad_maximum_fusion.17), channel_id=1, source_target_pairs={{0,32},{1,33},{2,34},{3,35},{4,36},{5,37},{6,38},{7,39},{8,40},{9,... | collective-permute-start | bytes 147464 | tf_op jit(solution)/shard_map/ppermute | solution.py:179
  82.5 6.3 %collective-permute-start.24 = (bf16[32,512]{1,0:T(8,128)(2,1)S(1)}, bf16[32,512]{1,0:T(8,128)(2,1)S(1)}, u32[]{:S(2)}, u32[]{:S(2)}) collective-permute-start(bf16[32,512]{1,0:T(8,128)(2,1)S(1)} %pad_maximum_fusion.18), channel_id=1, source_target_pairs={{0,64},{1,65},{2,66},{3,67},{4,68},{5,69},{6,70},{7,71},{8,72},{9,... | collective-permute-start | bytes 98312 | tf_op jit(solution)/shard_map/ppermute | solution.py:179
  89.0 6.9 %collective-permute-start.25 = (bf16[32,256]{1,0:T(8,128)(2,1)S(1)}, bf16[32,256]{1,0:T(8,128)(2,1)S(1)}, u32[]{:S(2)}, u32[]{:S(2)}) collective-permute-start(bf16[32,256]{1,0:T(8,128)(2,1)S(1)} %pad_maximum_fusion.24), channel_id=1, source_target_pairs={{0,224},{1,225},{2,226},{3,227},{4,228},{5,229},{6,230},{7,231},{8... | collective-permute-start | bytes 49160 | tf_op jit(solution)/shard_map/ppermute | solution.py:179
  (15 other events, 38.0 us)

commit v2 on v0

v2 whole, which is shorter than its diff:
```python
import functools

import jax
import jax.numpy as jnp
from jax import lax
from jax.experimental import pallas as pl
from jax.experimental.pallas import tpu as pltpu
from jax.sharding import PartitionSpec as P

BF = jnp.bfloat16
F32 = jnp.float32
LANE = 128
VMEM = pl.BlockSpec(memory_space=pltpu.VMEM)
SMEM = pl.BlockSpec(memory_space=pltpu.SMEM)
HBM = pl.BlockSpec(memory_space=pltpu.HBM)
NT = (((1,), (1,)), ((), ()))
LEVELS = 8
SUMMED = 3
BEFORE = 6


def scale(level):
    return 2.0 ** (-0.5 * level)


def dot(a, b):
    return jnp.dot(a, b, preferred_element_type=F32)


def dot_t(a, b):
    return lax.dot_general(a, b, NT, preferred_element_type=F32)


def one_hot(order, low, width):
    rows = lax.broadcasted_iota(jnp.int32, (order.shape[1], width), 0)
    return jnp.where(rows == order[:, low : low + width], 1.0, 0.0).astype(BF)


def columns(ref, level):
    return ref.at[:, pl.ds(level * LANE, LANE)]


def coefficient_kernel(
    live, order, vec, rhs, right, first_out, solve_out, tree_out, right_cat, fields, order_in, sems
):
    nvec = vec.shape[0]
    points = vec.shape[1]
    small = [
        pltpu.make_async_copy(order, order_in, sems.at[LEVELS]),
        pltpu.make_async_copy(vec, fields.at[pl.ds(0, nvec)], sems.at[LEVELS + 1]),
        pltpu.make_async_copy(rhs, fields.at[pl.ds(nvec, nvec)], sems.at[LEVELS + 2]),
    ]
    copies = [
        pltpu.make_async_copy(right.at[level], columns(right_cat, level), sems.at[level])
        for level in range(LEVELS)
    ]
    for copy in small + copies:
        copy.start()
    for copy in small:
        copy.wait()
    chunk = 256
    for low in range(0, points, chunk):
        moved = dot(fields[...], one_hot(order_in[...], low, chunk))
        slot = lax.broadcasted_iota(jnp.int32, moved.shape, 1) + low
        tree_out[:, low : low + chunk] = jnp.where(slot < live[0], moved, 0.0).astype(BF)
    for level in range(0, LEVELS, 2):
        copies[level].wait()
        copies[level + 1].wait()
        pair = dot(tree_out[...], right_cat[:, level * LANE : (level + 2) * LANE])
        for now in (level, level + 1):
            part = pair[:, (now - level) * LANE : (now - level + 1) * LANE] * scale(now)
            first_out[:, (now + 1) * LANE : (now + 2) * LANE] = part[:nvec].astype(BF)
            if now == 0:
                first_out[:, :LANE] = part[nvec:].astype(BF)
            else:
                solve_out[:, (now - 1) * LANE : now * LANE] = part[nvec:]


def update_kernel(live, index, coupling, left, right, *rest):
    outs, (right_cat, turned, left_cat, held, sems) = rest[: SUMMED + 3], rest[SUMMED + 3 :]
    home, away, bits = outs[SUMMED:]
    rights = {
        level: pltpu.make_async_copy(right.at[level], columns(right_cat, level - 1), sems.at[0, level])
        for level in range(1, LEVELS)
    }
    lefts = [
        pltpu.make_async_copy(left.at[level], columns(left_cat, level), sems.at[1, level])
        for level in range(LEVELS - 1)
    ]
    coupling_copy = pltpu.make_async_copy(coupling, held, sems.at[0, 0])
    for level in range(LEVELS - 1, 0, -1):
        rights[level].start()
    for copy in lefts[::-1]:
        copy.start()
    coupling_copy.start()
    levels = lax.broadcasted_iota(jnp.int32, bits.shape, 0)
    bits[...] = (lax.shift_right_logical(jnp.full(bits.shape, index[0], jnp.int32), levels) & 1).astype(F32)
    for level in range(LEVELS - 1, 0, -1):
        rights[level].wait()
        turned[(level - 1) * LANE : level * LANE, :] = right_cat[:, (level - 1) * LANE : level * LANE].T
    second_core = (lax.shift_right_logical(index[0], 2) & 1) == 1
    for low in range(LEVELS - 2, -1, -2):
        levels = [level for level in (low, low + 1) if level < LEVELS - 1]
        for level in levels[::-1]:
            lefts[level].wait()
        if low == LEVELS - 2:
            coupling_copy.wait()
        block = left_cat[:, low * LANE : (low + len(levels)) * LANE]
        rows = lax.broadcasted_iota(jnp.int32, block.shape, 0)
        block = jnp.where(rows < live[0], block.astype(F32), 0.0).astype(BF)
        gram = dot(turned[low * LANE :, :], block)
        for level in levels:
            side = slice((level - low) * LANE, (level - low + 1) * LANE)
            own = jnp.concatenate(
                [
                    (gram[(now - low - 1) * LANE : (now - low) * LANE, side] * scale(now)).astype(BF)
                    for now in range(level + 1, LEVELS)
                ],
                axis=0,
            )
            update = dot_t(canonical(held, index, level), own).astype(BF)
            if level < SUMMED:
                outs[level][...] = update
            else:
                at = sum(LEVELS - 1 - below for below in range(SUMMED, level)) * LANE
                to = slice(at, at + update.shape[1])
                first, second = update[:LANE], update[LANE:]
                home[:, to] = jnp.where(second_core, second, first)
                away[:, to] = jnp.where(second_core, first, second)


def canonical(coupling, index, level):
    held = coupling[level]
    swapped = jnp.concatenate([held[LANE:], held[:LANE]], axis=0)
    second = (lax.shift_right_logical(index[0], level) & 1) == 1
    return jnp.where(second, swapped, held)


def direct_kernel(live, order, tree, block, prod_out, hot_out):
    points = order.shape[1]
    nvec = prod_out.shape[0]
    chunk = 256
    for low in range(0, points, chunk):
        hot_out[:, low : low + chunk] = one_hot(order[...], low, chunk)
    prod_out[...] = dot_t(tree[:nvec, :], block[...])


def masked_rows(block, live):
    rows = lax.broadcasted_iota(jnp.int32, block.shape, 0)
    return jnp.where(rows < live[0], block.astype(F32), 0.0).astype(BF)


def moved_kernel(live, hot, left, moved_out, left_cat, sems):
    copies = [
        pltpu.make_async_copy(left.at[level], columns(left_cat, level - BEFORE), sems.at[level - BEFORE])
        for level in range(BEFORE, LEVELS)
    ]
    for copy in copies:
        copy.start()
    for copy in copies:
        copy.wait()
    moved_out[...] = dot(hot[...], masked_rows(left_cat[...], live)).astype(BF)


def partial_kernel(live, index, coupling, left, tree, direct, hot, *rest):
    siblings, joined = rest[:BEFORE], rest[BEFORE : 2 * BEFORE]
    prod_out, sol_out, coupling_out, left_cat, sems = rest[2 * BEFORE :]
    copies = [
        pltpu.make_async_copy(left.at[level], columns(left_cat, level), sems.at[level])
        for level in range(BEFORE)
    ]
    for copy in copies:
        copy.start()
    for level in range(BEFORE, LEVELS):
        at = (level - BEFORE) * 2 * LANE
        coupling_out[at : at + 2 * LANE, :] = canonical(coupling, index, level)
    coupled = [dot(joined[level][...], canonical(coupling, index, level)).astype(BF) for level in range(BEFORE)]
    siblings = [block[...] for block in siblings]
    terms = jnp.concatenate([jnp.concatenate(siblings, axis=1), jnp.concatenate(coupled, axis=1)], axis=0)
    for copy in copies:
        copy.wait()
    terms = dot_t(terms, left_cat[...])
    nvec = direct.shape[0]
    total = jnp.concatenate([direct[...] + terms[:nvec], tree[nvec:, :].astype(F32) - terms[nvec:]], axis=0)
    slot = lax.broadcasted_iota(jnp.int32, total.shape, 1)
    total = jnp.where(slot < live[0], total, 0.0)
    high = total.astype(BF)
    low = (total - high.astype(F32)).astype(BF)
    both = dot_t(jnp.concatenate([high, low], axis=0), hot[...])
    prod_out[...] = both[:nvec] + both[2 * nvec : 3 * nvec]
    sol_out[...] = both[nvec : 2 * nvec] + both[3 * nvec :]


def last_kernel(coupling, moved, prod, sol, *rest):
    count = LEVELS - BEFORE
    siblings, joined, (prod_out, sol_out) = rest[:count], rest[count : 2 * count], rest[2 * count :]
    coupled = [
        dot(joined[at][...], coupling[2 * at * LANE : 2 * (at + 1) * LANE, :]).astype(BF) for at in range(count)
    ]
    siblings = [block[...] for block in siblings]
    terms = jnp.concatenate([jnp.concatenate(siblings, axis=1), jnp.concatenate(coupled, axis=1)], axis=0)
    terms = dot_t(terms, moved[...])
    nvec = prod.shape[0]
    prod_out[...] = prod[...] + terms[:nvec]
    sol_out[...] = sol[...] - terms[nvec:]


def params(mib):
    return pltpu.CompilerParams(vmem_limit_bytes=mib << 20)


def shape(rows, lanes, dtype=BF):
    return jax.ShapeDtypeStruct((rows, lanes), dtype)


def swap(block, mask):
    count = lax.axis_size("leaf") * lax.axis_size("sub")
    return lax.ppermute(block, ("leaf", "sub"), [(i, i ^ mask) for i in range(count)])


def cols(block, low, high=None):
    return block[:, low * LANE : None if high is None else high * LANE]


def cat(*blocks):
    return jnp.concatenate([block.astype(BF) for block in blocks], axis=1)


def after(block, *others):
    return lax.optimization_barrier((block,) + others)[0]


def per_device(vectors, right_side, tree_order, live_counts, leaf_block, left_basis, right_bases, coupling):
    nvec, points = vectors.shape
    index = lax.axis_index("leaf") * lax.axis_size("sub") + lax.axis_index("sub")
    index_1 = index.astype(jnp.int32).reshape(1)
    coupling = coupling[0]

    def pick(level, if_set, if_clear):
        side = jnp.broadcast_to(bits[level : level + 1, : if_set.shape[1]], if_set.shape)
        return jnp.where(side > 0, if_set, if_clear)

    def join(mine, other, level):
        return cat(pick(level, other, mine), pick(level, mine, other))

    def whole_of(mine, theirs):
        width = mine.shape[1] // 4
        mine, theirs = (
            jnp.concatenate([half[:, at : at + width] for at in range(0, 4 * width, width)], axis=0)
            for half in (mine, theirs)
        )
        return jnp.concatenate([pick(2, theirs, mine), pick(2, mine, theirs)], axis=0)

    def by_sub(blocks):
        even = [pick(0, blocks[i ^ 1], blocks[i]) for i in range(4)]
        return [pick(1, even[i ^ 2], even[i]) for i in range(4)]

    first, coef, tree = pl.pallas_call(
        coefficient_kernel,
        out_shape=(
            shape(nvec, 9 * LANE),
            shape(nvec, 7 * LANE, F32),
            shape(2 * nvec, points),
        ),
        in_specs=[SMEM, HBM, HBM, HBM, HBM],
        out_specs=(VMEM,) * 3,
        scratch_shapes=[
            pltpu.VMEM((points, LEVELS * LANE), BF),
            pltpu.VMEM((2 * nvec, points), BF),
            pltpu.VMEM((1, points), jnp.int32),
            pltpu.SemaphoreType.DMA((LEVELS + 3,)),
        ],
        compiler_params=params(56),
        cost_estimate=pl.CostEstimate(flops=300_000_000, bytes_accessed=2_500_000, transcendentals=0),
        name="coefficients",
    )(after(live_counts, index_1), tree_order, vectors, right_side, right_bases)

    widths = [LEVELS - 1 - level for level in range(SUMMED)]
    summed = sum(LEVELS - 1 - level for level in range(SUMMED, LEVELS - 1))
    update_0, update_1, update_2, home, away, bits = pl.pallas_call(
        update_kernel,
        out_shape=tuple(shape(2 * LANE, width * LANE) for width in widths)
        + (shape(LANE, summed * LANE),) * 2
        + (shape(LEVELS, 2 * points, F32),),
        in_specs=[SMEM, SMEM, HBM, HBM, HBM],
        out_specs=(VMEM,) * 6,
        scratch_shapes=[
            pltpu.VMEM((points, 7 * LANE), BF),
            pltpu.VMEM((7 * LANE, points), BF),
            pltpu.VMEM((points, 7 * LANE), BF),
            pltpu.VMEM((LEVELS, 2 * LANE, LANE), BF),
            pltpu.SemaphoreType.DMA((2, LEVELS)),
        ],
        compiler_params=params(52),
        cost_estimate=pl.CostEstimate(flops=1_300_000_000, bytes_accessed=5_000_000, transcendentals=0),
        name="updates",
    )(live_counts, index_1, coupling, left_basis, right_bases)

    siblings, joined = [], []

    got = swap(first, 1)
    joined.append(join(cols(first, 0, 1), cols(got, 0, 1), 0))
    siblings.append(cols(got, 1, 2))
    prod = cols(first, 2).astype(F32) + cols(got, 2).astype(F32)
    coef = coef - dot(joined[0], update_0)

    halves = (home.astype(F32) + swap(away, 4).astype(F32)).astype(BF)
    piece = halves.shape[0] // 4
    rows_of = by_sub([halves[i * piece : (i + 1) * piece] for i in range(4)])

    mine = cols(coef, 0, 1).astype(BF)
    sent = {mask: cat(mine, rows_of[mask]) for mask in (1, 2, 3)}
    direct, hot = pl.pallas_call(
        direct_kernel,
        out_shape=(shape(nvec, points, F32), shape(points, points)),
        in_specs=[SMEM, VMEM, VMEM, VMEM],
        out_specs=(VMEM, VMEM),
        compiler_params=params(12),
        cost_estimate=pl.CostEstimate(flops=2_000_000_000, bytes_accessed=2_000_000, transcendentals=0),
        name="direct",
    )(after(live_counts, sent[3]), tree_order, tree, leaf_block)
    got = {mask: swap(sent[mask], mask) for mask in (1, 2, 3)}
    parts = {mask: cols(block, 0, 1).astype(F32) for mask, block in got.items()}
    pieces = rows_of[0].astype(F32)
    for mask in (1, 2, 3):
        pieces = pieces + cols(got[mask], 1).astype(F32)
    pieces = pieces.astype(BF)
    upper = cols(pieces, 4)
    near = swap(pieces, 8).astype(F32)
    upper = upper.astype(F32) + cols(near, 4) + swap(upper, 16).astype(F32) + swap(upper, 24).astype(F32)
    pieces = cat(cols(pieces, 0, 4).astype(F32) + cols(near, 0, 4), upper)
    joined.append(join((mine.astype(F32) + parts[1]).astype(BF), (parts[2] + parts[3]).astype(BF), 1))
    coef = cols(coef, 1) - dot(joined[1], update_1)
    coef, direct, hot = lax.optimization_barrier((coef, direct, hot))

    mine = cols(coef, 0, 1).astype(BF)
    with_prod = cat(mine, prod)
    got = {1: swap(mine, 1), 2: swap(mine, 2), 3: swap(with_prod, 3)}
    total = mine.astype(F32)
    for mask in (1, 2, 3):
        total = total + cols(got[mask], 0, 1).astype(F32)
    total = total.astype(BF)
    got_prod = cols(got[3], 1)
    siblings.append(cols(got_prod, 0, 1))
    prod = cols(prod, 1) + cols(got_prod, 1).astype(F32)
    got = swap(cat(total, prod), 4)
    got_total, got_prod = cols(got, 0, 1), cols(got, 1)
    joined.append(join(total, got_total, 2))
    siblings.append(cols(got_prod, 0, 1))
    prod = cols(prod, 1) + cols(got_prod, 1).astype(F32)
    coef = cols(coef, 1) - dot(joined[2], update_2)

    sent = cat(coef, pieces)
    got = {mask: swap(sent, mask) for mask in (1, 2, 3)}
    got[0] = sent
    lead = LEVELS - SUMMED
    total = sum(cols(got[mask], 0, lead).astype(F32) for mask in range(4))
    quarters = by_sub([cols(got[mask], lead) for mask in range(4)])
    sent = cat(total, *quarters)
    got = swap(sent, 4)
    total = total + cols(got, 0, lead).astype(F32)
    whole = whole_of(cols(sent, lead), cols(got, lead))
    updates_of = {3: cols(whole, 0, 4), 4: cols(whole, 4, 7)}

    def exchange(level, mask, sent, total, prod):
        left_over = LEVELS - level
        got = swap(sent, mask)
        got_total, got_prod = cols(got, 0, left_over), cols(got, left_over)
        joined.append(join(cols(sent, 0, 1), cols(got_total, 0, 1), level))
        siblings.append(cols(got_prod, 0, 1))
        prod = cols(prod, 1) + cols(got_prod, 1).astype(F32)
        return cols(total, 1) + cols(got_total, 1).astype(F32), prod

    def apply(level, total):
        return total - dot(joined[level], updates_of[level])

    sent = cat(total, prod)
    moved = pl.pallas_call(
        moved_kernel,
        out_shape=shape(points, (LEVELS - BEFORE) * LANE),
        in_specs=[SMEM, VMEM, HBM],
        out_specs=VMEM,
        scratch_shapes=[
            pltpu.VMEM((points, (LEVELS - BEFORE) * LANE), BF),
            pltpu.SemaphoreType.DMA((LEVELS - BEFORE,)),
        ],
        compiler_params=params(12),
        cost_estimate=pl.CostEstimate(flops=1_500_000_000, bytes_accessed=2_000_000, transcendentals=0),
        name="moved",
    )(after(live_counts, sent), hot, left_basis)
    late = after(cols(whole, 7), sent)
    late = late.astype(F32) + swap(late, 32).astype(F32)
    updates_of[5] = cols(late, 0, 2).astype(BF)
    total, prod = exchange(3, 8, sent, total, prod)
    total = apply(3, total)
    total, moved = lax.optimization_barrier((total, moved))

    sent = cat(total, prod)
    late = after(cols(late, 2).astype(BF), sent)
    late = (late.astype(F32) + swap(late, 64).astype(F32)).astype(BF)
    total, prod = exchange(4, 24, sent, total, prod)
    total = apply(4, total)

    total, prod = exchange(5, 32, cat(total, prod), total, prod)
    total = apply(5, total)
    total, updates_of[6] = lax.optimization_barrier((total, late))

    part_prod, part_sol, last_coupling = pl.pallas_call(
        partial_kernel,
        out_shape=(shape(nvec, points, F32),) * 2 + (shape((LEVELS - BEFORE) * 2 * LANE, LANE),),
        in_specs=[SMEM, SMEM, VMEM, HBM] + [VMEM] * (3 + 2 * BEFORE),
        out_specs=(VMEM,) * 3,
        scratch_shapes=[
            pltpu.VMEM((points, BEFORE * LANE), BF),
            pltpu.SemaphoreType.DMA((BEFORE,)),
        ],
        compiler_params=params(12),
        cost_estimate=pl.CostEstimate(flops=2_000_000_000, bytes_accessed=3_000_000, transcendentals=0),
        name="partial",
    )(live_counts, index_1, coupling, left_basis, tree, direct, hot, *siblings, *joined)
    total, prod = exchange(6, 64, cat(total, prod), total, prod)
    total = apply(6, total)
    total, part_prod, part_sol = lax.optimization_barrier((total, part_prod, part_sol))

    exchange(7, 192, cat(total, prod), total, prod)
    return pl.pallas_call(
        last_kernel,
        out_shape=(shape(nvec, points, F32),) * 2,
        in_specs=[VMEM] * (4 + 2 * (LEVELS - BEFORE)),
        out_specs=(VMEM, VMEM),
        compiler_params=params(8),
        cost_estimate=pl.CostEstimate(flops=30_000_000, bytes_accessed=1_000_000, transcendentals=0),
        name="last",
    )(last_coupling, moved, part_prod, part_sol, *siblings[BEFORE:], *joined[BEFORE:])


def solution(mesh):
    placed = (
        P(None, ("leaf", "sub")),
        P(None, ("leaf", "sub")),
        P(("leaf", "sub"), None),
        P(("leaf", "sub")),
        P(("leaf", "sub"), None),
        P(None, ("leaf", "sub"), None),
        P(None, ("leaf", "sub"), None),
        P(("leaf", "sub"), None, None, None),
    )
    return jax.shard_map(
        per_device,
        mesh=mesh,
        in_specs=placed,
        out_specs=(P(None, ("leaf", "sub")), P(None, ("leaf", "sub"))),
        check_vma=False,
    )
```

time: 189 us -> 81.6 us (0.43)
  starting transfers between devices: 78.9 us -> 37 us
  waiting for transfers between devices: 57.6 us -> 25.5 us
  matrix products: 23.8 us -> 1.12 us
  local copies, waits for them, and re-layouts: 18.1 us -> 0.08 us
  Pallas kernels: 0 us -> 14.8 us
  other arithmetic: 7.39 us -> 1.18 us
    ppermute x44 -> x23, starting transfers between devices: 78.9 us -> 37 us  [swap(): lax.ppermute(block, ('leaf', 'sub'), [(i, i ^ mask) for i in range(count)])]
    ppermute x44 -> x23, waiting for transfers between devices: 57.6 us -> 25.5 us  [swap(): lax.ppermute(block, ('leaf', 'sub'), [(i, i ^ mask) for i in range(count)])]
    dot_general x19 -> x7, matrix products: 23.8 us -> 1.12 us  [dot(): return jnp.dot(a, b, preferred_element_type=F32)]
    pallas_call x0 -> x6, Pallas kernels: none -> 14.8 us  [the longest x1 6.12 us: per_device(): pl.pallas_call(update_kernel, out_shape=tuple((shape(2 * LANE, width * LA...]
    gather x6 -> x0, local copies, waits for them, and re-layouts: 14.7 us -> none  [the longest x1 4.04 us: per_device(): product = jnp.take(total, inverse, axis=1)]
    sort x1 -> x0, other arithmetic: 4.37 us -> none  [per_device(): inverse = jnp.argsort(leaf_order)]
    unnamed x21 -> x14, local copies, waits for them, and re-layouts: 2.94 us -> 0.03 us
  transfers between devices with their start and end apart: 44 -> 23, of which waited for: 30 -> 13; matrix products, arithmetic and copies ran while one was open for 12% -> 2% of each run, Pallas kernels for 0% -> 13%
where the time goes in v2:
time: 81.6 us; the launch traced here: 81.5 us
  starting transfers between devices  37 us (45%)
  waiting for transfers between devices  25.5 us (31%)
  Pallas kernels  14.8 us (18%)
  between operations  1.78 us (2%)
  other arithmetic  1.18 us (1%)
  matrix products  1.12 us (1%)
    ppermute x23, starting transfers between devices, swap(): lax.ppermute(block, ('leaf', 'sub'), [(i, i ^ mask) for i in range(count)])  37 us
    ppermute x23, waiting for transfers between devices, swap(): lax.ppermute(block, ('leaf', 'sub'), [(i, i ^ mask) for i in range(count)])  25.5 us
    pallas_call x1, Pallas kernels, per_device(): pl.pallas_call(update_kernel, out_shape=tuple((shape(2 * LANE, width * LA...  6.12 us
    pallas_call x1, Pallas kernels, per_device(): pl.pallas_call(coefficient_kernel, out_shape=(shape(nvec, 9 * LANE), shap...  3.3 us
    pallas_call x1, Pallas kernels, per_device(): pl.pallas_call(partial_kernel, out_shape=(shape(nvec, points, F32),) * 2...  1.84 us
    pallas_call x1, Pallas kernels, per_device(): pl.pallas_call(direct_kernel, out_shape=(shape(nvec, points, F32), shape(...  1.67 us
  transfers between devices with their start and end apart: 23, of which 13 were waited for; matrix products, arithmetic and copies ran while one was open for 2% of the time, Pallas kernels for 13%

profile of v2, /device:TPU:32, one launch (start us, length us, event | category | flops | bytes accessed | tf_op | source)
XLA Modules:
  0.0 81.5 jit_solution(2346359943335954754)
XLA Ops:
  1.3 3.3 %coefficients.1 = (bf16[32,1152]{1,0:T(8,128)(2,1)}, f32[32,896]{1,0:T(8,128)}, bf16[64,1024]{1,0:T(8,128)(2,1)}) custom-call(s32[1]{0:T(128)S(6)} %copy.14.live, s32[1,1024]{1,0:T(1,128)} %order.3, bf16[32,1024]{1,0:T(8,128)(2,1)} %vec.1, bf16[32,1024]{1,0:T(8,128)(2,1)} %rhs.4, bf16[8,1024,128]{2,1,0:T(8,128)(2,1)} %right.3), custom_call_target="tpu_custom_call" | custom-call | flops 300000000 | bytes 2500000 | tf_op jit(solution)/shard_map/coefficients/pallas_call | solution.py:258
  4.6 1.7 %collective-permute-start = (bf16[32,1152]{1,0:T(8,128)(2,1)}, bf16[32,1152]{1,0:T(8,128)(2,1)S(1)}, u32[]{:S(2)}, u32[]{:S(2)}) collective-permute-start(bf16[32,1152]{1,0:T(8,128)(2,1)} %get-tuple-element.35), channel_id=1, source_target_pairs={{0,1},{1,0},{2,3},{3,2},{4,5},{5,4},{6,7},{7,6},{8,9},{9,8},{10,11... | collective-permute-start | bytes 221192 | tf_op jit(solution)/shard_map/ppermute | solution.py:218
  6.3 6.1 %updates.1 = (bf16[256,896]{1,0:T(8,128)(2,1)S(1)}, bf16[256,768]{1,0:T(8,128)(2,1)S(1)}, bf16[256,640]{1,0:T(8,128)(2,1)S(1)}, bf16[128,1280]{1,0:T(8,128)(2,1)...) custom-call(s32[1]{0:T(128)S(6)} %copy.14.live, s32[1]{0:T(128)} %bitcast.index, ...), custom_call_target="tpu_custom_call" | custom-call | flops 1300000000 | bytes 5000000 | tf_op jit(solution)/shard_map/updates/pallas_call | solution.py:280
  12.6 1.7 %direct.1 = (f32[32,1024]{1,0:T(8,128)S(1)}, bf16[1024,1024]{1,0:T(8,128)(2,1)S(1)}) custom-call(s32[1]{0:T(128)S(6)} %copy.14.live, s32[1,1024]{1,0:T(1,128)S(1)} %copy-done, bf16[64,1024]{1,0:T(8,128)(2,1)S(1)} %copy-done.4, bf16[1024,1024]{1,0:T(8,128)(2,1)S(1)} %copy-done.1), custom_call_target="tpu_custom_call" | custom-call | flops 2000000000 | bytes 2000000 | tf_op jit(solution)/shard_map/direct/pallas_call | solution.py:313
  14.8 3.0 %collective-permute-start.2 = (bf16[32,1408]{1,0:T(8,128)(2,1)S(1)}, bf16[32,1408]{1,0:T(8,128)(2,1)S(1)}, u32[]{:S(2)}, u32[]{:S(2)}) collective-permute-start(bf16[32,1408]{1,0:T(8,128)(2,1)S(1)} %get-tuple-element.125), channel_id=1, source_target_pairs={{0,2},{1,3},{2,0},{3,1},{4,6},{5,7},{6,4},{7,5},{8,10},{9,11},{10,... | collective-permute-start | bytes 270344 | tf_op jit(solution)/shard_map/ppermute | solution.py:218
  18.4 3.0 %collective-permute-done.2 = bf16[32,1408]{1,0:T(8,128)(2,1)S(1)} collective-permute-done((bf16[32,1408]{1,0:T(8,128)(2,1)S(1)}, bf16[32,1408]{1,0:T(8,128)(2,1)S(1)}, u32[]{:S(2)}, u32[]{:S(2)}) %collective-permute-start.2) | collective-permute-done | bytes 90144 | tf_op jit(solution)/shard_map/ppermute | solution.py:218
  21.4 2.3 %collective-permute-done.3 = bf16[32,1408]{1,0:T(8,128)(2,1)S(1)} collective-permute-done((bf16[32,1408]{1,0:T(8,128)(2,1)S(1)}, bf16[32,1408]{1,0:T(8,128)(2,1)S(1)}, u32[]{:S(2)}, u32[]{:S(2)}) %collective-permute-start.3) | collective-permute-done | bytes 90144 | tf_op jit(solution)/shard_map/ppermute | solution.py:218
  23.9 1.1 %collective-permute-start.6 = (bf16[32,128]{1,0:T(8,128)(2,1)S(1)}, bf16[32,128]{1,0:T(8,128)(2,1)S(1)}, u32[]{:S(2)}, u32[]{:S(2)}) collective-permute-start(bf16[32,128]{1,0:T(8,128)(2,1)S(1)} %slice.710), channel_id=1, source_target_pairs={{0,1},{1,0},{2,3},{3,2},{4,5},{5,4},{6,7},{7,6},{8,9},{9,8},{10,11... | collective-permute-start | bytes 24584 | tf_op jit(solution)/shard_map/ppermute | solution.py:218
  25.0 2.2 %collective-permute-start.7 = (bf16[32,128]{1,0:T(8,128)(2,1)S(1)}, bf16[32,128]{1,0:T(8,128)(2,1)S(1)}, u32[]{:S(2)}, u32[]{:S(2)}) collective-permute-start(bf16[32,128]{1,0:T(8,128)(2,1)S(1)} %slice.710), channel_id=1, source_target_pairs={{0,2},{1,3},{2,0},{3,1},{4,6},{5,7},{6,4},{7,5},{8,10},{9,11},{10,... | collective-permute-start | bytes 24584 | tf_op jit(solution)/shard_map/ppermute | solution.py:218
  27.3 1.4 %collective-permute-start.5 = (bf16[32,1024]{1,0:T(8,128)(2,1)S(1)}, bf16[32,1024]{1,0:T(8,128)(2,1)S(1)}, u32[]{:S(2)}, u32[]{:S(2)}) collective-permute-start(bf16[32,1024]{1,0:T(8,128)(2,1)S(1)} %pad_maximum_fusion.9), channel_id=1, source_target_pairs={{0,3},{1,2},{2,1},{3,0},{4,7},{5,6},{6,5},{7,4},{8,11},{9,10},{10,... | collective-permute-start | bytes 196616 | tf_op jit(solution)/shard_map/ppermute | solution.py:218
  28.8 1.6 %collective-permute-start.9 = (bf16[32,1280]{1,0:T(8,128)(2,1)S(1)}, bf16[32,1280]{1,0:T(8,128)(2,1)S(1)}, u32[]{:S(2)}, u32[]{:S(2)}) collective-permute-start(bf16[32,1280]{1,0:T(8,128)(2,1)S(1)} %add_convert_fusion.2), channel_id=1, source_target_pairs={{0,8},{1,9},{2,10},{3,11},{4,12},{5,13},{6,14},{7,15},{8,0},{9,1},... | collective-permute-start | bytes 245768 | tf_op jit(solution)/shard_map/ppermute | solution.py:218
  30.4 2.7 %collective-permute-start.10 = (bf16[32,768]{1,0:T(8,128)(2,1)S(1)}, bf16[32,768]{1,0:T(8,128)(2,1)S(1)}, u32[]{:S(2)}, u32[]{:S(2)}) collective-permute-start(bf16[32,768]{1,0:T(8,128)(2,1)S(1)} %slice.445), channel_id=1, source_target_pairs={{0,16},{1,17},{2,18},{3,19},{4,20},{5,21},{6,22},{7,23},{8,24},{9,... | collective-permute-start | bytes 147464 | tf_op jit(solution)/shard_map/ppermute | solution.py:218
  33.1 2.4 %collective-permute-start.11 = (bf16[32,768]{1,0:T(8,128)(2,1)S(1)}, bf16[32,768]{1,0:T(8,128)(2,1)S(1)}, u32[]{:S(2)}, u32[]{:S(2)}) collective-permute-start(bf16[32,768]{1,0:T(8,128)(2,1)S(1)} %slice.445), channel_id=1, source_target_pairs={{0,24},{1,25},{2,26},{3,27},{4,28},{5,29},{6,30},{7,31},{8,16},{9,... | collective-permute-start | bytes 147464 | tf_op jit(solution)/shard_map/ppermute | solution.py:218
  36.0 2.4 %collective-permute-done.11 = bf16[32,768]{1,0:T(8,128)(2,1)S(1)} collective-permute-done((bf16[32,768]{1,0:T(8,128)(2,1)S(1)}, bf16[32,768]{1,0:T(8,128)(2,1)S(1)}, u32[]{:S(2)}, u32[]{:S(2)}) %collective-permute-start.11) | collective-permute-done | bytes 49184 | tf_op jit(solution)/shard_map/ppermute | solution.py:218
  38.8 3.3 %collective-permute-start.13 = (bf16[32,1920]{1,0:T(8,128)(2,1)S(1)}, bf16[32,1920]{1,0:T(8,128)(2,1)S(1)}, u32[]{:S(2)}, u32[]{:S(2)}) collective-permute-start(bf16[32,1920]{1,0:T(8,128)(2,1)S(1)} %pad_maximum_fusion.6), channel_id=1, source_target_pairs={{0,2},{1,3},{2,0},{3,1},{4,6},{5,7},{6,4},{7,5},{8,10},{9,11},{10,... | collective-permute-start | bytes 368648 | tf_op jit(solution)/shard_map/ppermute | solution.py:218
  42.0 1.4 %collective-permute-start.14 = (bf16[32,1920]{1,0:T(8,128)(2,1)S(1)}, bf16[32,1920]{1,0:T(8,128)(2,1)S(1)}, u32[]{:S(2)}, u32[]{:S(2)}) collective-permute-start(bf16[32,1920]{1,0:T(8,128)(2,1)S(1)} %pad_maximum_fusion.6), channel_id=1, source_target_pairs={{0,3},{1,2},{2,1},{3,0},{4,7},{5,6},{6,5},{7,4},{8,11},{9,10},{10,... | collective-permute-start | bytes 368648 | tf_op jit(solution)/shard_map/ppermute | solution.py:218
  43.5 0.8 %moved.1 = bf16[1024,256]{1,0:T(8,128)(2,1)S(1)} custom-call(s32[1]{0:T(128)S(6)} %copy.14.live, bf16[1024,1024]{1,0:T(8,128)(2,1)S(1)} %get-tuple-element.44.hot, bf16[8,1024,128]{2,1,0:T(8,128)(2,1)S(1)} %copy-done.2), custom_call_target="tpu_custom_call" | custom-call | flops 1500000000 | bytes 2000000 | tf_op jit(solution)/shard_map/moved/pallas_call | solution.py:378
  44.3 2.0 %collective-permute-done.13 = bf16[32,1920]{1,0:T(8,128)(2,1)S(1)} collective-permute-done((bf16[32,1920]{1,0:T(8,128)(2,1)S(1)}, bf16[32,1920]{1,0:T(8,128)(2,1)S(1)}, u32[]{:S(2)}, u32[]{:S(2)}) %collective-permute-start.13) | collective-permute-done | bytes 122912 | tf_op jit(solution)/shard_map/ppermute | solution.py:218
  46.3 1.8 %collective-permute-done.14 = bf16[32,1920]{1,0:T(8,128)(2,1)S(1)} collective-permute-done((bf16[32,1920]{1,0:T(8,128)(2,1)S(1)}, bf16[32,1920]{1,0:T(8,128)(2,1)S(1)}, u32[]{:S(2)}, u32[]{:S(2)}) %collective-permute-start.14) | collective-permute-done | bytes 122912 | tf_op jit(solution)/shard_map/ppermute | solution.py:218
  48.6 1.6 %collective-permute-done.15 = bf16[32,5760]{1,0:T(8,128)(2,1)S(1)} collective-permute-done((bf16[32,5760]{1,0:T(8,128)(2,1)S(1)}, bf16[32,5760]{1,0:T(8,128)(2,1)S(1)}, u32[]{:S(2)}, u32[]{:S(2)}) %collective-permute-start.15) | collective-permute-done | bytes 368672 | tf_op jit(solution)/shard_map/ppermute | solution.py:218
  50.7 4.1 %collective-permute-done.16 = bf16[32,1280]{1,0:T(8,128)(2,1)S(1)} collective-permute-done((bf16[32,1280]{1,0:T(8,128)(2,1)S(1)}, bf16[32,1280]{1,0:T(8,128)(2,1)S(1)}, u32[]{:S(2)}, u32[]{:S(2)}) %collective-permute-start.16) | collective-permute-done | bytes 81952 | tf_op jit(solution)/shard_map/ppermute | solution.py:218
  55.0 2.1 %collective-permute-start.17 = (bf16[32,1024]{1,0:T(8,128)(2,1)S(1)}, bf16[32,1024]{1,0:T(8,128)(2,1)S(1)}, u32[]{:S(2)}, u32[]{:S(2)}) collective-permute-start(bf16[32,1024]{1,0:T(8,128)(2,1)S(1)} %pad_maximum_fusion.10), channel_id=1, source_target_pairs={{0,24},{1,25},{2,26},{3,27},{4,28},{5,29},{6,30},{7,31},{8,16},{9,... | collective-permute-start | bytes 196616 | tf_op jit(solution)/shard_map/ppermute | solution.py:218
  57.1 3.5 %collective-permute-done.17 = bf16[32,1024]{1,0:T(8,128)(2,1)S(1)} collective-permute-done((bf16[32,1024]{1,0:T(8,128)(2,1)S(1)}, bf16[32,1024]{1,0:T(8,128)(2,1)S(1)}, u32[]{:S(2)}, u32[]{:S(2)}) %collective-permute-start.17) | collective-permute-done | bytes 65568 | tf_op jit(solution)/shard_map/ppermute | solution.py:218
  61.1 3.4 %collective-permute-start.20 = (bf16[256,128]{1,0:T(8,128)(2,1)S(1)}, bf16[256,128]{1,0:T(8,128)(2,1)S(1)}, u32[]{:S(2)}, u32[]{:S(2)}) collective-permute-start(bf16[256,128]{1,0:T(8,128)(2,1)S(1)} %slice.483), channel_id=1, source_target_pairs={{0,64},{1,65},{2,66},{3,67},{4,68},{5,69},{6,70},{7,71},{8,72},{9,... | collective-permute-start | bytes 196616 | tf_op jit(solution)/shard_map/ppermute | solution.py:218
  64.4 0.7 collective-permute-done.18
  65.3 1.8 %collective-permute-done.20 = bf16[256,128]{1,0:T(8,128)(2,1)S(1)} collective-permute-done((bf16[256,128]{1,0:T(8,128)(2,1)S(1)}, bf16[256,128]{1,0:T(8,128)(2,1)S(1)}, u32[]{:S(2)}, u32[]{:S(2)}) %collective-permute-start.20) | collective-permute-done | bytes 65568 | tf_op jit(solution)/shard_map/ppermute | solution.py:218
  67.1 2.6 %collective-permute-start.21 = (bf16[32,512]{1,0:T(8,128)(2,1)S(1)}, bf16[32,512]{1,0:T(8,128)(2,1)S(1)}, u32[]{:S(2)}, u32[]{:S(2)}) collective-permute-start(bf16[32,512]{1,0:T(8,128)(2,1)S(1)} %pad_maximum_fusion.13), channel_id=1, source_target_pairs={{0,64},{1,65},{2,66},{3,67},{4,68},{5,69},{6,70},{7,71},{8,72},{9,... | collective-permute-start | bytes 98312 | tf_op jit(solution)/shard_map/ppermute | solution.py:218
  69.7 1.8 %partial.1 = (f32[32,1024]{1,0:T(8,128)S(1)}, f32[32,1024]{1,0:T(8,128)S(1)}, bf16[512,128]{1,0:T(8,128)(2,1)S(1)}) custom-call(s32[1]{0:T(128)S(6)} %copy.14.live, s32[1]{0:T(128)} %bitcast.index, bf16[8,256,128]{2,1,0:T(8,128)(2,1)S(1)} %bitcast.23, bf16[8,1024,128]{2,1,0:T(8,128)(2,1)S(1)} %copy-done.2, bf16[64,1024]{1,0:T(8,128)(2,1)S(1)} %copy-done.4, ...), custom_call_target="tpu_custom_call" | custom-call | flops 2000000000 | bytes 3000000 | tf_op jit(solution)/shard_map/partial/pallas_call | solution.py:408
  71.6 0.5 collective-permute-done.21
  72.2 6.5 %collective-permute-start.22 = (bf16[32,256]{1,0:T(8,128)(2,1)S(1)}, bf16[32,256]{1,0:T(8,128)(2,1)S(1)}, u32[]{:S(2)}, u32[]{:S(2)}) collective-permute-start(bf16[32,256]{1,0:T(8,128)(2,1)S(1)} %pad_maximum_fusion.21), channel_id=1, source_target_pairs={{0,192},{1,193},{2,194},{3,195},{4,196},{5,197},{6,198},{7,199},{8... | collective-permute-start | bytes 49160 | tf_op jit(solution)/shard_map/ppermute | solution.py:218
  78.7 1.7 %collective-permute-done.22 = bf16[32,256]{1,0:T(8,128)(2,1)S(1)} collective-permute-done((bf16[32,256]{1,0:T(8,128)(2,1)S(1)}, bf16[32,256]{1,0:T(8,128)(2,1)S(1)}, u32[]{:S(2)}, u32[]{:S(2)}) %collective-permute-start.22) | collective-permute-done | bytes 16416 | tf_op jit(solution)/shard_map/ppermute | solution.py:218
  80.4 1.0 %last.1 = (f32[32,1024]{1,0:T(8,128)}, f32[32,1024]{1,0:T(8,128)}) custom-call(bf16[512,128]{1,0:T(8,128)(2,1)S(1)} %get-tuple-element.49.coupling, bf16[1024,256]{1,0:T(8,128)(2,1)S(1)} %moved.1, f32[32,1024]{1,0:T(8,128)S(1)} %get-tuple-element.57.prod, f32[32,1024]{1,0:T(8,128)S(1)} %get-tuple-element.58.sol, ...), custom_call_target="tpu_custom_call" | custom-call | flops 30000000 | bytes 1000000 | tf_op jit(solution)/shard_map/last/pallas_call | solution.py:426
  (99 shorter events, 4.2 us)
Async XLA Ops:
  4.6 9.7 %collective-permute-start = (bf16[32,1152]{1,0:T(8,128)(2,1)}, bf16[32,1152]{1,0:T(8,128)(2,1)S(1)}, u32[]{:S(2)}, u32[]{:S(2)}) collective-permute-start(bf16[32,1152]{1,0:T(8,128)(2,1)} %get-tuple-element.35), channel_id=1, source_target_pairs={{0,1},{1,0},{2,3},{3,2},{4,5},{5,4},{6,7},{7,6},{8,9},{9,8},{10,11... | collective-permute-start | bytes 221192 | tf_op jit(solution)/shard_map/ppermute | solution.py:218
  6.2 6.3 %copy-start = (s32[1,1024]{1,0:T(1,128)S(1)}, s32[1,1024]{1,0:T(1,128)}, u32[]{:S(2)}) copy-start(s32[1,1024]{1,0:T(1,128)} %order.3) | copy-start | bytes 12292
  6.2 6.3 %copy-start.1 = (bf16[1024,1024]{1,0:T(8,128)(2,1)S(1)}, bf16[1024,1024]{1,0:T(8,128)(2,1)}, u32[]{:S(2)}) copy-start(bf16[1024,1024]{1,0:T(8,128)(2,1)} %block.1) | copy-start | bytes 6291460
  6.3 6.3 %copy-start.4 = (bf16[64,1024]{1,0:T(8,128)(2,1)S(1)}, bf16[64,1024]{1,0:T(8,128)(2,1)}, u32[]{:S(2)}) copy-start(bf16[64,1024]{1,0:T(8,128)(2,1)} %get-tuple-element.32.tree) | copy-start | bytes 393220
  12.4 2.2 %collective-permute-start.1 = (bf16[128,1280]{1,0:T(8,128)(2,1)S(1)}, bf16[128,1280]{1,0:T(8,128)(2,1)S(1)}, u32[]{:S(2)}, u32[]{:S(2)}) collective-permute-start(bf16[128,1280]{1,0:T(8,128)(2,1)S(1)} %get-tuple-element.38), channel_id=1, source_target_pairs={{0,4},{1,5},{2,6},{3,7},{4,0},{5,1},{6,2},{7,3},{8,12},{9,13},{10,... | collective-permute-start | bytes 983048 | tf_op jit(solution)/shard_map/ppermute | solution.py:218
  12.5 1.8 %copy-start.6 = (bf16[32,1152]{1,0:T(8,128)(2,1)S(1)}, bf16[32,1152]{1,0:T(8,128)(2,1)}, u32[]{:S(2)}) copy-start(bf16[32,1152]{1,0:T(8,128)(2,1)} %get-tuple-element.35) | copy-start | bytes 221188
  12.5 1.8 %copy-start.5 = (f32[32,896]{1,0:T(8,128)S(1)}, f32[32,896]{1,0:T(8,128)}, u32[]{:S(2)}) copy-start(f32[32,896]{1,0:T(8,128)} %get-tuple-element.33) | copy-start | bytes 344068
  14.7 28.7 %copy-start.2 = (bf16[8,1024,128]{2,1,0:T(8,128)(2,1)S(1)}, bf16[8,1024,128]{2,1,0:T(8,128)(2,1)}, u32[]{:S(2)}) copy-start(bf16[8,1024,128]{2,1,0:T(8,128)(2,1)} %left.5) | copy-start | bytes 6291460
  14.8 6.6 %collective-permute-start.2 = (bf16[32,1408]{1,0:T(8,128)(2,1)S(1)}, bf16[32,1408]{1,0:T(8,128)(2,1)S(1)}, u32[]{:S(2)}, u32[]{:S(2)}) collective-permute-start(bf16[32,1408]{1,0:T(8,128)(2,1)S(1)} %get-tuple-element.125), channel_id=1, source_target_pairs={{0,2},{1,3},{2,0},{3,1},{4,6},{5,7},{6,4},{7,5},{8,10},{9,11},{10,... | collective-permute-start | bytes 270344 | tf_op jit(solution)/shard_map/ppermute | solution.py:218
  17.7 5.9 %collective-permute-start.3 = (bf16[32,1408]{1,0:T(8,128)(2,1)S(1)}, bf16[32,1408]{1,0:T(8,128)(2,1)S(1)}, u32[]{:S(2)}, u32[]{:S(2)}) collective-permute-start(bf16[32,1408]{1,0:T(8,128)(2,1)S(1)} %get-tuple-element.126), channel_id=1, source_target_pairs={{0,3},{1,2},{2,1},{3,0},{4,7},{5,6},{6,5},{7,4},{8,11},{9,10},{10,... | collective-permute-start | bytes 270344 | tf_op jit(solution)/shard_map/ppermute | solution.py:218
  18.0 5.7 %collective-permute-start.4 = (bf16[32,1408]{1,0:T(8,128)(2,1)S(1)}, bf16[32,1408]{1,0:T(8,128)(2,1)S(1)}, u32[]{:S(2)}, u32[]{:S(2)}) collective-permute-start(bf16[32,1408]{1,0:T(8,128)(2,1)S(1)} %get-tuple-element.127), channel_id=1, source_target_pairs={{0,1},{1,0},{2,3},{3,2},{4,5},{5,4},{6,7},{7,6},{8,9},{9,8},{10,11... | collective-permute-start | bytes 270344 | tf_op jit(solution)/shard_map/ppermute | solution.py:218
  23.9 11.6 %collective-permute-start.6 = (bf16[32,128]{1,0:T(8,128)(2,1)S(1)}, bf16[32,128]{1,0:T(8,128)(2,1)S(1)}, u32[]{:S(2)}, u32[]{:S(2)}) collective-permute-start(bf16[32,128]{1,0:T(8,128)(2,1)S(1)} %slice.710), channel_id=1, source_target_pairs={{0,1},{1,0},{2,3},{3,2},{4,5},{5,4},{6,7},{7,6},{8,9},{9,8},{10,11... | collective-permute-start | bytes 24584 | tf_op jit(solution)/shard_map/ppermute | solution.py:218
  25.0 10.5 %collective-permute-start.7 = (bf16[32,128]{1,0:T(8,128)(2,1)S(1)}, bf16[32,128]{1,0:T(8,128)(2,1)S(1)}, u32[]{:S(2)}, u32[]{:S(2)}) collective-permute-start(bf16[32,128]{1,0:T(8,128)(2,1)S(1)} %slice.710), channel_id=1, source_target_pairs={{0,2},{1,3},{2,0},{3,1},{4,6},{5,7},{6,4},{7,5},{8,10},{9,11},{10,... | collective-permute-start | bytes 24584 | tf_op jit(solution)/shard_map/ppermute | solution.py:218
  27.3 5.8 %collective-permute-start.5 = (bf16[32,1024]{1,0:T(8,128)(2,1)S(1)}, bf16[32,1024]{1,0:T(8,128)(2,1)S(1)}, u32[]{:S(2)}, u32[]{:S(2)}) collective-permute-start(bf16[32,1024]{1,0:T(8,128)(2,1)S(1)} %pad_maximum_fusion.9), channel_id=1, source_target_pairs={{0,3},{1,2},{2,1},{3,0},{4,7},{5,6},{6,5},{7,4},{8,11},{9,10},{10,... | collective-permute-start | bytes 196616 | tf_op jit(solution)/shard_map/ppermute | solution.py:218
  28.8 7.1 %collective-permute-start.9 = (bf16[32,1280]{1,0:T(8,128)(2,1)S(1)}, bf16[32,1280]{1,0:T(8,128)(2,1)S(1)}, u32[]{:S(2)}, u32[]{:S(2)}) collective-permute-start(bf16[32,1280]{1,0:T(8,128)(2,1)S(1)} %add_convert_fusion.2), channel_id=1, source_target_pairs={{0,8},{1,9},{2,10},{3,11},{4,12},{5,13},{6,14},{7,15},{8,0},{9,1},... | collective-permute-start | bytes 245768 | tf_op jit(solution)/shard_map/ppermute | solution.py:218
  30.4 5.7 %collective-permute-start.10 = (bf16[32,768]{1,0:T(8,128)(2,1)S(1)}, bf16[32,768]{1,0:T(8,128)(2,1)S(1)}, u32[]{:S(2)}, u32[]{:S(2)}) collective-permute-start(bf16[32,768]{1,0:T(8,128)(2,1)S(1)} %slice.445), channel_id=1, source_target_pairs={{0,16},{1,17},{2,18},{3,19},{4,20},{5,21},{6,22},{7,23},{8,24},{9,... | collective-permute-start | bytes 147464 | tf_op jit(solution)/shard_map/ppermute | solution.py:218
  33.1 5.3 %collective-permute-start.11 = (bf16[32,768]{1,0:T(8,128)(2,1)S(1)}, bf16[32,768]{1,0:T(8,128)(2,1)S(1)}, u32[]{:S(2)}, u32[]{:S(2)}) collective-permute-start(bf16[32,768]{1,0:T(8,128)(2,1)S(1)} %slice.445), channel_id=1, source_target_pairs={{0,24},{1,25},{2,26},{3,27},{4,28},{5,29},{6,30},{7,31},{8,16},{9,... | collective-permute-start | bytes 147464 | tf_op jit(solution)/shard_map/ppermute | solution.py:218
  35.6 2.9 %collective-permute-start.8 = (bf16[32,896]{1,0:T(8,128)(2,1)S(1)}, bf16[32,896]{1,0:T(8,128)(2,1)S(1)}, u32[]{:S(2)}, u32[]{:S(2)}) collective-permute-start(bf16[32,896]{1,0:T(8,128)(2,1)S(1)} %pad_maximum_fusion.11), channel_id=1, source_target_pairs={{0,4},{1,5},{2,6},{3,7},{4,0},{5,1},{6,2},{7,3},{8,12},{9,13},{10,... | collective-permute-start | bytes 172040 | tf_op jit(solution)/shard_map/ppermute | solution.py:218
  38.7 5.6 %collective-permute-start.12 = (bf16[32,1920]{1,0:T(8,128)(2,1)S(1)}, bf16[32,1920]{1,0:T(8,128)(2,1)S(1)}, u32[]{:S(2)}, u32[]{:S(2)}) collective-permute-start(bf16[32,1920]{1,0:T(8,128)(2,1)S(1)} %pad_maximum_fusion.6), channel_id=1, source_target_pairs={{0,1},{1,0},{2,3},{3,2},{4,5},{5,4},{6,7},{7,6},{8,9},{9,8},{10,11... | collective-permute-start | bytes 368648 | tf_op jit(solution)/shard_map/ppermute | solution.py:218
  38.8 7.5 %collective-permute-start.13 = (bf16[32,1920]{1,0:T(8,128)(2,1)S(1)}, bf16[32,1920]{1,0:T(8,128)(2,1)S(1)}, u32[]{:S(2)}, u32[]{:S(2)}) collective-permute-start(bf16[32,1920]{1,0:T(8,128)(2,1)S(1)} %pad_maximum_fusion.6), channel_id=1, source_target_pairs={{0,2},{1,3},{2,0},{3,1},{4,6},{5,7},{6,4},{7,5},{8,10},{9,11},{10,... | collective-permute-start | bytes 368648 | tf_op jit(solution)/shard_map/ppermute | solution.py:218
  42.0 6.1 %collective-permute-start.14 = (bf16[32,1920]{1,0:T(8,128)(2,1)S(1)}, bf16[32,1920]{1,0:T(8,128)(2,1)S(1)}, u32[]{:S(2)}, u32[]{:S(2)}) collective-permute-start(bf16[32,1920]{1,0:T(8,128)(2,1)S(1)} %pad_maximum_fusion.6), channel_id=1, source_target_pairs={{0,3},{1,2},{2,1},{3,0},{4,7},{5,6},{6,5},{7,4},{8,11},{9,10},{10,... | collective-permute-start | bytes 368648 | tf_op jit(solution)/shard_map/ppermute | solution.py:218
  48.4 1.8 %collective-permute-start.15 = (bf16[32,5760]{1,0:T(8,128)(2,1)S(1)}, bf16[32,5760]{1,0:T(8,128)(2,1)S(1)}, u32[]{:S(2)}, u32[]{:S(2)}) collective-permute-start(bf16[32,5760]{1,0:T(8,128)(2,1)S(1)} %get-tuple-element.71), channel_id=1, source_target_pairs={{0,4},{1,5},{2,6},{3,7},{4,0},{5,1},{6,2},{7,3},{8,12},{9,13},{10,... | collective-permute-start | bytes 1105928 | tf_op jit(solution)/shard_map/ppermute | solution.py:218
  50.2 4.6 %collective-permute-start.16 = (bf16[32,1280]{1,0:T(8,128)(2,1)S(1)}, bf16[32,1280]{1,0:T(8,128)(2,1)S(1)}, u32[]{:S(2)}, u32[]{:S(2)}) collective-permute-start(bf16[32,1280]{1,0:T(8,128)(2,1)S(1)} %pad_maximum_fusion.8), channel_id=1, source_target_pairs={{0,8},{1,9},{2,10},{3,11},{4,12},{5,13},{6,14},{7,15},{8,0},{9,1},... | collective-permute-start | bytes 245768 | tf_op jit(solution)/shard_map/ppermute | solution.py:218
  50.5 19.2 %copy-start.3 = (bf16[1,8,256,128]{3,2,1,0:T(8,128)(2,1)S(1)}, bf16[1,8,256,128]{3,2,1,0:T(8,128)(2,1)}, u32[]{:S(2)}) copy-start(bf16[1,8,256,128]{3,2,1,0:T(8,128)(2,1)} %param.15) | copy-start | bytes 1572868
  50.5 10.5 %collective-permute-start.19 = (bf16[256,384]{1,0:T(8,128)(2,1)S(1)}, bf16[256,384]{1,0:T(8,128)(2,1)S(1)}, u32[]{:S(2)}, u32[]{:S(2)}) collective-permute-start(bf16[256,384]{1,0:T(8,128)(2,1)S(1)} %pad_maximum_fusion.2), channel_id=1, source_target_pairs={{0,32},{1,33},{2,34},{3,35},{4,36},{5,37},{6,38},{7,39},{8,40},{9,... | collective-permute-start | bytes 589832 | tf_op jit(solution)/shard_map/ppermute | solution.py:218
  55.0 5.6 %collective-permute-start.17 = (bf16[32,1024]{1,0:T(8,128)(2,1)S(1)}, bf16[32,1024]{1,0:T(8,128)(2,1)S(1)}, u32[]{:S(2)}, u32[]{:S(2)}) collective-permute-start(bf16[32,1024]{1,0:T(8,128)(2,1)S(1)} %pad_maximum_fusion.10), channel_id=1, source_target_pairs={{0,24},{1,25},{2,26},{3,27},{4,28},{5,29},{6,30},{7,31},{8,16},{9,... | collective-permute-start | bytes 196616 | tf_op jit(solution)/shard_map/ppermute | solution.py:218
  60.8 4.4 %collective-permute-start.18 = (bf16[32,768]{1,0:T(8,128)(2,1)S(1)}, bf16[32,768]{1,0:T(8,128)(2,1)S(1)}, u32[]{:S(2)}, u32[]{:S(2)}) collective-permute-start(bf16[32,768]{1,0:T(8,128)(2,1)S(1)} %pad_maximum_fusion.12), channel_id=1, source_target_pairs={{0,32},{1,33},{2,34},{3,35},{4,36},{5,37},{6,38},{7,39},{8,40},{9,... | collective-permute-start | bytes 147464 | tf_op jit(solution)/shard_map/ppermute | solution.py:218
  61.1 6.0 %collective-permute-start.20 = (bf16[256,128]{1,0:T(8,128)(2,1)S(1)}, bf16[256,128]{1,0:T(8,128)(2,1)S(1)}, u32[]{:S(2)}, u32[]{:S(2)}) collective-permute-start(bf16[256,128]{1,0:T(8,128)(2,1)S(1)} %slice.483), channel_id=1, source_target_pairs={{0,64},{1,65},{2,66},{3,67},{4,68},{5,69},{6,70},{7,71},{8,72},{9,... | collective-permute-start | bytes 196616 | tf_op jit(solution)/shard_map/ppermute | solution.py:218
  67.1 4.9 %collective-permute-start.21 = (bf16[32,512]{1,0:T(8,128)(2,1)S(1)}, bf16[32,512]{1,0:T(8,128)(2,1)S(1)}, u32[]{:S(2)}, u32[]{:S(2)}) collective-permute-start(bf16[32,512]{1,0:T(8,128)(2,1)S(1)} %pad_maximum_fusion.13), channel_id=1, source_target_pairs={{0,64},{1,65},{2,66},{3,67},{4,68},{5,69},{6,70},{7,71},{8,72},{9,... | collective-permute-start | bytes 98312 | tf_op jit(solution)/shard_map/ppermute | solution.py:218
  72.2 8.2 %collective-permute-start.22 = (bf16[32,256]{1,0:T(8,128)(2,1)S(1)}, bf16[32,256]{1,0:T(8,128)(2,1)S(1)}, u32[]{:S(2)}, u32[]{:S(2)}) collective-permute-start(bf16[32,256]{1,0:T(8,128)(2,1)S(1)} %pad_maximum_fusion.21), channel_id=1, source_target_pairs={{0,192},{1,193},{2,194},{3,195},{4,196},{5,197},{6,198},{7,199},{8... | collective-permute-start | bytes 49160 | tf_op jit(solution)/shard_map/ppermute | solution.py:218

commit v3 on v2

v3 whole, which is shorter than its diff:
```python
import functools

import jax
import jax.numpy as jnp
from jax import lax
from jax.experimental import pallas as pl
from jax.experimental.pallas import tpu as pltpu
from jax.sharding import PartitionSpec as P

BF = jnp.bfloat16
F32 = jnp.float32
LANE = 128
VMEM = pl.BlockSpec(memory_space=pltpu.VMEM)
SMEM = pl.BlockSpec(memory_space=pltpu.SMEM)
HBM = pl.BlockSpec(memory_space=pltpu.HBM)
NT = (((1,), (1,)), ((), ()))
LEVELS = 8
SUMMED = 2
BEFORE = 6


def scale(level):
    return 2.0 ** (-0.5 * level)


def dot(a, b):
    return jnp.dot(a, b, preferred_element_type=F32)


def dot_t(a, b):
    return lax.dot_general(a, b, NT, preferred_element_type=F32)


def one_hot(order, low, width):
    rows = lax.broadcasted_iota(jnp.int32, (order.shape[1], width), 0)
    return jnp.where(rows == order[:, low : low + width], 1.0, 0.0).astype(BF)


def columns(ref, level):
    return ref.at[:, pl.ds(level * LANE, LANE)]


def pair_of(ref, level):
    return jnp.concatenate([ref[level], ref[level + 1]], axis=1)


def update_kernel(live, index, order, vec, rhs, coupling, left, right, *rest):
    outs, scratch = rest[: SUMMED + 5], rest[SUMMED + 5 :]
    home, away, bits, tree, right_in = outs[SUMMED:]
    order_in, fields, held, left_in, turned, sems = scratch
    nvec, points = vec.shape
    small = [
        pltpu.make_async_copy(order, order_in, sems.at[0, LEVELS]),
        pltpu.make_async_copy(vec, fields.at[pl.ds(0, nvec)], sems.at[0, LEVELS + 1]),
        pltpu.make_async_copy(rhs, fields.at[pl.ds(nvec, nvec)], sems.at[0, LEVELS + 2]),
    ]
    rights = [pltpu.make_async_copy(right.at[level], right_in.at[level], sems.at[0, level]) for level in range(LEVELS)]
    lefts = [pltpu.make_async_copy(left.at[level], left_in.at[level], sems.at[1, level]) for level in range(LEVELS - 1)]
    coupling_copy = pltpu.make_async_copy(coupling, held, sems.at[1, LEVELS])
    for copy in small + rights[1:] + [coupling_copy] + lefts + rights[:1]:
        copy.start()
    levels = lax.broadcasted_iota(jnp.int32, bits.shape, 0)
    bits[...] = (lax.shift_right_logical(jnp.full(bits.shape, index[0], jnp.int32), levels) & 1).astype(F32)
    for copy in small:
        copy.wait()
    chunk = 256
    for low in range(0, points, chunk):
        moved = dot(fields[...], one_hot(order_in[...], low, chunk))
        slot = lax.broadcasted_iota(jnp.int32, moved.shape, 1) + low
        tree[:, low : low + chunk] = jnp.where(slot < live[0], moved, 0.0).astype(BF)
    for level in range(1, LEVELS):
        rights[level].wait()
        turned[(level - 1) * LANE : level * LANE, :] = right_in[level].T
    coupling_copy.wait()
    second_core = (lax.shift_right_logical(index[0], 2) & 1) == 1
    for low in range(0, LEVELS - 1, 2):
        levels = [level for level in (low, low + 1) if level < LEVELS - 1]
        for level in levels:
            lefts[level].wait()
        block = pair_of(left_in, low) if len(levels) == 2 else left_in[low]
        gram = dot(turned[low * LANE :, :], masked_rows(block, live))
        for level in levels:
            side = slice((level - low) * LANE, (level - low + 1) * LANE)
            own = jnp.concatenate(
                [
                    (gram[(now - low - 1) * LANE : (now - low) * LANE, side] * scale(now)).astype(BF)
                    for now in range(level + 1, LEVELS)
                ],
                axis=0,
            )
            update = dot_t(canonical(held, index, level), own).astype(BF)
            if level < SUMMED:
                outs[level][...] = update
            else:
                at = sum(LEVELS - 1 - below for below in range(SUMMED, level)) * LANE
                to = slice(at, at + update.shape[1])
                first, second = update[:LANE], update[LANE:]
                home[:, to] = jnp.where(second_core, second, first)
                away[:, to] = jnp.where(second_core, first, second)
    rights[0].wait()


def coefficient_kernel(tree, right, first_out, solve_out):
    nvec = first_out.shape[0]
    for level in range(0, LEVELS, 2):
        pair = dot(tree[...], pair_of(right, level))
        for now in (level, level + 1):
            part = pair[:, (now - level) * LANE : (now - level + 1) * LANE] * scale(now)
            first_out[:, (now + 1) * LANE : (now + 2) * LANE] = part[:nvec].astype(BF)
            if now == 0:
                first_out[:, :LANE] = part[nvec:].astype(BF)
            else:
                solve_out[:, (now - 1) * LANE : now * LANE] = part[nvec:]


def canonical(coupling, index, level):
    held = coupling[level]
    swapped = jnp.concatenate([held[LANE:], held[:LANE]], axis=0)
    second = (lax.shift_right_logical(index[0], level) & 1) == 1
    return jnp.where(second, swapped, held)


def direct_kernel(order, tree, block, lead, prod_out, hot_out):
    points = order.shape[1]
    nvec = prod_out.shape[0]
    chunk = 256
    for low in range(0, points, chunk):
        hot_out[:, low : low + chunk] = one_hot(order[...], low, chunk)
    prod_out[...] = dot_t(tree[:nvec, :], block[...])


def masked_rows(block, live):
    rows = lax.broadcasted_iota(jnp.int32, block.shape, 0)
    return jnp.where(rows < live[0], block.astype(F32), 0.0).astype(BF)


def moved_kernel(live, hot, left, moved_out, left_cat, sems):
    copies = [
        pltpu.make_async_copy(left.at[level], columns(left_cat, level - BEFORE), sems.at[level - BEFORE])
        for level in range(BEFORE, LEVELS)
    ]
    for copy in copies:
        copy.start()
    for copy in copies:
        copy.wait()
    moved_out[...] = dot(hot[...], masked_rows(left_cat[...], live)).astype(BF)


def partial_kernel(live, index, coupling, left, tree, direct, hot, *rest):
    siblings, joined = rest[:BEFORE], rest[BEFORE : 2 * BEFORE]
    prod_out, sol_out, coupling_out, left_cat, sems = rest[2 * BEFORE :]
    copies = [
        pltpu.make_async_copy(left.at[level], columns(left_cat, level), sems.at[level])
        for level in range(BEFORE)
    ]
    for copy in copies:
        copy.start()
    for level in range(BEFORE, LEVELS):
        at = (level - BEFORE) * 2 * LANE
        coupling_out[at : at + 2 * LANE, :] = canonical(coupling, index, level)
    coupled = [dot(joined[level][...], canonical(coupling, index, level)).astype(BF) for level in range(BEFORE)]
    siblings = [block[...] for block in siblings]
    terms = jnp.concatenate([jnp.concatenate(siblings, axis=1), jnp.concatenate(coupled, axis=1)], axis=0)
    for copy in copies:
        copy.wait()
    terms = dot_t(terms, left_cat[...])
    nvec = direct.shape[0]
    total = jnp.concatenate([direct[...] + terms[:nvec], tree[nvec:, :].astype(F32) - terms[nvec:]], axis=0)
    slot = lax.broadcasted_iota(jnp.int32, total.shape, 1)
    total = jnp.where(slot < live[0], total, 0.0)
    high = total.astype(BF)
    low = (total - high.astype(F32)).astype(BF)
    both = dot_t(jnp.concatenate([high, low], axis=0), hot[...])
    prod_out[...] = both[:nvec] + both[2 * nvec : 3 * nvec]
    sol_out[...] = both[nvec : 2 * nvec] + both[3 * nvec :]


def last_kernel(coupling, moved, prod, sol, *rest):
    count = LEVELS - BEFORE
    siblings, joined, (prod_out, sol_out) = rest[:count], rest[count : 2 * count], rest[2 * count :]
    coupled = [
        dot(joined[at][...], coupling[2 * at * LANE : 2 * (at + 1) * LANE, :]).astype(BF) for at in range(count)
    ]
    siblings = [block[...] for block in siblings]
    terms = jnp.concatenate([jnp.concatenate(siblings, axis=1), jnp.concatenate(coupled, axis=1)], axis=0)
    terms = dot_t(terms, moved[...])
    nvec = prod.shape[0]
    prod_out[...] = prod[...] + terms[:nvec]
    sol_out[...] = sol[...] - terms[nvec:]


def params(mib):
    return pltpu.CompilerParams(vmem_limit_bytes=mib << 20)


def shape(rows, lanes, dtype=BF):
    return jax.ShapeDtypeStruct((rows, lanes), dtype)


def swap(block, mask):
    count = lax.axis_size("leaf") * lax.axis_size("sub")
    return lax.ppermute(block, ("leaf", "sub"), [(i, i ^ mask) for i in range(count)])


def cols(block, low, high=None):
    return block[:, low * LANE : None if high is None else high * LANE]


def cat(*blocks):
    return jnp.concatenate([block.astype(BF) for block in blocks], axis=1)


def in_hbm(block):
    return pltpu.with_memory_space_constraint(block, pltpu.HBM)


def behind(block, lead):
    def kernel(block_in, lead_in, block_out):
        block_out[...] = block_in[...]

    return pl.pallas_call(
        kernel,
        out_shape=pltpu.VMEM(block.shape, block.dtype),
        in_specs=[VMEM, pl.BlockSpec(memory_space=pl.ANY)],
        out_specs=VMEM,
        compiler_params=params(4),
        cost_estimate=pl.CostEstimate(flops=1_000_000, bytes_accessed=200_000, transcendentals=0),
        name="behind",
    )(block, lead)


def per_device(vectors, right_side, tree_order, live_counts, leaf_block, left_basis, right_bases, coupling):
    nvec, points = vectors.shape
    index = lax.axis_index("leaf") * lax.axis_size("sub") + lax.axis_index("sub")
    index_1 = index.astype(jnp.int32).reshape(1)
    coupling = coupling[0]

    def pick(level, if_set, if_clear):
        side = jnp.broadcast_to(bits[level : level + 1, : if_set.shape[1]], if_set.shape)
        return jnp.where(side > 0, if_set, if_clear)

    def join(mine, other, level):
        return cat(pick(level, other, mine), pick(level, mine, other))

    def whole_of(mine, theirs):
        width = mine.shape[1] // 4
        mine, theirs = (
            jnp.concatenate([half[:, at : at + width] for at in range(0, 4 * width, width)], axis=0)
            for half in (mine, theirs)
        )
        return jnp.concatenate([pick(2, theirs, mine), pick(2, mine, theirs)], axis=0)

    def by_sub(blocks):
        even = [pick(0, blocks[i ^ 1], blocks[i]) for i in range(4)]
        return [pick(1, even[i ^ 2], even[i]) for i in range(4)]

    widths = [LEVELS - 1 - level for level in range(SUMMED)]
    summed = sum(LEVELS - 1 - level for level in range(SUMMED, LEVELS - 1))
    update_0, update_1, home, away, bits, tree, right_in = pl.pallas_call(
        update_kernel,
        out_shape=tuple(pltpu.VMEM((2 * LANE, width * LANE), BF) for width in widths)
        + (pltpu.VMEM((LANE, summed * LANE), BF),) * 2
        + (pltpu.VMEM((LEVELS, 2 * points), F32), pltpu.VMEM((2 * nvec, points), BF))
        + (pltpu.VMEM(right_bases.shape, BF),),
        in_specs=[SMEM, SMEM] + [HBM] * 6,
        out_specs=(VMEM,) * 7,
        scratch_shapes=[
            pltpu.VMEM((1, points), jnp.int32),
            pltpu.VMEM((2 * nvec, points), BF),
            pltpu.VMEM(coupling.shape, BF),
            pltpu.VMEM((LEVELS - 1, points, LANE), BF),
            pltpu.VMEM((7 * LANE, points), BF),
            pltpu.SemaphoreType.DMA((2, LEVELS + 3)),
        ],
        compiler_params=params(20),
        cost_estimate=pl.CostEstimate(flops=1_500_000_000, bytes_accessed=5_000_000, transcendentals=0),
        name="updates",
    )(
        live_counts,
        index_1,
        *map(in_hbm, (tree_order, vectors, right_side, coupling, left_basis, right_bases)),
    )
    got = swap(away, 4)
    first, coef = pl.pallas_call(
        coefficient_kernel,
        out_shape=(pltpu.VMEM((nvec, 9 * LANE), BF), pltpu.VMEM((nvec, 7 * LANE), F32)),
        in_specs=[VMEM, VMEM],
        out_specs=(VMEM, VMEM),
        compiler_params=params(12),
        cost_estimate=pl.CostEstimate(flops=150_000_000, bytes_accessed=2_500_000, transcendentals=0),
        name="coefficients",
    )(tree, right_in)
    halves = (home.astype(F32) + got.astype(F32)).astype(BF)
    piece = halves.shape[0] // 4
    rows_of = by_sub([halves[i * piece : (i + 1) * piece] for i in range(4)])

    siblings, joined = [], []

    sent = {1: cat(first, rows_of[1]), 2: rows_of[2], 3: rows_of[3]}
    got = {mask: swap(sent[mask], mask) for mask in (1, 2, 3)}
    pieces = sum(
        block.astype(F32) for block in (rows_of[0], cols(got[1], 1 + LEVELS), got[2], got[3])
    ).astype(BF)
    joined.append(join(cols(first, 0, 1), cols(got[1], 0, 1), 0))
    siblings.append(cols(got[1], 1, 2))
    prod = cols(first, 2).astype(F32) + cols(got[1], 2, 1 + LEVELS).astype(F32)
    coef = coef - dot(joined[0], update_0)

    mine = cols(coef, 0, 1).astype(BF)
    got = {1: swap(mine, 1), 2: swap(mine, 2), 3: swap(cat(mine, prod), 3)}
    at = [sum(LEVELS - 1 - below for below in range(SUMMED, level)) for level in range(LEVELS)]
    upper = cols(pieces, at[3])
    pieces = cat(cols(pieces, 0, at[3]), upper.astype(F32) + swap(upper, 8).astype(F32))
    parts = {mask: cols(block, 0, 1).astype(F32) for mask, block in got.items()}
    joined.append(join((mine.astype(F32) + parts[1]).astype(BF), (parts[2] + parts[3]).astype(BF), 1))
    got_prod = cols(got[3], 1)
    siblings.append(cols(got_prod, 0, 1))
    prod = cols(prod, 1) + cols(got_prod, 1).astype(F32)
    coef = cols(coef, 1) - dot(joined[1], update_1)

    sent = cat(coef, pieces)
    direct, hot = pl.pallas_call(
        direct_kernel,
        out_shape=(pltpu.VMEM((nvec, points), F32), pltpu.VMEM((points, points), BF)),
        in_specs=[VMEM, VMEM, VMEM, pl.BlockSpec(memory_space=pl.ANY)],
        out_specs=(VMEM, VMEM),
        compiler_params=params(12),
        cost_estimate=pl.CostEstimate(flops=2_000_000_000, bytes_accessed=2_000_000, transcendentals=0),
        name="direct",
    )(tree_order, tree, leaf_block, sent)
    moved = pl.pallas_call(
        moved_kernel,
        out_shape=pltpu.VMEM((points, (LEVELS - BEFORE) * LANE), BF),
        in_specs=[SMEM, VMEM, HBM],
        out_specs=VMEM,
        scratch_shapes=[
            pltpu.VMEM((points, (LEVELS - BEFORE) * LANE), BF),
            pltpu.SemaphoreType.DMA((LEVELS - BEFORE,)),
        ],
        compiler_params=params(12),
        cost_estimate=pl.CostEstimate(flops=1_500_000_000, bytes_accessed=2_000_000, transcendentals=0),
        name="moved",
    )(live_counts, hot, left_basis)
    got = {mask: swap(sent, mask) for mask in (1, 2, 3)}
    got[0] = sent
    lead = LEVELS - SUMMED
    total = sum(cols(got[mask], 0, lead).astype(F32) for mask in range(4))
    quarters = by_sub([cols(got[mask], lead) for mask in range(4)])
    total, moved, direct = lax.optimization_barrier((total, moved, direct))

    early = [cols(quarter, 0, at[4]) for quarter in quarters]
    sent = cat(total, prod, *early)
    late = cat(*(cols(quarter, at[4]) for quarter in quarters))

    def from_four(block, low, high):
        width = block.shape[1] // (4 * LANE)
        return cat(*(cols(block, i * width + low, i * width + high) for i in range(4)))

    def exchange(level, mask, sent, total, prod):
        left_over = LEVELS - level
        got = swap(sent, mask)
        got_total, got_prod = cols(got, 0, left_over), cols(got, left_over, 2 * left_over)
        joined.append(join(cols(sent, 0, 1), cols(got_total, 0, 1), level))
        siblings.append(cols(got_prod, 0, 1))
        prod = cols(prod, 1) + cols(got_prod, 1).astype(F32)
        return cols(total, 1) + cols(got_total, 1).astype(F32), prod, cols(got, 2 * left_over)

    def apply(level, total):
        return total - dot(joined[level], updates_of[level])

    total, prod, theirs = exchange(2, 4, sent, total, prod)
    whole = whole_of(cat(*early), theirs)
    updates_of = {level: cols(whole, at[level], at[level + 1]) for level in (2, 3)}
    total = apply(2, total)

    sent = cat(total, prod)
    late = behind(late, sent)
    late = (late.astype(F32) + swap(late, 24).astype(F32)).astype(BF)
    total, prod, _ = exchange(3, 8, sent, total, prod)
    total = apply(3, total)

    sent = cat(total, prod)
    late = behind(late, sent)
    own, late = from_four(late, 0, 3), from_four(late, 3, 6)
    updates_of[4] = whole_of(own, swap(own, 4))
    late = (late.astype(F32) + swap(late, 32).astype(F32)).astype(BF)
    total, prod, _ = exchange(4, 24, sent, total, prod)
    total = apply(4, total)

    sent = cat(total, prod)
    late = behind(late, sent)
    whole = whole_of(late, swap(late, 4))
    updates_of[5], update_6 = cols(whole, 0, 2), cols(whole, 2)
    total, prod, _ = exchange(5, 32, sent, total, prod)
    total = apply(5, total)

    part_prod, part_sol, last_coupling = pl.pallas_call(
        partial_kernel,
        out_shape=(pltpu.VMEM((nvec, points), F32),) * 2
        + (pltpu.VMEM(((LEVELS - BEFORE) * 2 * LANE, LANE), BF),),
        in_specs=[SMEM, SMEM, VMEM, HBM] + [VMEM] * (3 + 2 * BEFORE),
        out_specs=(VMEM,) * 3,
        scratch_shapes=[
            pltpu.VMEM((points, BEFORE * LANE), BF),
            pltpu.SemaphoreType.DMA((BEFORE,)),
        ],
        compiler_params=params(12),
        cost_estimate=pl.CostEstimate(flops=2_000_000_000, bytes_accessed=3_000_000, transcendentals=0),
        name="partial",
    )(live_counts, index_1, coupling, left_basis, tree, direct, hot, *siblings, *joined)
    rows = [update_6[low : low + nvec] for low in range(0, 2 * LANE, nvec)]
    total, prod, theirs = exchange(6, 64, cat(total, prod, *rows), total, prod)
    theirs = jnp.concatenate([cols(theirs, low, low + 1) for low in range(len(rows))], axis=0)
    updates_of[6] = (update_6.astype(F32) + theirs.astype(F32)).astype(BF)
    total = apply(6, total)
    total, part_prod, part_sol = lax.optimization_barrier((total, part_prod, part_sol))

    exchange(7, 192, cat(total, prod), total, prod)
    return pl.pallas_call(
        last_kernel,
        out_shape=(shape(nvec, points, F32),) * 2,
        in_specs=[VMEM] * (4 + 2 * (LEVELS - BEFORE)),
        out_specs=(VMEM, VMEM),
        compiler_params=params(8),
        cost_estimate=pl.CostEstimate(flops=30_000_000, bytes_accessed=1_000_000, transcendentals=0),
        name="last",
    )(last_coupling, moved, part_prod, part_sol, *siblings[BEFORE:], *joined[BEFORE:])


def solution(mesh):
    placed = (
        P(None, ("leaf", "sub")),
        P(None, ("leaf", "sub")),
        P(("leaf", "sub"), None),
        P(("leaf", "sub")),
        P(("leaf", "sub"), None),
        P(None, ("leaf", "sub"), None),
        P(None, ("leaf", "sub"), None),
        P(("leaf", "sub"), None, None, None),
    )
    return jax.shard_map(
        per_device,
        mesh=mesh,
        in_specs=placed,
        out_specs=(P(None, ("leaf", "sub")), P(None, ("leaf", "sub"))),
        check_vma=False,
    )
```

time: 81.6 us -> 75.5 us (0.925)
  starting transfers between devices: 37 us -> 32.5 us
  Pallas kernels: 14.8 us -> 12.2 us
    ppermute x23 -> x21, starting transfers between devices: 37 us -> 32.5 us  [swap(): lax.ppermute(block, ('leaf', 'sub'), [(i, i ^ mask) for i in range(count)])]
    pallas_call x5 -> x8, Pallas kernels: 13.8 us -> 11.2 us  [the longest x1 6.29 us: per_device(): pl.pallas_call(update_kernel, out_shape=tuple((pltpu.VMEM((2 * LANE, widt...]
    ppermute x23 -> x21, waiting for transfers between devices: 25.5 us -> 26.2 us  [swap(): lax.ppermute(block, ('leaf', 'sub'), [(i, i ^ mask) for i in range(count)])]
  transfers between devices with their start and end apart: 23 -> 21, of which waited for: 13 -> 16; matrix products, arithmetic and copies ran while one was open for 2% -> 2% of each run, Pallas kernels for 13% -> 6%
where the time goes in v3:
time: 75.5 us; the launch traced here: 75.4 us
  starting transfers between devices  32.5 us (43%)
  waiting for transfers between devices  26.2 us (35%)
  Pallas kernels  12.2 us (16%)
  between operations  1.8 us (2%)
  other arithmetic  1.32 us (2%)
  matrix products  1.15 us (2%)
    ppermute x21, starting transfers between devices, swap(): lax.ppermute(block, ('leaf', 'sub'), [(i, i ^ mask) for i in range(count)])  32.5 us
    ppermute x21, waiting for transfers between devices, swap(): lax.ppermute(block, ('leaf', 'sub'), [(i, i ^ mask) for i in range(count)])  26.2 us
    pallas_call x1, Pallas kernels, per_device(): pl.pallas_call(update_kernel, out_shape=tuple((pltpu.VMEM((2 * LANE, widt...  6.29 us
    pallas_call x1, Pallas kernels, per_device(): pl.pallas_call(partial_kernel, out_shape=(pltpu.VMEM((nvec, points), F32)...  1.84 us
    pallas_call x1, Pallas kernels, per_device(): pl.pallas_call(direct_kernel, out_shape=(pltpu.VMEM((nvec, points), F32),...  1.66 us
  transfers between devices with their start and end apart: 21, of which 16 were waited for; matrix products, arithmetic and copies ran while one was open for 2% of the time, Pallas kernels for 6%

profile of v3, /device:TPU:32, one launch (start us, length us, event | category | flops | bytes accessed | tf_op | source)
XLA Modules:
  0.0 75.4 jit_solution(2291712819803342968)
XLA Ops:
  1.3 6.3 %updates.1 = (bf16[256,896]{1,0:T(8,128)(2,1)S(1)}, bf16[256,768]{1,0:T(8,128)(2,1)S(1)}, bf16[128,1920]{1,0:T(8,128)(2,1)S(1)}, bf16[128,1920]{1,0:T(8,128)(2,1...) custom-call(s32[1]{0:T(128)S(6)} %copy.31.live, s32[1]{0:T(128)} %bitcast.index, ...), custom_call_target="tpu_custom_call" | custom-call | flops 1500000000 | bytes 5000000 | tf_op jit(solution)/shard_map/updates/pallas_call | solution.py:259
  8.3 1.3 %collective-permute-done = bf16[128,1920]{1,0:T(8,128)(2,1)S(1)} collective-permute-done((bf16[128,1920]{1,0:T(8,128)(2,1)S(1)}, bf16[128,1920]{1,0:T(8,128)(2,1)S(1)}, u32[]{:S(2)}, u32[]{:S(2)}) %collective-permute-start) | collective-permute-done | bytes 491552 | tf_op jit(solution)/shard_map/ppermute | solution.py:202
  9.8 1.7 %collective-permute-start.1 = (bf16[32,3072]{1,0:T(8,128)(2,1)S(1)}, bf16[32,3072]{1,0:T(8,128)(2,1)S(1)}, u32[]{:S(2)}, u32[]{:S(2)}) collective-permute-start(bf16[32,3072]{1,0:T(8,128)(2,1)S(1)} %pad_maximum_fusion.4), channel_id=1, source_target_pairs={{0,1},{1,0},{2,3},{3,2},{4,5},{5,4},{6,7},{7,6},{8,9},{9,8},{10,11... | collective-permute-start | bytes 589832 | tf_op jit(solution)/shard_map/ppermute | solution.py:202
  11.5 3.0 %collective-permute-start.5 = (bf16[32,1920]{1,0:T(8,128)(2,1)S(1)}, bf16[32,1920]{1,0:T(8,128)(2,1)S(1)}, u32[]{:S(2)}, u32[]{:S(2)}) collective-permute-start(bf16[32,1920]{1,0:T(8,128)(2,1)S(1)} %get-tuple-element.63), channel_id=1, source_target_pairs={{0,2},{1,3},{2,0},{3,1},{4,6},{5,7},{6,4},{7,5},{8,10},{9,11},{10,... | collective-permute-start | bytes 368648 | tf_op jit(solution)/shard_map/ppermute | solution.py:202
  14.7 2.9 %collective-permute-done.1 = bf16[32,3072]{1,0:T(8,128)(2,1)S(1)} collective-permute-done((bf16[32,3072]{1,0:T(8,128)(2,1)S(1)}, bf16[32,3072]{1,0:T(8,128)(2,1)S(1)}, u32[]{:S(2)}, u32[]{:S(2)}) %collective-permute-start.1) | collective-permute-done | bytes 196640 | tf_op jit(solution)/shard_map/ppermute | solution.py:202
  17.8 3.3 %collective-permute-start.2 = (bf16[32,128]{1,0:T(8,128)(2,1)S(1)}, bf16[32,128]{1,0:T(8,128)(2,1)S(1)}, u32[]{:S(2)}, u32[]{:S(2)}) collective-permute-start(bf16[32,128]{1,0:T(8,128)(2,1)S(1)} %slice.902), channel_id=1, source_target_pairs={{0,2},{1,3},{2,0},{3,1},{4,6},{5,7},{6,4},{7,5},{8,10},{9,11},{10,... | collective-permute-start | bytes 24584 | tf_op jit(solution)/shard_map/ppermute | solution.py:202
  21.1 0.7 collective-permute-start.4
  22.3 1.0 %collective-permute-done.6 = bf16[32,1920]{1,0:T(8,128)(2,1)S(1)} collective-permute-done((bf16[32,1920]{1,0:T(8,128)(2,1)S(1)}, bf16[32,1920]{1,0:T(8,128)(2,1)S(1)}, u32[]{:S(2)}, u32[]{:S(2)}) %collective-permute-start.6) | collective-permute-done | bytes 122912 | tf_op jit(solution)/shard_map/ppermute | solution.py:202
  23.4 1.6 %collective-permute-start.7 = (bf16[32,1280]{1,0:T(8,128)(2,1)S(1)}, bf16[32,1280]{1,0:T(8,128)(2,1)S(1)}, u32[]{:S(2)}, u32[]{:S(2)}) collective-permute-start(bf16[32,1280]{1,0:T(8,128)(2,1)S(1)} %slice.601), channel_id=1, source_target_pairs={{0,8},{1,9},{2,10},{3,11},{4,12},{5,13},{6,14},{7,15},{8,0},{9,1},... | collective-permute-start | bytes 245768 | tf_op jit(solution)/shard_map/ppermute | solution.py:202
  25.0 2.4 %collective-permute-done.3 = bf16[32,1024]{1,0:T(8,128)(2,1)S(1)} collective-permute-done((bf16[32,1024]{1,0:T(8,128)(2,1)S(1)}, bf16[32,1024]{1,0:T(8,128)(2,1)S(1)}, u32[]{:S(2)}, u32[]{:S(2)}) %collective-permute-start.3) | collective-permute-done | bytes 65568 | tf_op jit(solution)/shard_map/ppermute | solution.py:202
  28.0 2.0 %collective-permute-start.10 = (bf16[32,2688]{1,0:T(8,128)(2,1)S(1)}, bf16[32,2688]{1,0:T(8,128)(2,1)S(1)}, u32[]{:S(2)}, u32[]{:S(2)}) collective-permute-start(bf16[32,2688]{1,0:T(8,128)(2,1)S(1)} %pad_maximum_fusion.6.lead), channel_id=1, source_target_pairs={{0,3},{1,2},{2,1},{3,0},{4,7},{5,6},{6,5},{7,4},{8,11},{9,10},{10,... | collective-permute-start | bytes 516104 | tf_op jit(solution)/shard_map/ppermute | solution.py:202
  30.0 0.6 collective-permute-start.9
  30.6 1.6 %collective-permute-start.8 = (bf16[32,2688]{1,0:T(8,128)(2,1)S(1)}, bf16[32,2688]{1,0:T(8,128)(2,1)S(1)}, u32[]{:S(2)}, u32[]{:S(2)}) collective-permute-start(bf16[32,2688]{1,0:T(8,128)(2,1)S(1)} %pad_maximum_fusion.6.lead), channel_id=1, source_target_pairs={{0,1},{1,0},{2,3},{3,2},{4,5},{5,4},{6,7},{7,6},{8,9},{9,8},{10,11... | collective-permute-start | bytes 516104 | tf_op jit(solution)/shard_map/ppermute | solution.py:202
  32.2 1.7 %direct.1 = (f32[32,1024]{1,0:T(8,128)S(1)}, bf16[1024,1024]{1,0:T(8,128)(2,1)S(1)}) custom-call(s32[1,1024]{1,0:T(1,128)S(1)} %copy-done.3, bf16[64,1024]{1,0:T(8,128)(2,1)S(1)} %get-tuple-element.22.tree, bf16[1024,1024]{1,0:T(8,128)(2,1)S(1)} %copy-done, bf16[32,2688]{1,0:T(8,128)(2,1)S(1)} %pad_maximum_fusion.6.lead), custom_call_target="tpu_custom_call" | custom-call | flops 2000000000 | bytes 2000000 | tf_op jit(solution)/shard_map/direct/pallas_call | solution.py:322
  33.9 0.9 %moved.1 = bf16[1024,256]{1,0:T(8,128)(2,1)S(1)} custom-call(s32[1]{0:T(128)S(6)} %copy.31.live, bf16[1024,1024]{1,0:T(8,128)(2,1)S(1)} %get-tuple-element.31.hot, bf16[8,1024,128]{2,1,0:T(8,128)(2,1)S(1)} %copy-done.1), custom_call_target="tpu_custom_call" | custom-call | flops 1500000000 | bytes 2000000 | tf_op jit(solution)/shard_map/moved/pallas_call | solution.py:331
  34.8 2.3 %collective-permute-done.10 = bf16[32,2688]{1,0:T(8,128)(2,1)S(1)} collective-permute-done((bf16[32,2688]{1,0:T(8,128)(2,1)S(1)}, bf16[32,2688]{1,0:T(8,128)(2,1)S(1)}, u32[]{:S(2)}, u32[]{:S(2)}) %collective-permute-start.10) | collective-permute-done | bytes 172064 | tf_op jit(solution)/shard_map/ppermute | solution.py:202
  38.3 1.6 %collective-permute-done.11 = bf16[32,6144]{1,0:T(8,128)(2,1)S(1)} collective-permute-done((bf16[32,6144]{1,0:T(8,128)(2,1)S(1)}, bf16[32,6144]{1,0:T(8,128)(2,1)S(1)}, u32[]{:S(2)}, u32[]{:S(2)}) %collective-permute-start.11) | collective-permute-done | bytes 393248 | tf_op jit(solution)/shard_map/ppermute | solution.py:202
  40.3 1.6 %collective-permute-start.12 = (bf16[32,1280]{1,0:T(8,128)(2,1)S(1)}, bf16[32,1280]{1,0:T(8,128)(2,1)S(1)}, u32[]{:S(2)}, u32[]{:S(2)}) collective-permute-start(bf16[32,1280]{1,0:T(8,128)(2,1)S(1)} %pad_maximum_fusion.14.lead_in), channel_id=1, source_target_pairs={{0,8},{1,9},{2,10},{3,11},{4,12},{5,13},{6,14},{7,15},{8,0},{9,1},... | collective-permute-start | bytes 245768 | tf_op jit(solution)/shard_map/ppermute | solution.py:202
  41.8 2.2 %collective-permute-start.14 = (bf16[32,3072]{1,0:T(8,128)(2,1)S(1)}, bf16[32,3072]{1,0:T(8,128)(2,1)S(1)}, u32[]{:S(2)}, u32[]{:S(2)}) collective-permute-start(bf16[32,3072]{1,0:T(8,128)(2,1)S(1)} %behind.3), channel_id=1, source_target_pairs={{0,24},{1,25},{2,26},{3,27},{4,28},{5,29},{6,30},{7,31},{8,16},{9,... | collective-permute-start | bytes 589832 | tf_op jit(solution)/shard_map/ppermute | solution.py:202
  44.0 0.8 %collective-permute-done.12 = bf16[32,1280]{1,0:T(8,128)(2,1)S(1)} collective-permute-done((bf16[32,1280]{1,0:T(8,128)(2,1)S(1)}, bf16[32,1280]{1,0:T(8,128)(2,1)S(1)}, u32[]{:S(2)}, u32[]{:S(2)}) %collective-permute-start.12) | collective-permute-done | bytes 81952 | tf_op jit(solution)/shard_map/ppermute | solution.py:202
  45.0 2.8 %collective-permute-start.13 = (bf16[32,1024]{1,0:T(8,128)(2,1)S(1)}, bf16[32,1024]{1,0:T(8,128)(2,1)S(1)}, u32[]{:S(2)}, u32[]{:S(2)}) collective-permute-start(bf16[32,1024]{1,0:T(8,128)(2,1)S(1)} %pad_maximum_fusion.18.lead_in), channel_id=1, source_target_pairs={{0,24},{1,25},{2,26},{3,27},{4,28},{5,29},{6,30},{7,31},{8,16},{9,... | collective-permute-start | bytes 196616 | tf_op jit(solution)/shard_map/ppermute | solution.py:202
  47.9 3.3 %collective-permute-done.13 = bf16[32,1024]{1,0:T(8,128)(2,1)S(1)} collective-permute-done((bf16[32,1024]{1,0:T(8,128)(2,1)S(1)}, bf16[32,1024]{1,0:T(8,128)(2,1)S(1)}, u32[]{:S(2)}, u32[]{:S(2)}) %collective-permute-start.13) | collective-permute-done | bytes 65568 | tf_op jit(solution)/shard_map/ppermute | solution.py:202
  51.7 1.1 %collective-permute-done.15 = bf16[32,1536]{1,0:T(8,128)(2,1)S(1)} collective-permute-done((bf16[32,1536]{1,0:T(8,128)(2,1)S(1)}, bf16[32,1536]{1,0:T(8,128)(2,1)S(1)}, u32[]{:S(2)}, u32[]{:S(2)}) %collective-permute-start.15) | collective-permute-done | bytes 98336 | tf_op jit(solution)/shard_map/ppermute | solution.py:202
  53.0 0.9 %collective-permute-start.16 = (bf16[32,768]{1,0:T(8,128)(2,1)S(1)}, bf16[32,768]{1,0:T(8,128)(2,1)S(1)}, u32[]{:S(2)}, u32[]{:S(2)}) collective-permute-start(bf16[32,768]{1,0:T(8,128)(2,1)S(1)} %pad_maximum_fusion.19.lead_in), channel_id=1, source_target_pairs={{0,32},{1,33},{2,34},{3,35},{4,36},{5,37},{6,38},{7,39},{8,40},{9,... | collective-permute-start | bytes 147464 | tf_op jit(solution)/shard_map/ppermute | solution.py:202
  54.0 3.2 %collective-permute-done.17 = bf16[32,1536]{1,0:T(8,128)(2,1)S(1)} collective-permute-done((bf16[32,1536]{1,0:T(8,128)(2,1)S(1)}, bf16[32,1536]{1,0:T(8,128)(2,1)S(1)}, u32[]{:S(2)}, u32[]{:S(2)}) %collective-permute-start.17) | collective-permute-done | bytes 98336 | tf_op jit(solution)/shard_map/ppermute | solution.py:202
  57.9 0.8 %collective-permute-done.18 = bf16[32,1536]{1,0:T(8,128)(2,1)S(1)} collective-permute-done((bf16[32,1536]{1,0:T(8,128)(2,1)S(1)}, bf16[32,1536]{1,0:T(8,128)(2,1)S(1)}, u32[]{:S(2)}, u32[]{:S(2)}) %collective-permute-start.18) | collective-permute-done | bytes 98336 | tf_op jit(solution)/shard_map/ppermute | solution.py:202
  59.0 3.4 %collective-permute-start.19 = (bf16[32,1536]{1,0:T(8,128)(2,1)S(1)}, bf16[32,1536]{1,0:T(8,128)(2,1)S(1)}, u32[]{:S(2)}, u32[]{:S(2)}) collective-permute-start(bf16[32,1536]{1,0:T(8,128)(2,1)S(1)} %constant_dynamic-update-slice_fusion.6), channel_id=1, source_target_pairs={{0,64},{1,65},{2,66},{3,67},{4,68},{5,69},{6,70},{7,71},{8,72},{9,... | collective-permute-start | bytes 294920 | tf_op jit(solution)/shard_map/ppermute | solution.py:202
  62.3 1.8 %partial.1 = (f32[32,1024]{1,0:T(8,128)S(1)}, f32[32,1024]{1,0:T(8,128)S(1)}, bf16[512,128]{1,0:T(8,128)(2,1)S(1)}) custom-call(s32[1]{0:T(128)S(6)} %copy.31.live, s32[1]{0:T(128)} %bitcast.index, bf16[8,256,128]{2,1,0:T(8,128)(2,1)S(1)} %bitcast.21, bf16[8,1024,128]{2,1,0:T(8,128)(2,1)S(1)} %copy-done.1, bf16[64,1024]{1,0:T(8,128)(2,1)S(1)} %get-tuple-element.22.tree, ...), custom_call_target="tpu_custom_call" | custom-call | flops 2000000000 | bytes 3000000 | tf_op jit(solution)/shard_map/partial/pallas_call | solution.py:397
  64.2 2.3 %collective-permute-done.19 = bf16[32,1536]{1,0:T(8,128)(2,1)S(1)} collective-permute-done((bf16[32,1536]{1,0:T(8,128)(2,1)S(1)}, bf16[32,1536]{1,0:T(8,128)(2,1)S(1)}, u32[]{:S(2)}, u32[]{:S(2)}) %collective-permute-start.19) | collective-permute-done | bytes 98336 | tf_op jit(solution)/shard_map/ppermute | solution.py:202
  66.7 6.0 %collective-permute-start.20 = (bf16[32,256]{1,0:T(8,128)(2,1)S(1)}, bf16[32,256]{1,0:T(8,128)(2,1)S(1)}, u32[]{:S(2)}, u32[]{:S(2)}) collective-permute-start(bf16[32,256]{1,0:T(8,128)(2,1)S(1)} %pad_maximum_fusion.27), channel_id=1, source_target_pairs={{0,192},{1,193},{2,194},{3,195},{4,196},{5,197},{6,198},{7,199},{8... | collective-permute-start | bytes 49160 | tf_op jit(solution)/shard_map/ppermute | solution.py:202
  72.7 1.7 %collective-permute-done.20 = bf16[32,256]{1,0:T(8,128)(2,1)S(1)} collective-permute-done((bf16[32,256]{1,0:T(8,128)(2,1)S(1)}, bf16[32,256]{1,0:T(8,128)(2,1)S(1)}, u32[]{:S(2)}, u32[]{:S(2)}) %collective-permute-start.20) | collective-permute-done | bytes 16416 | tf_op jit(solution)/shard_map/ppermute | solution.py:202
  74.4 1.0 %last.1 = (f32[32,1024]{1,0:T(8,128)}, f32[32,1024]{1,0:T(8,128)}) custom-call(bf16[512,128]{1,0:T(8,128)(2,1)S(1)} %get-tuple-element.35.coupling, bf16[1024,256]{1,0:T(8,128)(2,1)S(1)} %moved.1, f32[32,1024]{1,0:T(8,128)S(1)} %get-tuple-element.39.prod, f32[32,1024]{1,0:T(8,128)S(1)} %get-tuple-element.40.sol, ...), custom_call_target="tpu_custom_call" | custom-call | flops 30000000 | bytes 1000000 | tf_op jit(solution)/shard_map/last/pallas_call | solution.py:419
  (115 shorter events, 6.0 us)
Async XLA Ops:
  7.6 2.0 %collective-permute-start = (bf16[128,1920]{1,0:T(8,128)(2,1)S(1)}, bf16[128,1920]{1,0:T(8,128)(2,1)S(1)}, u32[]{:S(2)}, u32[]{:S(2)}) collective-permute-start(bf16[128,1920]{1,0:T(8,128)(2,1)S(1)} %get-tuple-element.28), channel_id=1, source_target_pairs={{0,4},{1,5},{2,6},{3,7},{4,0},{5,1},{6,2},{7,3},{8,12},{9,13},{10,... | collective-permute-start | bytes 1474568 | tf_op jit(solution)/shard_map/ppermute | solution.py:202
  9.7 22.5 %copy-start = (bf16[1024,1024]{1,0:T(8,128)(2,1)S(1)}, bf16[1024,1024]{1,0:T(8,128)(2,1)}, u32[]{:S(2)}) copy-start(bf16[1024,1024]{1,0:T(8,128)(2,1)} %block.1) | copy-start | bytes 6291460
  9.7 22.5 %copy-start.3 = (s32[1,1024]{1,0:T(1,128)S(1)}, s32[1,1024]{1,0:T(1,128)}, u32[]{:S(2)}) copy-start(s32[1,1024]{1,0:T(1,128)} %order.3) | copy-start | bytes 12292
  9.8 7.8 %collective-permute-start.1 = (bf16[32,3072]{1,0:T(8,128)(2,1)S(1)}, bf16[32,3072]{1,0:T(8,128)(2,1)S(1)}, u32[]{:S(2)}, u32[]{:S(2)}) collective-permute-start(bf16[32,3072]{1,0:T(8,128)(2,1)S(1)} %pad_maximum_fusion.4), channel_id=1, source_target_pairs={{0,1},{1,0},{2,3},{3,2},{4,5},{5,4},{6,7},{7,6},{8,9},{9,8},{10,11... | collective-permute-start | bytes 589832 | tf_op jit(solution)/shard_map/ppermute | solution.py:202
  11.5 10.8 %collective-permute-start.5 = (bf16[32,1920]{1,0:T(8,128)(2,1)S(1)}, bf16[32,1920]{1,0:T(8,128)(2,1)S(1)}, u32[]{:S(2)}, u32[]{:S(2)}) collective-permute-start(bf16[32,1920]{1,0:T(8,128)(2,1)S(1)} %get-tuple-element.63), channel_id=1, source_target_pairs={{0,2},{1,3},{2,0},{3,1},{4,6},{5,7},{6,4},{7,5},{8,10},{9,11},{10,... | collective-permute-start | bytes 368648 | tf_op jit(solution)/shard_map/ppermute | solution.py:202
  14.4 8.8 %collective-permute-start.6 = (bf16[32,1920]{1,0:T(8,128)(2,1)S(1)}, bf16[32,1920]{1,0:T(8,128)(2,1)S(1)}, u32[]{:S(2)}, u32[]{:S(2)}) collective-permute-start(bf16[32,1920]{1,0:T(8,128)(2,1)S(1)} %get-tuple-element.64), channel_id=1, source_target_pairs={{0,3},{1,2},{2,1},{3,0},{4,7},{5,6},{6,5},{7,4},{8,11},{9,10},{10,... | collective-permute-start | bytes 368648 | tf_op jit(solution)/shard_map/ppermute | solution.py:202
  17.8 7.2 %collective-permute-start.2 = (bf16[32,128]{1,0:T(8,128)(2,1)S(1)}, bf16[32,128]{1,0:T(8,128)(2,1)S(1)}, u32[]{:S(2)}, u32[]{:S(2)}) collective-permute-start(bf16[32,128]{1,0:T(8,128)(2,1)S(1)} %slice.902), channel_id=1, source_target_pairs={{0,2},{1,3},{2,0},{3,1},{4,6},{5,7},{6,4},{7,5},{8,10},{9,11},{10,... | collective-permute-start | bytes 24584 | tf_op jit(solution)/shard_map/ppermute | solution.py:202
  21.1 3.9 %collective-permute-start.4 = (bf16[32,128]{1,0:T(8,128)(2,1)S(1)}, bf16[32,128]{1,0:T(8,128)(2,1)S(1)}, u32[]{:S(2)}, u32[]{:S(2)}) collective-permute-start(bf16[32,128]{1,0:T(8,128)(2,1)S(1)} %slice.902), channel_id=1, source_target_pairs={{0,1},{1,0},{2,3},{3,2},{4,5},{5,4},{6,7},{7,6},{8,9},{9,8},{10,11... | collective-permute-start | bytes 24584 | tf_op jit(solution)/shard_map/ppermute | solution.py:202
  21.8 5.6 %collective-permute-start.3 = (bf16[32,1024]{1,0:T(8,128)(2,1)S(1)}, bf16[32,1024]{1,0:T(8,128)(2,1)S(1)}, u32[]{:S(2)}, u32[]{:S(2)}) collective-permute-start(bf16[32,1024]{1,0:T(8,128)(2,1)S(1)} %pad_maximum_fusion.17), channel_id=1, source_target_pairs={{0,3},{1,2},{2,1},{3,0},{4,7},{5,6},{6,5},{7,4},{8,11},{9,10},{10,... | collective-permute-start | bytes 196616 | tf_op jit(solution)/shard_map/ppermute | solution.py:202
  23.4 4.5 %collective-permute-start.7 = (bf16[32,1280]{1,0:T(8,128)(2,1)S(1)}, bf16[32,1280]{1,0:T(8,128)(2,1)S(1)}, u32[]{:S(2)}, u32[]{:S(2)}) collective-permute-start(bf16[32,1280]{1,0:T(8,128)(2,1)S(1)} %slice.601), channel_id=1, source_target_pairs={{0,8},{1,9},{2,10},{3,11},{4,12},{5,13},{6,14},{7,15},{8,0},{9,1},... | collective-permute-start | bytes 245768 | tf_op jit(solution)/shard_map/ppermute | solution.py:202
  28.0 5.9 %copy-start.1 = (bf16[8,1024,128]{2,1,0:T(8,128)(2,1)S(1)}, bf16[8,1024,128]{2,1,0:T(8,128)(2,1)}, u32[]{:S(2)}) copy-start(bf16[8,1024,128]{2,1,0:T(8,128)(2,1)} %left.5) | copy-start | bytes 6291460
  28.0 9.1 %collective-permute-start.10 = (bf16[32,2688]{1,0:T(8,128)(2,1)S(1)}, bf16[32,2688]{1,0:T(8,128)(2,1)S(1)}, u32[]{:S(2)}, u32[]{:S(2)}) collective-permute-start(bf16[32,2688]{1,0:T(8,128)(2,1)S(1)} %pad_maximum_fusion.6.lead), channel_id=1, source_target_pairs={{0,3},{1,2},{2,1},{3,0},{4,7},{5,6},{6,5},{7,4},{8,11},{9,10},{10,... | collective-permute-start | bytes 516104 | tf_op jit(solution)/shard_map/ppermute | solution.py:202
  30.0 7.1 %collective-permute-start.9 = (bf16[32,2688]{1,0:T(8,128)(2,1)S(1)}, bf16[32,2688]{1,0:T(8,128)(2,1)S(1)}, u32[]{:S(2)}, u32[]{:S(2)}) collective-permute-start(bf16[32,2688]{1,0:T(8,128)(2,1)S(1)} %pad_maximum_fusion.6.lead), channel_id=1, source_target_pairs={{0,2},{1,3},{2,0},{3,1},{4,6},{5,7},{6,4},{7,5},{8,10},{9,11},{10,... | collective-permute-start | bytes 516104 | tf_op jit(solution)/shard_map/ppermute | solution.py:202
  30.6 7.0 %collective-permute-start.8 = (bf16[32,2688]{1,0:T(8,128)(2,1)S(1)}, bf16[32,2688]{1,0:T(8,128)(2,1)S(1)}, u32[]{:S(2)}, u32[]{:S(2)}) collective-permute-start(bf16[32,2688]{1,0:T(8,128)(2,1)S(1)} %pad_maximum_fusion.6.lead), channel_id=1, source_target_pairs={{0,1},{1,0},{2,3},{3,2},{4,5},{5,4},{6,7},{7,6},{8,9},{9,8},{10,11... | collective-permute-start | bytes 516104 | tf_op jit(solution)/shard_map/ppermute | solution.py:202
  38.1 1.8 %collective-permute-start.11 = (bf16[32,6144]{1,0:T(8,128)(2,1)S(1)}, bf16[32,6144]{1,0:T(8,128)(2,1)S(1)}, u32[]{:S(2)}, u32[]{:S(2)}) collective-permute-start(bf16[32,6144]{1,0:T(8,128)(2,1)S(1)} %get-tuple-element.99), channel_id=1, source_target_pairs={{0,4},{1,5},{2,6},{3,7},{4,0},{5,1},{6,2},{7,3},{8,12},{9,13},{10,... | collective-permute-start | bytes 1179656 | tf_op jit(solution)/shard_map/ppermute | solution.py:202
  40.3 4.6 %collective-permute-start.12 = (bf16[32,1280]{1,0:T(8,128)(2,1)S(1)}, bf16[32,1280]{1,0:T(8,128)(2,1)S(1)}, u32[]{:S(2)}, u32[]{:S(2)}) collective-permute-start(bf16[32,1280]{1,0:T(8,128)(2,1)S(1)} %pad_maximum_fusion.14.lead_in), channel_id=1, source_target_pairs={{0,8},{1,9},{2,10},{3,11},{4,12},{5,13},{6,14},{7,15},{8,0},{9,1},... | collective-permute-start | bytes 245768 | tf_op jit(solution)/shard_map/ppermute | solution.py:202
  41.8 9.4 %collective-permute-start.14 = (bf16[32,3072]{1,0:T(8,128)(2,1)S(1)}, bf16[32,3072]{1,0:T(8,128)(2,1)S(1)}, u32[]{:S(2)}, u32[]{:S(2)}) collective-permute-start(bf16[32,3072]{1,0:T(8,128)(2,1)S(1)} %behind.3), channel_id=1, source_target_pairs={{0,24},{1,25},{2,26},{3,27},{4,28},{5,29},{6,30},{7,31},{8,16},{9,... | collective-permute-start | bytes 589832 | tf_op jit(solution)/shard_map/ppermute | solution.py:202
  45.0 6.2 %collective-permute-start.13 = (bf16[32,1024]{1,0:T(8,128)(2,1)S(1)}, bf16[32,1024]{1,0:T(8,128)(2,1)S(1)}, u32[]{:S(2)}, u32[]{:S(2)}) collective-permute-start(bf16[32,1024]{1,0:T(8,128)(2,1)S(1)} %pad_maximum_fusion.18.lead_in), channel_id=1, source_target_pairs={{0,24},{1,25},{2,26},{3,27},{4,28},{5,29},{6,30},{7,31},{8,16},{9,... | collective-permute-start | bytes 196616 | tf_op jit(solution)/shard_map/ppermute | solution.py:202
  51.3 11.0 %copy-start.2 = (bf16[1,8,256,128]{3,2,1,0:T(8,128)(2,1)S(1)}, bf16[1,8,256,128]{3,2,1,0:T(8,128)(2,1)}, u32[]{:S(2)}) copy-start(bf16[1,8,256,128]{3,2,1,0:T(8,128)(2,1)} %param.15) | copy-start | bytes 1572868
  51.4 1.4 %collective-permute-start.15 = (bf16[32,1536]{1,0:T(8,128)(2,1)S(1)}, bf16[32,1536]{1,0:T(8,128)(2,1)S(1)}, u32[]{:S(2)}, u32[]{:S(2)}) collective-permute-start(bf16[32,1536]{1,0:T(8,128)(2,1)S(1)} %pad_maximum_fusion.8), channel_id=1, source_target_pairs={{0,4},{1,5},{2,6},{3,7},{4,0},{5,1},{6,2},{7,3},{8,12},{9,13},{10,... | collective-permute-start | bytes 294920 | tf_op jit(solution)/shard_map/ppermute | solution.py:202
  51.5 5.7 %collective-permute-start.17 = (bf16[32,1536]{1,0:T(8,128)(2,1)S(1)}, bf16[32,1536]{1,0:T(8,128)(2,1)S(1)}, u32[]{:S(2)}, u32[]{:S(2)}) collective-permute-start(bf16[32,1536]{1,0:T(8,128)(2,1)S(1)} %pad_maximum_fusion.11), channel_id=1, source_target_pairs={{0,32},{1,33},{2,34},{3,35},{4,36},{5,37},{6,38},{7,39},{8,40},{9,... | collective-permute-start | bytes 294920 | tf_op jit(solution)/shard_map/ppermute | solution.py:202
  53.0 4.8 %collective-permute-start.16 = (bf16[32,768]{1,0:T(8,128)(2,1)S(1)}, bf16[32,768]{1,0:T(8,128)(2,1)S(1)}, u32[]{:S(2)}, u32[]{:S(2)}) collective-permute-start(bf16[32,768]{1,0:T(8,128)(2,1)S(1)} %pad_maximum_fusion.19.lead_in), channel_id=1, source_target_pairs={{0,32},{1,33},{2,34},{3,35},{4,36},{5,37},{6,38},{7,39},{8,40},{9,... | collective-permute-start | bytes 147464 | tf_op jit(solution)/shard_map/ppermute | solution.py:202
  57.3 1.4 %collective-permute-start.18 = (bf16[32,1536]{1,0:T(8,128)(2,1)S(1)}, bf16[32,1536]{1,0:T(8,128)(2,1)S(1)}, u32[]{:S(2)}, u32[]{:S(2)}) collective-permute-start(bf16[32,1536]{1,0:T(8,128)(2,1)S(1)} %behind.5), channel_id=1, source_target_pairs={{0,4},{1,5},{2,6},{3,7},{4,0},{5,1},{6,2},{7,3},{8,12},{9,13},{10,... | collective-permute-start | bytes 294920 | tf_op jit(solution)/shard_map/ppermute | solution.py:202
  59.0 7.5 %collective-permute-start.19 = (bf16[32,1536]{1,0:T(8,128)(2,1)S(1)}, bf16[32,1536]{1,0:T(8,128)(2,1)S(1)}, u32[]{:S(2)}, u32[]{:S(2)}) collective-permute-start(bf16[32,1536]{1,0:T(8,128)(2,1)S(1)} %constant_dynamic-update-slice_fusion.6), channel_id=1, source_target_pairs={{0,64},{1,65},{2,66},{3,67},{4,68},{5,69},{6,70},{7,71},{8,72},{9,... | collective-permute-start | bytes 294920 | tf_op jit(solution)/shard_map/ppermute | solution.py:202
  66.7 7.7 %collective-permute-start.20 = (bf16[32,256]{1,0:T(8,128)(2,1)S(1)}, bf16[32,256]{1,0:T(8,128)(2,1)S(1)}, u32[]{:S(2)}, u32[]{:S(2)}) collective-permute-start(bf16[32,256]{1,0:T(8,128)(2,1)S(1)} %pad_maximum_fusion.27), channel_id=1, source_target_pairs={{0,192},{1,193},{2,194},{3,195},{4,196},{5,197},{6,198},{7,199},{8... | collective-permute-start | bytes 49160 | tf_op jit(solution)/shard_map/ppermute | solution.py:202

commit v4 on v3

--- a/solution.py
+++ b/solution.py
@@ -44,10 +44,20 @@
     return jnp.concatenate([ref[level], ref[level + 1]], axis=1)
 
 
-def update_kernel(live, index, order, vec, rhs, coupling, left, right, *rest):
-    outs, scratch = rest[: SUMMED + 5], rest[SUMMED + 5 :]
-    home, away, bits, tree, right_in = outs[SUMMED:]
-    order_in, fields, held, left_in, turned, sems = scratch
+def updates_of_level(gram, low, level, held):
+    side = slice((level - low) * LANE, (level - low + 1) * LANE)
+    own = jnp.concatenate(
+        [
+            (gram[(now - low - 1) * LANE : (now - low) * LANE, side] * scale(now)).astype(BF)
+            for now in range(level + 1, LEVELS)
+        ],
+        axis=0,
+    )
+    return dot_t(held, own).astype(BF)
+
+
+def summed_kernel(live, index, order, vec, rhs, coupling, left, right, *rest):
+    home, away, bits, tree, right_in, turned, order_in, fields, held, left_in, sems = rest
     nvec, points = vec.shape
     small = [
         pltpu.make_async_copy(order, order_in, sems.at[0, LEVELS]),
@@ -55,10 +65,19 @@
         pltpu.make_async_copy(rhs, fields.at[pl.ds(nvec, nvec)], sems.at[0, LEVELS + 2]),
     ]
     rights = [pltpu.make_async_copy(right.at[level], right_in.at[level], sems.at[0, level]) for level in range(LEVELS)]
-    lefts = [pltpu.make_async_copy(left.at[level], left_in.at[level], sems.at[1, level]) for level in range(LEVELS - 1)]
+    lefts = {
+        level: pltpu.make_async_copy(left.at[level], left_in.at[level - SUMMED], sems.at[1, level])
+        for level in range(SUMMED, LEVELS - 1)
+    }
     coupling_copy = pltpu.make_async_copy(coupling, held, sems.at[1, LEVELS])
-    for copy in small + rights[1:] + [coupling_copy] + lefts + rights[:1]:
+    for copy in small + [rights[LEVELS - 1]]:
         copy.start()
+    coupling_copy.start()
+    for level in range(LEVELS - 2, SUMMED - 1, -1):
+        lefts[level].start()
+        rights[level].start()
+    for level in range(SUMMED - 1, -1, -1):
+        rights[level].start()
     levels = lax.broadcasted_iota(jnp.int32, bits.shape, 0)
     bits[...] = (lax.shift_right_logical(jnp.full(bits.shape, index[0], jnp.int32), levels) & 1).astype(F32)
     for copy in small:
@@ -68,36 +87,44 @@
         moved = dot(fields[...], one_hot(order_in[...], low, chunk))
         slot = lax.broadcasted_iota(jnp.int32, moved.shape, 1) + low
         tree[:, low : low + chunk] = jnp.where(slot < live[0], moved, 0.0).astype(BF)
-    for level in range(1, LEVELS):
+
+    def turn(level):
         rights[level].wait()
         turned[(level - 1) * LANE : level * LANE, :] = right_in[level].T
+
+    turn(LEVELS - 1)
     coupling_copy.wait()
     second_core = (lax.shift_right_logical(index[0], 2) & 1) == 1
-    for low in range(0, LEVELS - 1, 2):
+    for low in range(LEVELS - 2, SUMMED - 1, -2):
         levels = [level for level in (low, low + 1) if level < LEVELS - 1]
-        for level in levels:
+        for level in levels[::-1]:
             lefts[level].wait()
-        block = pair_of(left_in, low) if len(levels) == 2 else left_in[low]
+        block = pair_of(left_in, low - SUMMED) if len(levels) == 2 else left_in[low - SUMMED]
         gram = dot(turned[low * LANE :, :], masked_rows(block, live))
         for level in levels:
-            side = slice((level - low) * LANE, (level - low + 1) * LANE)
-            own = jnp.concatenate(
-                [
-                    (gram[(now - low - 1) * LANE : (now - low) * LANE, side] * scale(now)).astype(BF)
-                    for now in range(level + 1, LEVELS)
-                ],
-                axis=0,
-            )
-            update = dot_t(canonical(held, index, level), own).astype(BF)
-            if level < SUMMED:
-                outs[level][...] = update
-            else:
-                at = sum(LEVELS - 1 - below for below in range(SUMMED, level)) * LANE
-                to = slice(at, at + update.shape[1])
-                first, second = update[:LANE], update[LANE:]
-                home[:, to] = jnp.where(second_core, second, first)
-                away[:, to] = jnp.where(second_core, first, second)
+            update = updates_of_level(gram, low, level, canonical(held, index, level))
+            at = sum(LEVELS - 1 - below for below in range(SUMMED, level)) * LANE
+            to = slice(at, at + update.shape[1])
+            first, second = update[:LANE], update[LANE:]
+            home[:, to] = jnp.where(second_core, second, first)
+            away[:, to] = jnp.where(second_core, first, second)
+        for level in (low, low - 1):
+            turn(level)
     rights[0].wait()
+
+
+def own_kernel(live, index, coupling, left, turned, lead, update_0, update_1, held, left_in, sems):
+    copies = [
+        pltpu.make_async_copy(coupling.at[pl.ds(0, SUMMED)], held, sems.at[0]),
+        pltpu.make_async_copy(left.at[pl.ds(0, SUMMED)], left_in, sems.at[1]),
+    ]
+    for copy in copies:
+        copy.start()
+    for copy in copies:
+        copy.wait()
+    gram = dot(turned[...], masked_rows(pair_of(left_in, 0), live))
+    for level, out in ((0, update_0), (1, update_1)):
+        out[...] = updates_of_level(gram, 0, level, canonical(held, index, level))
 
 
 def coefficient_kernel(tree, right, first_out, solve_out):
@@ -214,19 +241,19 @@
     return pltpu.with_memory_space_constraint(block, pltpu.HBM)
 
 
-def behind(block, lead):
-    def kernel(block_in, lead_in, block_out):
-        block_out[...] = block_in[...]
+def behind(lead, *blocks):
+    def kernel(lead_in, *refs):
+        refs[-1][...] = sum(ref[...].astype(F32) for ref in refs[:-1]).astype(BF)
 
     return pl.pallas_call(
         kernel,
-        out_shape=pltpu.VMEM(block.shape, block.dtype),
-        in_specs=[VMEM, pl.BlockSpec(memory_space=pl.ANY)],
+        out_shape=pltpu.VMEM(blocks[0].shape, BF),
+        in_specs=[pl.BlockSpec(memory_space=pl.ANY)] + [VMEM] * len(blocks),
         out_specs=VMEM,
         compiler_params=params(4),
         cost_estimate=pl.CostEstimate(flops=1_000_000, bytes_accessed=200_000, transcendentals=0),
         name="behind",
-    )(block, lead)
+    )(lead, *blocks)
 
 
 def per_device(vectors, right_side, tree_order, live_counts, leaf_block, left_basis, right_bases, coupling):
@@ -242,39 +269,49 @@
     def join(mine, other, level):
         return cat(pick(level, other, mine), pick(level, mine, other))
 
-    def whole_of(mine, theirs):
+    def whole_of(mine, theirs, cost=1):
         width = mine.shape[1] // 4
-        mine, theirs = (
-            jnp.concatenate([half[:, at : at + width] for at in range(0, 4 * width, width)], axis=0)
-            for half in (mine, theirs)
-        )
-        return jnp.concatenate([pick(2, theirs, mine), pick(2, mine, theirs)], axis=0)
+
+        def kernel(index_in, mine_in, theirs_in, out):
+            second = (lax.shift_right_logical(index_in[0], 2) & 1) == 1
+            for at in range(4):
+                side = slice(at * width, (at + 1) * width)
+                own, other = mine_in[:, side], theirs_in[:, side]
+                out[at * nvec : (at + 1) * nvec, :] = jnp.where(second, other, own)
+                out[(at + 4) * nvec : (at + 5) * nvec, :] = jnp.where(second, own, other)
+
+        return pl.pallas_call(
+            kernel,
+            out_shape=pltpu.VMEM((8 * nvec, width), BF),
+            in_specs=[SMEM, VMEM, VMEM],
+            out_specs=VMEM,
+            compiler_params=params(4),
+            cost_estimate=pl.CostEstimate(flops=cost * 1_000_000_000, bytes_accessed=1_000_000, transcendentals=0),
+            name="whole",
+        )(index_1, mine, theirs)
 
     def by_sub(blocks):
         even = [pick(0, blocks[i ^ 1], blocks[i]) for i in range(4)]
         return [pick(1, even[i ^ 2], even[i]) for i in range(4)]
 
-    widths = [LEVELS - 1 - level for level in range(SUMMED)]
     summed = sum(LEVELS - 1 - level for level in range(SUMMED, LEVELS - 1))
-    update_0, update_1, home, away, bits, tree, right_in = pl.pallas_call(
-        update_kernel,
-        out_shape=tuple(pltpu.VMEM((2 * LANE, width * LANE), BF) for width in widths)
-        + (pltpu.VMEM((LANE, summed * LANE), BF),) * 2
+    home, away, bits, tree, right_in, turned = pl.pallas_call(
+        summed_kernel,
+        out_shape=(pltpu.VMEM((LANE, summed * LANE), BF),) * 2
         + (pltpu.VMEM((LEVELS, 2 * points), F32), pltpu.VMEM((2 * nvec, points), BF))
-        + (pltpu.VMEM(right_bases.shape, BF),),
+        + (pltpu.VMEM(right_bases.shape, BF), pltpu.VMEM((7 * LANE, points), BF)),
         in_specs=[SMEM, SMEM] + [HBM] * 6,
-        out_specs=(VMEM,) * 7,
+        out_specs=(VMEM,) * 6,
         scratch_shapes=[
             pltpu.VMEM((1, points), jnp.int32),
             pltpu.VMEM((2 * nvec, points), BF),
             pltpu.VMEM(coupling.shape, BF),
-            pltpu.VMEM((LEVELS - 1, points, LANE), BF),
-            pltpu.VMEM((7 * LANE, points), BF),
+            pltpu.VMEM((LEVELS - 1 - SUMMED, points, LANE), BF),
             pltpu.SemaphoreType.DMA((2, LEVELS + 3)),
         ],
         compiler_params=params(20),
         cost_estimate=pl.CostEstimate(flops=1_500_000_000, bytes_accessed=5_000_000, transcendentals=0),
-        name="updates",
+        name="summed",
     )(
         live_counts,
         index_1,
@@ -297,6 +334,20 @@
     siblings, joined = [], []
 
     sent = {1: cat(first, rows_of[1]), 2: rows_of[2], 3: rows_of[3]}
+    update_0, update_1 = pl.pallas_call(
+        own_kernel,
+        out_shape=(pltpu.VMEM((2 * LANE, 7 * LANE), BF), pltpu.VMEM((2 * LANE, 6 * LANE), BF)),
+        in_specs=[SMEM, SMEM, HBM, HBM, VMEM, pl.BlockSpec(memory_space=pl.ANY)],
+        out_specs=(VMEM, VMEM),
+        scratch_shapes=[
+            pltpu.VMEM((SUMMED, 2 * LANE, LANE), BF),
+            pltpu.VMEM((SUMMED, points, LANE), BF),
+            pltpu.SemaphoreType.DMA((2,)),
+        ],
+        compiler_params=params(16),
+        cost_estimate=pl.CostEstimate(flops=1_500_000_000, bytes_accessed=1_000_000, transcendentals=0),
+        name="own",
+    )(live_counts, index_1, in_hbm(coupling), in_hbm(left_basis), turned, sent[1])
     got = {mask: swap(sent[mask], mask) for mask in (1, 2, 3)}
     pieces = sum(
         block.astype(F32) for block in (rows_of[0], cols(got[1], 1 + LEVELS), got[2], got[3])
@@ -310,7 +361,11 @@
     got = {1: swap(mine, 1), 2: swap(mine, 2), 3: swap(cat(mine, prod), 3)}
     at = [sum(LEVELS - 1 - below for below in range(SUMMED, level)) for level in range(LEVELS)]
     upper = cols(pieces, at[3])
-    pieces = cat(cols(pieces, 0, at[3]), upper.astype(F32) + swap(upper, 8).astype(F32))
+    near = swap(upper, 8)
+    far = behind(upper, cols(pieces, at[4]))
+    far = swap(far, 16).astype(F32) + swap(far, 24).astype(F32)
+    upper = upper.astype(F32) + near.astype(F32)
+    pieces = cat(cols(pieces, 0, at[3]), cols(upper, 0, at[4] - at[3]), cols(upper, at[4] - at[3]) + far)
     parts = {mask: cols(block, 0, 1).astype(F32) for mask, block in got.items()}
     joined.append(join((mine.astype(F32) + parts[1]).astype(BF), (parts[2] + parts[3]).astype(BF), 1))
     got_prod = cols(got[3], 1)
@@ -348,9 +403,9 @@
     quarters = by_sub([cols(got[mask], lead) for mask in range(4)])
     total, moved, direct = lax.optimization_barrier((total, moved, direct))
 
-    early = [cols(quarter, 0, at[4]) for quarter in quarters]
+    early = [cols(quarter, 0, at[5]) for quarter in quarters]
     sent = cat(total, prod, *early)
-    late = cat(*(cols(quarter, at[4]) for quarter in quarters))
+    late = cat(*(cols(quarter, at[5]) for quarter in quarters))
 
     def from_four(block, low, high):
         width = block.shape[1] // (4 * LANE)
@@ -370,27 +425,26 @@
 
     total, prod, theirs = exchange(2, 4, sent, total, prod)
     whole = whole_of(cat(*early), theirs)
-    updates_of = {level: cols(whole, at[level], at[level + 1]) for level in (2, 3)}
+    updates_of = {level: cols(whole, at[level], at[level + 1]) for level in (2, 3, 4)}
     total = apply(2, total)
 
     sent = cat(total, prod)
-    late = behind(late, sent)
-    late = (late.astype(F32) + swap(late, 24).astype(F32)).astype(BF)
+    late = behind(sent, late)
+    got_late = swap(late, 32)
     total, prod, _ = exchange(3, 8, sent, total, prod)
     total = apply(3, total)
 
     sent = cat(total, prod)
-    late = behind(late, sent)
-    own, late = from_four(late, 0, 3), from_four(late, 3, 6)
-    updates_of[4] = whole_of(own, swap(own, 4))
-    late = (late.astype(F32) + swap(late, 32).astype(F32)).astype(BF)
+    late = behind(sent, late, got_late)
+    own, late = from_four(late, 0, 2), from_four(late, 2, 3)
+    updates_of[5] = whole_of(own, swap(own, 4))
+    got_late = swap(late, 64)
     total, prod, _ = exchange(4, 24, sent, total, prod)
     total = apply(4, total)
 
     sent = cat(total, prod)
-    late = behind(late, sent)
-    whole = whole_of(late, swap(late, 4))
-    updates_of[5], update_6 = cols(whole, 0, 2), cols(whole, 2)
+    late = behind(sent, late, got_late)
+    updates_of[6] = whole_of(late, swap(late, 4))
     total, prod, _ = exchange(5, 32, sent, total, prod)
     total = apply(5, total)
 
@@ -408,10 +462,7 @@
         cost_estimate=pl.CostEstimate(flops=2_000_000_000, bytes_accessed=3_000_000, transcendentals=0),
         name="partial",
     )(live_counts, index_1, coupling, left_basis, tree, direct, hot, *siblings, *joined)
-    rows = [update_6[low : low + nvec] for low in range(0, 2 * LANE, nvec)]
-    total, prod, theirs = exchange(6, 64, cat(total, prod, *rows), total, prod)
-    theirs = jnp.concatenate([cols(theirs, low, low + 1) for low in range(len(rows))], axis=0)
-    updates_of[6] = (update_6.astype(F32) + theirs.astype(F32)).astype(BF)
+    total, prod, _ = exchange(6, 64, cat(total, prod), total, prod)
     total = apply(6, total)
     total, part_prod, part_sol = lax.optimization_barrier((total, part_prod, part_sol))
 

time: 75.5 us -> 70.8 us (0.938)
  waiting for transfers between devices: 26.2 us -> 20.5 us
  Pallas kernels: 12.2 us -> 13.1 us
    ppermute x21 -> x23, waiting for transfers between devices: 26.2 us -> 20.5 us  [swap(): lax.ppermute(block, ('leaf', 'sub'), [(i, i ^ mask) for i in range(count)])]
    pallas_call x4 -> x9, Pallas kernels: 6.33 us -> 7.28 us  [the longest x1 4.71 us: per_device(): pl.pallas_call(summed_kernel, out_shape=(pltpu.VMEM((LANE, summed * LANE)...]
    ppermute x21 -> x23, starting transfers between devices: 32.5 us -> 33 us  [swap(): lax.ppermute(block, ('leaf', 'sub'), [(i, i ^ mask) for i in range(count)])]
  transfers between devices with their start and end apart: 21 -> 23, of which waited for: 16 -> 15; matrix products, arithmetic and copies ran while one was open for 2% -> 2% of each run, Pallas kernels for 6% -> 10%
where the time goes in v4:
time: 70.8 us; the launch traced here: 70.7 us
  starting transfers between devices  33 us (47%)
  waiting for transfers between devices  20.5 us (29%)
  Pallas kernels  13.1 us (19%)
  between operations  1.77 us (2%)
  matrix products  1.13 us (2%)
  other arithmetic  1.03 us (1%)
    ppermute x23, starting transfers between devices, swap(): lax.ppermute(block, ('leaf', 'sub'), [(i, i ^ mask) for i in range(count)])  33 us
    ppermute x23, waiting for transfers between devices, swap(): lax.ppermute(block, ('leaf', 'sub'), [(i, i ^ mask) for i in range(count)])  20.5 us
    pallas_call x1, Pallas kernels, per_device(): pl.pallas_call(summed_kernel, out_shape=(pltpu.VMEM((LANE, summed * LANE)...  4.71 us
    pallas_call x1, Pallas kernels, per_device(): pl.pallas_call(own_kernel, out_shape=(pltpu.VMEM((2 * LANE, 7 * LANE), BF...  2.4 us
    pallas_call x1, Pallas kernels, per_device(): pl.pallas_call(partial_kernel, out_shape=(pltpu.VMEM((nvec, points), F32)...  1.83 us
    pallas_call x1, Pallas kernels, per_device(): pl.pallas_call(direct_kernel, out_shape=(pltpu.VMEM((nvec, points), F32),...  1.66 us
  transfers between devices with their start and end apart: 23, of which 15 were waited for; matrix products, arithmetic and copies ran while one was open for 2% of the time, Pallas kernels for 10%

profile of v4, /device:TPU:32, one launch (start us, length us, event | category | flops | bytes accessed | tf_op | source)
XLA Modules:
  0.0 70.7 jit_solution(17356253005987384440)
XLA Ops:
  1.3 4.7 %summed.1 = (bf16[128,1920]{1,0:T(8,128)(2,1)S(1)}, bf16[128,1920]{1,0:T(8,128)(2,1)S(1)}, f32[8,2048]{1,0:T(8,128)S(1)}, bf16[64,1024]{1,0:T(8,128)(2,1)S(1)}, ...) custom-call(s32[1]{0:T(128)S(6)} %copy.15.live, s32[1]{0:T(128)} %bitcast.index.index_in, ...), custom_call_target="tpu_custom_call" | custom-call | flops 1500000000 | bytes 5000000 | tf_op jit(solution)/shard_map/summed/pallas_call | solution.py:298
  6.6 1.3 %collective-permute-done = bf16[128,1920]{1,0:T(8,128)(2,1)S(1)} collective-permute-done((bf16[128,1920]{1,0:T(8,128)(2,1)S(1)}, bf16[128,1920]{1,0:T(8,128)(2,1)S(1)}, u32[]{:S(2)}, u32[]{:S(2)}) %collective-permute-start) | collective-permute-done | bytes 491552 | tf_op jit(solution)/shard_map/ppermute | solution.py:229
  8.2 1.7 %collective-permute-start.1 = (bf16[32,3072]{1,0:T(8,128)(2,1)S(1)}, bf16[32,3072]{1,0:T(8,128)(2,1)S(1)}, u32[]{:S(2)}, u32[]{:S(2)}) collective-permute-start(bf16[32,3072]{1,0:T(8,128)(2,1)S(1)} %pad_maximum_fusion.1.lead), channel_id=1, source_target_pairs={{0,1},{1,0},{2,3},{3,2},{4,5},{5,4},{6,7},{7,6},{8,9},{9,8},{10,11... | collective-permute-start | bytes 589832 | tf_op jit(solution)/shard_map/ppermute | solution.py:229
  9.9 3.0 %collective-permute-start.5 = (bf16[32,1920]{1,0:T(8,128)(2,1)S(1)}, bf16[32,1920]{1,0:T(8,128)(2,1)S(1)}, u32[]{:S(2)}, u32[]{:S(2)}) collective-permute-start(bf16[32,1920]{1,0:T(8,128)(2,1)S(1)} %get-tuple-element.64), channel_id=1, source_target_pairs={{0,2},{1,3},{2,0},{3,1},{4,6},{5,7},{6,4},{7,5},{8,10},{9,11},{10,... | collective-permute-start | bytes 368648 | tf_op jit(solution)/shard_map/ppermute | solution.py:229
  13.1 2.4 %own.1 = (bf16[256,896]{1,0:T(8,128)(2,1)S(1)}, bf16[256,768]{1,0:T(8,128)(2,1)S(1)}) custom-call(s32[1]{0:T(128)S(6)} %copy.15.live, s32[1]{0:T(128)} %bitcast.index.index_in, bf16[8,256,128]{2,1,0:T(8,128)(2,1)} %bitcast.23, bf16[8,1024,128]{2,1,0:T(8,128)(2,1)} %left.7, bf16[896,1024]{1,0:T(8,128)(2,1)S(1)} %get-tuple-element.30.turned, ...), custom_call_target="tpu_custom_call" | custom-call | flops 1500000000 | bytes 1000000 | tf_op jit(solution)/shard_map/own/pallas_call | solution.py:337
  15.5 0.5 collective-permute-done.1
  16.2 3.3 %collective-permute-start.2 = (bf16[32,128]{1,0:T(8,128)(2,1)S(1)}, bf16[32,128]{1,0:T(8,128)(2,1)S(1)}, u32[]{:S(2)}, u32[]{:S(2)}) collective-permute-start(bf16[32,128]{1,0:T(8,128)(2,1)S(1)} %slice.691), channel_id=1, source_target_pairs={{0,2},{1,3},{2,0},{3,1},{4,6},{5,7},{6,4},{7,5},{8,10},{9,11},{10,... | collective-permute-start | bytes 24584 | tf_op jit(solution)/shard_map/ppermute | solution.py:229
  19.5 0.7 collective-permute-start.4
  20.7 1.0 %collective-permute-done.6 = bf16[32,1920]{1,0:T(8,128)(2,1)S(1)} collective-permute-done((bf16[32,1920]{1,0:T(8,128)(2,1)S(1)}, bf16[32,1920]{1,0:T(8,128)(2,1)S(1)}, u32[]{:S(2)}, u32[]{:S(2)}) %collective-permute-start.6) | collective-permute-done | bytes 122912 | tf_op jit(solution)/shard_map/ppermute | solution.py:229
  21.9 2.8 %collective-permute-start.9 = (bf16[32,768]{1,0:T(8,128)(2,1)S(1)}, bf16[32,768]{1,0:T(8,128)(2,1)S(1)}, u32[]{:S(2)}, u32[]{:S(2)}) collective-permute-start(bf16[32,768]{1,0:T(8,128)(2,1)S(1)} %behind.4), channel_id=1, source_target_pairs={{0,24},{1,25},{2,26},{3,27},{4,28},{5,29},{6,30},{7,31},{8,16},{9,... | collective-permute-start | bytes 147464 | tf_op jit(solution)/shard_map/ppermute | solution.py:229
  24.7 0.8 %collective-permute-start.8 = (bf16[32,768]{1,0:T(8,128)(2,1)S(1)}, bf16[32,768]{1,0:T(8,128)(2,1)S(1)}, u32[]{:S(2)}, u32[]{:S(2)}) collective-permute-start(bf16[32,768]{1,0:T(8,128)(2,1)S(1)} %behind.4), channel_id=1, source_target_pairs={{0,16},{1,17},{2,18},{3,19},{4,20},{5,21},{6,22},{7,23},{8,24},{9,... | collective-permute-start | bytes 147464 | tf_op jit(solution)/shard_map/ppermute | solution.py:229
  26.3 3.7 %collective-permute-done.7 = bf16[32,1280]{1,0:T(8,128)(2,1)S(1)} collective-permute-done((bf16[32,1280]{1,0:T(8,128)(2,1)S(1)}, bf16[32,1280]{1,0:T(8,128)(2,1)S(1)}, u32[]{:S(2)}, u32[]{:S(2)}) %collective-permute-start.7) | collective-permute-done | bytes 81952 | tf_op jit(solution)/shard_map/ppermute | solution.py:229
  30.4 2.0 %collective-permute-start.12 = (bf16[32,2688]{1,0:T(8,128)(2,1)S(1)}, bf16[32,2688]{1,0:T(8,128)(2,1)S(1)}, u32[]{:S(2)}, u32[]{:S(2)}) collective-permute-start(bf16[32,2688]{1,0:T(8,128)(2,1)S(1)} %pad_maximum_fusion.2.lead), channel_id=1, source_target_pairs={{0,3},{1,2},{2,1},{3,0},{4,7},{5,6},{6,5},{7,4},{8,11},{9,10},{10,... | collective-permute-start | bytes 516104 | tf_op jit(solution)/shard_map/ppermute | solution.py:229
  32.4 0.6 collective-permute-start.11
  33.0 1.6 %collective-permute-start.10 = (bf16[32,2688]{1,0:T(8,128)(2,1)S(1)}, bf16[32,2688]{1,0:T(8,128)(2,1)S(1)}, u32[]{:S(2)}, u32[]{:S(2)}) collective-permute-start(bf16[32,2688]{1,0:T(8,128)(2,1)S(1)} %pad_maximum_fusion.2.lead), channel_id=1, source_target_pairs={{0,1},{1,0},{2,3},{3,2},{4,5},{5,4},{6,7},{7,6},{8,9},{9,8},{10,11... | collective-permute-start | bytes 516104 | tf_op jit(solution)/shard_map/ppermute | solution.py:229
  34.6 1.7 %direct.1 = (f32[32,1024]{1,0:T(8,128)S(1)}, bf16[1024,1024]{1,0:T(8,128)(2,1)S(1)}) custom-call(s32[1,1024]{1,0:T(1,128)S(1)} %copy-done.3, bf16[64,1024]{1,0:T(8,128)(2,1)S(1)} %get-tuple-element.23.tree, bf16[1024,1024]{1,0:T(8,128)(2,1)S(1)} %copy-done, bf16[32,2688]{1,0:T(8,128)(2,1)S(1)} %pad_maximum_fusion.2.lead), custom_call_target="tpu_custom_call" | custom-call | flops 2000000000 | bytes 2000000 | tf_op jit(solution)/shard_map/direct/pallas_call | solution.py:377
  36.2 0.9 %moved.1 = bf16[1024,256]{1,0:T(8,128)(2,1)S(1)} custom-call(s32[1]{0:T(128)S(6)} %copy.15.live, bf16[1024,1024]{1,0:T(8,128)(2,1)S(1)} %get-tuple-element.33.hot, bf16[8,1024,128]{2,1,0:T(8,128)(2,1)S(1)} %copy-done.1), custom_call_target="tpu_custom_call" | custom-call | flops 1500000000 | bytes 2000000 | tf_op jit(solution)/shard_map/moved/pallas_call | solution.py:386
  37.3 2.0 %collective-permute-done.11 = bf16[32,2688]{1,0:T(8,128)(2,1)S(1)} collective-permute-done((bf16[32,2688]{1,0:T(8,128)(2,1)S(1)}, bf16[32,2688]{1,0:T(8,128)(2,1)S(1)}, u32[]{:S(2)}, u32[]{:S(2)}) %collective-permute-start.11) | collective-permute-done | bytes 172064 | tf_op jit(solution)/shard_map/ppermute | solution.py:229
  39.3 0.5 collective-permute-done.10
  40.4 1.8 %collective-permute-done.13 = bf16[32,7680]{1,0:T(8,128)(2,1)S(1)} collective-permute-done((bf16[32,7680]{1,0:T(8,128)(2,1)S(1)}, bf16[32,7680]{1,0:T(8,128)(2,1)S(1)}, u32[]{:S(2)}, u32[]{:S(2)}) %collective-permute-start.13) | collective-permute-done | bytes 491552 | tf_op jit(solution)/shard_map/ppermute | solution.py:229
  42.9 0.8 %collective-permute-start.17 = (bf16[32,1536]{1,0:T(8,128)(2,1)S(1)}, bf16[32,1536]{1,0:T(8,128)(2,1)S(1)}, u32[]{:S(2)}, u32[]{:S(2)}) collective-permute-start(bf16[32,1536]{1,0:T(8,128)(2,1)S(1)} %behind.5.refs_0_), channel_id=1, source_target_pairs={{0,32},{1,33},{2,34},{3,35},{4,36},{5,37},{6,38},{7,39},{8,40},{9,... | collective-permute-start | bytes 294920 | tf_op jit(solution)/shard_map/ppermute | solution.py:229
  43.7 3.4 %collective-permute-done.14 = bf16[32,1280]{1,0:T(8,128)(2,1)S(1)} collective-permute-done((bf16[32,1280]{1,0:T(8,128)(2,1)S(1)}, bf16[32,1280]{1,0:T(8,128)(2,1)S(1)}, u32[]{:S(2)}, u32[]{:S(2)}) %collective-permute-start.14) | collective-permute-done | bytes 81952 | tf_op jit(solution)/shard_map/ppermute | solution.py:229
  47.3 1.9 %collective-permute-start.15 = (bf16[32,1024]{1,0:T(8,128)(2,1)S(1)}, bf16[32,1024]{1,0:T(8,128)(2,1)S(1)}, u32[]{:S(2)}, u32[]{:S(2)}) collective-permute-start(bf16[32,1024]{1,0:T(8,128)(2,1)S(1)} %pad_maximum_fusion.7.lead_in), channel_id=1, source_target_pairs={{0,24},{1,25},{2,26},{3,27},{4,28},{5,29},{6,30},{7,31},{8,16},{9,... | collective-permute-start | bytes 196616 | tf_op jit(solution)/shard_map/ppermute | solution.py:229
  49.3 3.3 %collective-permute-start.20 = (bf16[32,512]{1,0:T(8,128)(2,1)S(1)}, bf16[32,512]{1,0:T(8,128)(2,1)S(1)}, u32[]{:S(2)}, u32[]{:S(2)}) collective-permute-start(bf16[32,512]{1,0:T(8,128)(2,1)S(1)} %pad_maximum_fusion.11.refs_0_), channel_id=1, source_target_pairs={{0,64},{1,65},{2,66},{3,67},{4,68},{5,69},{6,70},{7,71},{8,72},{9,... | collective-permute-start | bytes 98312 | tf_op jit(solution)/shard_map/ppermute | solution.py:229
  53.4 1.2 %collective-permute-done.20.refs_1_ = bf16[32,512]{1,0:T(8,128)(2,1)S(1)} collective-permute-done((bf16[32,512]{1,0:T(8,128)(2,1)S(1)}, bf16[32,512]{1,0:T(8,128)(2,1)S(1)}, u32[]{:S(2)}, u32[]{:S(2)}) %collective-permute-start.20) | collective-permute-done | bytes 32800 | tf_op jit(solution)/shard_map/ppermute | solution.py:229
  54.7 1.1 %collective-permute-done.21.theirs_in = bf16[32,512]{1,0:T(8,128)(2,1)S(1)} collective-permute-done((bf16[32,512]{1,0:T(8,128)(2,1)S(1)}, bf16[32,512]{1,0:T(8,128)(2,1)S(1)}, u32[]{:S(2)}, u32[]{:S(2)}) %collective-permute-start.21) | collective-permute-done | bytes 32800 | tf_op jit(solution)/shard_map/ppermute | solution.py:229
  55.9 1.4 %collective-permute-done.16 = bf16[32,768]{1,0:T(8,128)(2,1)S(1)} collective-permute-done((bf16[32,768]{1,0:T(8,128)(2,1)S(1)}, bf16[32,768]{1,0:T(8,128)(2,1)S(1)}, u32[]{:S(2)}, u32[]{:S(2)}) %collective-permute-start.16) | collective-permute-done | bytes 49184 | tf_op jit(solution)/shard_map/ppermute | solution.py:229
  57.5 3.3 %collective-permute-start.19 = (bf16[32,512]{1,0:T(8,128)(2,1)S(1)}, bf16[32,512]{1,0:T(8,128)(2,1)S(1)}, u32[]{:S(2)}, u32[]{:S(2)}) collective-permute-start(bf16[32,512]{1,0:T(8,128)(2,1)S(1)} %pad_maximum_fusion.10), channel_id=1, source_target_pairs={{0,64},{1,65},{2,66},{3,67},{4,68},{5,69},{6,70},{7,71},{8,72},{9,... | collective-permute-start | bytes 98312 | tf_op jit(solution)/shard_map/ppermute | solution.py:229
  60.8 1.8 %partial.1 = (f32[32,1024]{1,0:T(8,128)S(1)}, f32[32,1024]{1,0:T(8,128)S(1)}, bf16[512,128]{1,0:T(8,128)(2,1)S(1)}) custom-call(s32[1]{0:T(128)S(6)} %copy.15.live, s32[1]{0:T(128)} %bitcast.index.index_in, bf16[8,256,128]{2,1,0:T(8,128)(2,1)S(1)} %bitcast.24, bf16[8,1024,128]{2,1,0:T(8,128)(2,1)S(1)} %copy-done.1, ...), custom_call_target="tpu_custom_call" | custom-call | flops 2000000000 | bytes 3000000 | tf_op jit(solution)/shard_map/partial/pallas_call | solution.py:451
  62.8 5.1 %collective-permute-start.22 = (bf16[32,256]{1,0:T(8,128)(2,1)S(1)}, bf16[32,256]{1,0:T(8,128)(2,1)S(1)}, u32[]{:S(2)}, u32[]{:S(2)}) collective-permute-start(bf16[32,256]{1,0:T(8,128)(2,1)S(1)} %pad_maximum_fusion.19), channel_id=1, source_target_pairs={{0,192},{1,193},{2,194},{3,195},{4,196},{5,197},{6,198},{7,199},{8... | collective-permute-start | bytes 49160 | tf_op jit(solution)/shard_map/ppermute | solution.py:229
  68.0 1.7 %collective-permute-done.22 = bf16[32,256]{1,0:T(8,128)(2,1)S(1)} collective-permute-done((bf16[32,256]{1,0:T(8,128)(2,1)S(1)}, bf16[32,256]{1,0:T(8,128)(2,1)S(1)}, u32[]{:S(2)}, u32[]{:S(2)}) %collective-permute-start.22) | collective-permute-done | bytes 16416 | tf_op jit(solution)/shard_map/ppermute | solution.py:229
  69.7 1.0 %last.1 = (f32[32,1024]{1,0:T(8,128)}, f32[32,1024]{1,0:T(8,128)}) custom-call(bf16[512,128]{1,0:T(8,128)(2,1)S(1)} %get-tuple-element.37.coupling, bf16[1024,256]{1,0:T(8,128)(2,1)S(1)} %moved.1, f32[32,1024]{1,0:T(8,128)S(1)} %get-tuple-element.41.prod, f32[32,1024]{1,0:T(8,128)S(1)} %get-tuple-element.42.sol, ...), custom_call_target="tpu_custom_call" | custom-call | flops 30000000 | bytes 1000000 | tf_op jit(solution)/shard_map/last/pallas_call | solution.py:470
  (105 shorter events, 5.9 us)
Async XLA Ops:
  6.0 2.0 %collective-permute-start = (bf16[128,1920]{1,0:T(8,128)(2,1)S(1)}, bf16[128,1920]{1,0:T(8,128)(2,1)S(1)}, u32[]{:S(2)}, u32[]{:S(2)}) collective-permute-start(bf16[128,1920]{1,0:T(8,128)(2,1)S(1)} %get-tuple-element.29), channel_id=1, source_target_pairs={{0,4},{1,5},{2,6},{3,7},{4,0},{5,1},{6,2},{7,3},{8,12},{9,13},{10,... | collective-permute-start | bytes 1474568 | tf_op jit(solution)/shard_map/ppermute | solution.py:229
  8.2 7.8 %collective-permute-start.1 = (bf16[32,3072]{1,0:T(8,128)(2,1)S(1)}, bf16[32,3072]{1,0:T(8,128)(2,1)S(1)}, u32[]{:S(2)}, u32[]{:S(2)}) collective-permute-start(bf16[32,3072]{1,0:T(8,128)(2,1)S(1)} %pad_maximum_fusion.1.lead), channel_id=1, source_target_pairs={{0,1},{1,0},{2,3},{3,2},{4,5},{5,4},{6,7},{7,6},{8,9},{9,8},{10,11... | collective-permute-start | bytes 589832 | tf_op jit(solution)/shard_map/ppermute | solution.py:229
  9.9 10.9 %collective-permute-start.5 = (bf16[32,1920]{1,0:T(8,128)(2,1)S(1)}, bf16[32,1920]{1,0:T(8,128)(2,1)S(1)}, u32[]{:S(2)}, u32[]{:S(2)}) collective-permute-start(bf16[32,1920]{1,0:T(8,128)(2,1)S(1)} %get-tuple-element.64), channel_id=1, source_target_pairs={{0,2},{1,3},{2,0},{3,1},{4,6},{5,7},{6,4},{7,5},{8,10},{9,11},{10,... | collective-permute-start | bytes 368648 | tf_op jit(solution)/shard_map/ppermute | solution.py:229
  12.8 8.8 %collective-permute-start.6 = (bf16[32,1920]{1,0:T(8,128)(2,1)S(1)}, bf16[32,1920]{1,0:T(8,128)(2,1)S(1)}, u32[]{:S(2)}, u32[]{:S(2)}) collective-permute-start(bf16[32,1920]{1,0:T(8,128)(2,1)S(1)} %get-tuple-element.65), channel_id=1, source_target_pairs={{0,3},{1,2},{2,1},{3,0},{4,7},{5,6},{6,5},{7,4},{8,11},{9,10},{10,... | collective-permute-start | bytes 368648 | tf_op jit(solution)/shard_map/ppermute | solution.py:229
  16.0 18.5 %copy-start = (bf16[1024,1024]{1,0:T(8,128)(2,1)S(1)}, bf16[1024,1024]{1,0:T(8,128)(2,1)}, u32[]{:S(2)}) copy-start(bf16[1024,1024]{1,0:T(8,128)(2,1)} %block.1) | copy-start | bytes 6291460
  16.0 18.5 %copy-start.3 = (s32[1,1024]{1,0:T(1,128)S(1)}, s32[1,1024]{1,0:T(1,128)}, u32[]{:S(2)}) copy-start(s32[1,1024]{1,0:T(1,128)} %order.3) | copy-start | bytes 12292
  16.2 9.3 %collective-permute-start.2 = (bf16[32,128]{1,0:T(8,128)(2,1)S(1)}, bf16[32,128]{1,0:T(8,128)(2,1)S(1)}, u32[]{:S(2)}, u32[]{:S(2)}) collective-permute-start(bf16[32,128]{1,0:T(8,128)(2,1)S(1)} %slice.691), channel_id=1, source_target_pairs={{0,2},{1,3},{2,0},{3,1},{4,6},{5,7},{6,4},{7,5},{8,10},{9,11},{10,... | collective-permute-start | bytes 24584 | tf_op jit(solution)/shard_map/ppermute | solution.py:229
  19.5 6.5 %collective-permute-start.4 = (bf16[32,128]{1,0:T(8,128)(2,1)S(1)}, bf16[32,128]{1,0:T(8,128)(2,1)S(1)}, u32[]{:S(2)}, u32[]{:S(2)}) collective-permute-start(bf16[32,128]{1,0:T(8,128)(2,1)S(1)} %slice.691), channel_id=1, source_target_pairs={{0,1},{1,0},{2,3},{3,2},{4,5},{5,4},{6,7},{7,6},{8,9},{9,8},{10,11... | collective-permute-start | bytes 24584 | tf_op jit(solution)/shard_map/ppermute | solution.py:229
  20.2 5.8 %collective-permute-start.3 = (bf16[32,1024]{1,0:T(8,128)(2,1)S(1)}, bf16[32,1024]{1,0:T(8,128)(2,1)S(1)}, u32[]{:S(2)}, u32[]{:S(2)}) collective-permute-start(bf16[32,1024]{1,0:T(8,128)(2,1)S(1)} %pad_maximum_fusion.6), channel_id=1, source_target_pairs={{0,3},{1,2},{2,1},{3,0},{4,7},{5,6},{6,5},{7,4},{8,11},{9,10},{10,... | collective-permute-start | bytes 196616 | tf_op jit(solution)/shard_map/ppermute | solution.py:229
  21.9 8.1 %collective-permute-start.9 = (bf16[32,768]{1,0:T(8,128)(2,1)S(1)}, bf16[32,768]{1,0:T(8,128)(2,1)S(1)}, u32[]{:S(2)}, u32[]{:S(2)}) collective-permute-start(bf16[32,768]{1,0:T(8,128)(2,1)S(1)} %behind.4), channel_id=1, source_target_pairs={{0,24},{1,25},{2,26},{3,27},{4,28},{5,29},{6,30},{7,31},{8,16},{9,... | collective-permute-start | bytes 147464 | tf_op jit(solution)/shard_map/ppermute | solution.py:229
  24.7 5.6 %collective-permute-start.8 = (bf16[32,768]{1,0:T(8,128)(2,1)S(1)}, bf16[32,768]{1,0:T(8,128)(2,1)S(1)}, u32[]{:S(2)}, u32[]{:S(2)}) collective-permute-start(bf16[32,768]{1,0:T(8,128)(2,1)S(1)} %behind.4), channel_id=1, source_target_pairs={{0,16},{1,17},{2,18},{3,19},{4,20},{5,21},{6,22},{7,23},{8,24},{9,... | collective-permute-start | bytes 147464 | tf_op jit(solution)/shard_map/ppermute | solution.py:229
  25.5 4.4 %collective-permute-start.7 = (bf16[32,1280]{1,0:T(8,128)(2,1)S(1)}, bf16[32,1280]{1,0:T(8,128)(2,1)S(1)}, u32[]{:S(2)}, u32[]{:S(2)}) collective-permute-start(bf16[32,1280]{1,0:T(8,128)(2,1)S(1)} %slice.444.lead_in), channel_id=1, source_target_pairs={{0,8},{1,9},{2,10},{3,11},{4,12},{5,13},{6,14},{7,15},{8,0},{9,1},... | collective-permute-start | bytes 245768 | tf_op jit(solution)/shard_map/ppermute | solution.py:229
  30.4 5.9 %copy-start.1 = (bf16[8,1024,128]{2,1,0:T(8,128)(2,1)S(1)}, bf16[8,1024,128]{2,1,0:T(8,128)(2,1)}, u32[]{:S(2)}) copy-start(bf16[8,1024,128]{2,1,0:T(8,128)(2,1)} %left.7) | copy-start | bytes 6291460
  30.4 6.9 %collective-permute-start.12 = (bf16[32,2688]{1,0:T(8,128)(2,1)S(1)}, bf16[32,2688]{1,0:T(8,128)(2,1)S(1)}, u32[]{:S(2)}, u32[]{:S(2)}) collective-permute-start(bf16[32,2688]{1,0:T(8,128)(2,1)S(1)} %pad_maximum_fusion.2.lead), channel_id=1, source_target_pairs={{0,3},{1,2},{2,1},{3,0},{4,7},{5,6},{6,5},{7,4},{8,11},{9,10},{10,... | collective-permute-start | bytes 516104 | tf_op jit(solution)/shard_map/ppermute | solution.py:229
  32.4 6.9 %collective-permute-start.11 = (bf16[32,2688]{1,0:T(8,128)(2,1)S(1)}, bf16[32,2688]{1,0:T(8,128)(2,1)S(1)}, u32[]{:S(2)}, u32[]{:S(2)}) collective-permute-start(bf16[32,2688]{1,0:T(8,128)(2,1)S(1)} %pad_maximum_fusion.2.lead), channel_id=1, source_target_pairs={{0,2},{1,3},{2,0},{3,1},{4,6},{5,7},{6,4},{7,5},{8,10},{9,11},{10,... | collective-permute-start | bytes 516104 | tf_op jit(solution)/shard_map/ppermute | solution.py:229
  33.0 6.8 %collective-permute-start.10 = (bf16[32,2688]{1,0:T(8,128)(2,1)S(1)}, bf16[32,2688]{1,0:T(8,128)(2,1)S(1)}, u32[]{:S(2)}, u32[]{:S(2)}) collective-permute-start(bf16[32,2688]{1,0:T(8,128)(2,1)S(1)} %pad_maximum_fusion.2.lead), channel_id=1, source_target_pairs={{0,1},{1,0},{2,3},{3,2},{4,5},{5,4},{6,7},{7,6},{8,9},{9,8},{10,11... | collective-permute-start | bytes 516104 | tf_op jit(solution)/shard_map/ppermute | solution.py:229
  40.3 2.0 %collective-permute-start.13 = (bf16[32,7680]{1,0:T(8,128)(2,1)S(1)}, bf16[32,7680]{1,0:T(8,128)(2,1)S(1)}, u32[]{:S(2)}, u32[]{:S(2)}) collective-permute-start(bf16[32,7680]{1,0:T(8,128)(2,1)S(1)} %get-tuple-element.82), channel_id=1, source_target_pairs={{0,4},{1,5},{2,6},{3,7},{4,0},{5,1},{6,2},{7,3},{8,12},{9,13},{10,... | collective-permute-start | bytes 1474568 | tf_op jit(solution)/shard_map/ppermute | solution.py:229
  42.6 4.6 %collective-permute-start.14 = (bf16[32,1280]{1,0:T(8,128)(2,1)S(1)}, bf16[32,1280]{1,0:T(8,128)(2,1)S(1)}, u32[]{:S(2)}, u32[]{:S(2)}) collective-permute-start(bf16[32,1280]{1,0:T(8,128)(2,1)S(1)} %pad_maximum_fusion.5.lead_in), channel_id=1, source_target_pairs={{0,8},{1,9},{2,10},{3,11},{4,12},{5,13},{6,14},{7,15},{8,0},{9,1},... | collective-permute-start | bytes 245768 | tf_op jit(solution)/shard_map/ppermute | solution.py:229
  42.9 6.3 %collective-permute-start.17 = (bf16[32,1536]{1,0:T(8,128)(2,1)S(1)}, bf16[32,1536]{1,0:T(8,128)(2,1)S(1)}, u32[]{:S(2)}, u32[]{:S(2)}) collective-permute-start(bf16[32,1536]{1,0:T(8,128)(2,1)S(1)} %behind.5.refs_0_), channel_id=1, source_target_pairs={{0,32},{1,33},{2,34},{3,35},{4,36},{5,37},{6,38},{7,39},{8,40},{9,... | collective-permute-start | bytes 294920 | tf_op jit(solution)/shard_map/ppermute | solution.py:229
  47.3 5.6 %collective-permute-start.15 = (bf16[32,1024]{1,0:T(8,128)(2,1)S(1)}, bf16[32,1024]{1,0:T(8,128)(2,1)S(1)}, u32[]{:S(2)}, u32[]{:S(2)}) collective-permute-start(bf16[32,1024]{1,0:T(8,128)(2,1)S(1)} %pad_maximum_fusion.7.lead_in), channel_id=1, source_target_pairs={{0,24},{1,25},{2,26},{3,27},{4,28},{5,29},{6,30},{7,31},{8,16},{9,... | collective-permute-start | bytes 196616 | tf_op jit(solution)/shard_map/ppermute | solution.py:229
  49.3 5.2 %collective-permute-start.20 = (bf16[32,512]{1,0:T(8,128)(2,1)S(1)}, bf16[32,512]{1,0:T(8,128)(2,1)S(1)}, u32[]{:S(2)}, u32[]{:S(2)}) collective-permute-start(bf16[32,512]{1,0:T(8,128)(2,1)S(1)} %pad_maximum_fusion.11.refs_0_), channel_id=1, source_target_pairs={{0,64},{1,65},{2,66},{3,67},{4,68},{5,69},{6,70},{7,71},{8,72},{9,... | collective-permute-start | bytes 98312 | tf_op jit(solution)/shard_map/ppermute | solution.py:229
  52.7 2.0 %collective-permute-start.18 = (bf16[32,1024]{1,0:T(8,128)(2,1)S(1)}, bf16[32,1024]{1,0:T(8,128)(2,1)S(1)}, u32[]{:S(2)}, u32[]{:S(2)}) collective-permute-start(bf16[32,1024]{1,0:T(8,128)(2,1)S(1)} %pad_maximum_fusion.8.mine_in), channel_id=1, source_target_pairs={{0,4},{1,5},{2,6},{3,7},{4,0},{5,1},{6,2},{7,3},{8,12},{9,13},{10,... | collective-permute-start | bytes 196616 | tf_op jit(solution)/shard_map/ppermute | solution.py:229
  53.1 4.2 %collective-permute-start.16 = (bf16[32,768]{1,0:T(8,128)(2,1)S(1)}, bf16[32,768]{1,0:T(8,128)(2,1)S(1)}, u32[]{:S(2)}, u32[]{:S(2)}) collective-permute-start(bf16[32,768]{1,0:T(8,128)(2,1)S(1)} %pad_maximum_fusion.9.lead_in), channel_id=1, source_target_pairs={{0,32},{1,33},{2,34},{3,35},{4,36},{5,37},{6,38},{7,39},{8,40},{9,... | collective-permute-start | bytes 147464 | tf_op jit(solution)/shard_map/ppermute | solution.py:229
  54.6 1.3 %collective-permute-start.21 = (bf16[32,512]{1,0:T(8,128)(2,1)S(1)}, bf16[32,512]{1,0:T(8,128)(2,1)S(1)}, u32[]{:S(2)}, u32[]{:S(2)}) collective-permute-start(bf16[32,512]{1,0:T(8,128)(2,1)S(1)} %behind.7.mine_in), channel_id=1, source_target_pairs={{0,4},{1,5},{2,6},{3,7},{4,0},{5,1},{6,2},{7,3},{8,12},{9,13},{10,... | collective-permute-start | bytes 98312 | tf_op jit(solution)/shard_map/ppermute | solution.py:229
  54.7 6.1 %copy-start.2 = (bf16[1,8,256,128]{3,2,1,0:T(8,128)(2,1)S(1)}, bf16[1,8,256,128]{3,2,1,0:T(8,128)(2,1)}, u32[]{:S(2)}) copy-start(bf16[1,8,256,128]{3,2,1,0:T(8,128)(2,1)} %param.15) | copy-start | bytes 1572868
  57.5 5.2 %collective-permute-start.19 = (bf16[32,512]{1,0:T(8,128)(2,1)S(1)}, bf16[32,512]{1,0:T(8,128)(2,1)S(1)}, u32[]{:S(2)}, u32[]{:S(2)}) collective-permute-start(bf16[32,512]{1,0:T(8,128)(2,1)S(1)} %pad_maximum_fusion.10), channel_id=1, source_target_pairs={{0,64},{1,65},{2,66},{3,67},{4,68},{5,69},{6,70},{7,71},{8,72},{9,... | collective-permute-start | bytes 98312 | tf_op jit(solution)/shard_map/ppermute | solution.py:229
  62.8 6.9 %collective-permute-start.22 = (bf16[32,256]{1,0:T(8,128)(2,1)S(1)}, bf16[32,256]{1,0:T(8,128)(2,1)S(1)}, u32[]{:S(2)}, u32[]{:S(2)}) collective-permute-start(bf16[32,256]{1,0:T(8,128)(2,1)S(1)} %pad_maximum_fusion.19), channel_id=1, source_target_pairs={{0,192},{1,193},{2,194},{3,195},{4,196},{5,197},{6,198},{7,199},{8... | collective-permute-start | bytes 49160 | tf_op jit(solution)/shard_map/ppermute | solution.py:229

commit v5 on v4

--- a/solution.py
+++ b/solution.py
@@ -16,7 +16,7 @@
 NT = (((1,), (1,)), ((), ()))
 LEVELS = 8
 SUMMED = 2
-BEFORE = 6
+BEFORE = 5
 
 
 def scale(level):
@@ -69,7 +69,8 @@
         level: pltpu.make_async_copy(left.at[level], left_in.at[level - SUMMED], sems.at[1, level])
         for level in range(SUMMED, LEVELS - 1)
     }
-    coupling_copy = pltpu.make_async_copy(coupling, held, sems.at[1, LEVELS])
+    kept = pl.ds(SUMMED, LEVELS - 1 - SUMMED)
+    coupling_copy = pltpu.make_async_copy(coupling.at[kept], held.at[kept], sems.at[1, LEVELS])
     for copy in small + [rights[LEVELS - 1]]:
         copy.start()
     coupling_copy.start()
@@ -90,7 +91,8 @@
 
     def turn(level):
         rights[level].wait()
-        turned[(level - 1) * LANE : level * LANE, :] = right_in[level].T
+        at = (level - SUMMED - 1) * LANE
+        turned[at : at + LANE, :] = right_in[level].T
 
     turn(LEVELS - 1)
     coupling_copy.wait()
@@ -100,7 +102,7 @@
         for level in levels[::-1]:
             lefts[level].wait()
         block = pair_of(left_in, low - SUMMED) if len(levels) == 2 else left_in[low - SUMMED]
-        gram = dot(turned[low * LANE :, :], masked_rows(block, live))
+        gram = dot(turned[(low - SUMMED) * LANE :, :], masked_rows(block, live))
         for level in levels:
             update = updates_of_level(gram, low, level, canonical(held, index, level))
             at = sum(LEVELS - 1 - below for below in range(SUMMED, level)) * LANE
@@ -108,21 +110,26 @@
             first, second = update[:LANE], update[LANE:]
             home[:, to] = jnp.where(second_core, second, first)
             away[:, to] = jnp.where(second_core, first, second)
-        for level in (low, low - 1):
-            turn(level)
-    rights[0].wait()
-
-
-def own_kernel(live, index, coupling, left, turned, lead, update_0, update_1, held, left_in, sems):
+        if low > SUMMED:
+            turn(low)
+            turn(low - 1)
+    for level in range(SUMMED, -1, -1):
+        rights[level].wait()
+
+
+def own_kernel(live, index, coupling, left, right, turned, lead, update_0, update_1, held, left_in, low_turned, sems):
     copies = [
         pltpu.make_async_copy(coupling.at[pl.ds(0, SUMMED)], held, sems.at[0]),
         pltpu.make_async_copy(left.at[pl.ds(0, SUMMED)], left_in, sems.at[1]),
     ]
     for copy in copies:
         copy.start()
+    for level in range(1, SUMMED + 1):
+        low_turned[(level - 1) * LANE : level * LANE, :] = right[level].T
     for copy in copies:
         copy.wait()
-    gram = dot(turned[...], masked_rows(pair_of(left_in, 0), live))
+    block = masked_rows(pair_of(left_in, 0), live)
+    gram = jnp.concatenate([dot(low_turned[...], block), dot(turned[...], block)], axis=0)
     for level, out in ((0, update_0), (1, update_1)):
         out[...] = updates_of_level(gram, 0, level, canonical(held, index, level))
 
@@ -299,7 +306,7 @@
         summed_kernel,
         out_shape=(pltpu.VMEM((LANE, summed * LANE), BF),) * 2
         + (pltpu.VMEM((LEVELS, 2 * points), F32), pltpu.VMEM((2 * nvec, points), BF))
-        + (pltpu.VMEM(right_bases.shape, BF), pltpu.VMEM((7 * LANE, points), BF)),
+        + (pltpu.VMEM(right_bases.shape, BF), pltpu.VMEM(((LEVELS - 1 - SUMMED) * LANE, points), BF)),
         in_specs=[SMEM, SMEM] + [HBM] * 6,
         out_specs=(VMEM,) * 6,
         scratch_shapes=[
@@ -337,17 +344,18 @@
     update_0, update_1 = pl.pallas_call(
         own_kernel,
         out_shape=(pltpu.VMEM((2 * LANE, 7 * LANE), BF), pltpu.VMEM((2 * LANE, 6 * LANE), BF)),
-        in_specs=[SMEM, SMEM, HBM, HBM, VMEM, pl.BlockSpec(memory_space=pl.ANY)],
+        in_specs=[SMEM, SMEM, HBM, HBM, VMEM, VMEM, pl.BlockSpec(memory_space=pl.ANY)],
         out_specs=(VMEM, VMEM),
         scratch_shapes=[
             pltpu.VMEM((SUMMED, 2 * LANE, LANE), BF),
             pltpu.VMEM((SUMMED, points, LANE), BF),
+            pltpu.VMEM((SUMMED * LANE, points), BF),
             pltpu.SemaphoreType.DMA((2,)),
         ],
         compiler_params=params(16),
         cost_estimate=pl.CostEstimate(flops=1_500_000_000, bytes_accessed=1_000_000, transcendentals=0),
         name="own",
-    )(live_counts, index_1, in_hbm(coupling), in_hbm(left_basis), turned, sent[1])
+    )(live_counts, index_1, in_hbm(coupling), in_hbm(left_basis), right_in, turned, sent[1])
     got = {mask: swap(sent[mask], mask) for mask in (1, 2, 3)}
     pieces = sum(
         block.astype(F32) for block in (rows_of[0], cols(got[1], 1 + LEVELS), got[2], got[3])
@@ -436,18 +444,18 @@
 
     sent = cat(total, prod)
     late = behind(sent, late, got_late)
-    own, late = from_four(late, 0, 2), from_four(late, 2, 3)
+    own = from_four(late, 0, 2)
     updates_of[5] = whole_of(own, swap(own, 4))
     got_late = swap(late, 64)
     total, prod, _ = exchange(4, 24, sent, total, prod)
     total = apply(4, total)
 
     sent = cat(total, prod)
-    late = behind(sent, late, got_late)
-    updates_of[6] = whole_of(late, swap(late, 4))
-    total, prod, _ = exchange(5, 32, sent, total, prod)
-    total = apply(5, total)
-
+    far = behind(sent, got_late)
+    last = from_four(late, 2, 3).astype(F32) + from_four(far, 2, 3).astype(F32)
+    own = cat(from_four(far, 0, 2), last)
+    theirs = swap(own, 4)
+    far_update, updates_of[6] = whole_of(cols(own, 0, 8), cols(theirs, 0, 8)), whole_of(cols(own, 8), cols(theirs, 8))
     part_prod, part_sol, last_coupling = pl.pallas_call(
         partial_kernel,
         out_shape=(pltpu.VMEM((nvec, points), F32),) * 2
@@ -462,8 +470,19 @@
         cost_estimate=pl.CostEstimate(flops=2_000_000_000, bytes_accessed=3_000_000, transcendentals=0),
         name="partial",
     )(live_counts, index_1, coupling, left_basis, tree, direct, hot, *siblings, *joined)
-    total, prod, _ = exchange(6, 64, cat(total, prod), total, prod)
-    total = apply(6, total)
+    got = [sent] + [swap(sent, mask) for mask in (32, 64, 96)]
+    sums = []
+    for low, update in ((0, updates_of[5]), (2, far_update)):
+        pair = join(cols(got[low], 0, 1), cols(got[low + 1], 0, 1), 5)
+        if low == 0:
+            joined.append(pair)
+        both = [cols(block, 1, 3).astype(F32) for block in got[low : low + 2]]
+        sums.append(both[0] + both[1] - dot(pair, update))
+    joined.append(join(cols(sums[0], 0, 1).astype(BF), cols(sums[1], 0, 1).astype(BF), 6))
+    total = cols(sums[0], 1) + cols(sums[1], 1) - dot(joined[6], updates_of[6])
+    siblings.append(cols(got[1], 3, 4))
+    siblings.append((cols(got[2], 4, 5).astype(F32) + cols(got[3], 4, 5).astype(F32)).astype(BF))
+    prod = sum(cols(block, 5).astype(F32) for block in got)
     total, part_prod, part_sol = lax.optimization_barrier((total, part_prod, part_sol))
 
     exchange(7, 192, cat(total, prod), total, prod)

time: 70.8 us -> 69.7 us (0.984)
  waiting for transfers between devices: 20.5 us -> 17.3 us
  starting transfers between devices: 33 us -> 34.1 us
    ppermute x23 -> x24, waiting for transfers between devices: 20.5 us -> 17.3 us  [swap(): lax.ppermute(block, ('leaf', 'sub'), [(i, i ^ mask) for i in range(count)])]
    ppermute x23 -> x24, starting transfers between devices: 33 us -> 34.1 us  [swap(): lax.ppermute(block, ('leaf', 'sub'), [(i, i ^ mask) for i in range(count)])]
  transfers between devices with their start and end apart: 23 -> 24, of which waited for: 15 -> 13; matrix products, arithmetic and copies ran while one was open for 2% -> 2% of each run, Pallas kernels for 10% -> 11%
where the time goes in v5:
time: 69.7 us; the launch traced here: 69.3 us
  starting transfers between devices  34.1 us (49%)
  waiting for transfers between devices  17.3 us (25%)
  Pallas kernels  13.5 us (19%)
  between operations  1.88 us (3%)
  matrix products  1.27 us (2%)
  other arithmetic  1.06 us (2%)
    ppermute x24, starting transfers between devices, swap(): lax.ppermute(block, ('leaf', 'sub'), [(i, i ^ mask) for i in range(count)])  34.1 us
    ppermute x24, waiting for transfers between devices, swap(): lax.ppermute(block, ('leaf', 'sub'), [(i, i ^ mask) for i in range(count)])  17.3 us
    pallas_call x1, Pallas kernels, per_device(): pl.pallas_call(summed_kernel, out_shape=(pltpu.VMEM((LANE, summed * LANE)...  4.47 us
    pallas_call x1, Pallas kernels, per_device(): pl.pallas_call(own_kernel, out_shape=(pltpu.VMEM((2 * LANE, 7 * LANE), BF...  2.37 us
    pallas_call x1, Pallas kernels, per_device(): pl.pallas_call(partial_kernel, out_shape=(pltpu.VMEM((nvec, points), F32)...  1.72 us
    pallas_call x1, Pallas kernels, per_device(): pl.pallas_call(direct_kernel, out_shape=(pltpu.VMEM((nvec, points), F32),...  1.66 us
    pallas_call x1, Pallas kernels, per_device(): pl.pallas_call(moved_kernel, out_shape=pltpu.VMEM((points, (LEVELS - BEFO...  1.47 us
  transfers between devices with their start and end apart: 24, of which 13 were waited for; matrix products, arithmetic and copies ran while one was open for 2% of the time, Pallas kernels for 11%

profile of v5, /device:TPU:32, one launch (start us, length us, event | category | flops | bytes accessed | tf_op | source)
XLA Modules:
  0.0 69.3 jit_solution(13002797458850346256)
XLA Ops:
  1.3 4.5 %summed.1 = (bf16[128,1920]{1,0:T(8,128)(2,1)S(1)}, bf16[128,1920]{1,0:T(8,128)(2,1)S(1)}, f32[8,2048]{1,0:T(8,128)S(1)}, bf16[64,1024]{1,0:T(8,128)(2,1)S(1)}, ...) custom-call(s32[1]{0:T(128)S(6)} %copy.19.live, s32[1]{0:T(128)} %bitcast.index.index_in, ...), custom_call_target="tpu_custom_call" | custom-call | flops 1500000000 | bytes 5000000 | tf_op jit(solution)/shard_map/summed/pallas_call | solution.py:305
  6.4 1.3 %collective-permute-done = bf16[128,1920]{1,0:T(8,128)(2,1)S(1)} collective-permute-done((bf16[128,1920]{1,0:T(8,128)(2,1)S(1)}, bf16[128,1920]{1,0:T(8,128)(2,1)S(1)}, u32[]{:S(2)}, u32[]{:S(2)}) %collective-permute-start) | collective-permute-done | bytes 491552 | tf_op jit(solution)/shard_map/ppermute | solution.py:236
  8.0 1.7 %collective-permute-start.1 = (bf16[32,3072]{1,0:T(8,128)(2,1)S(1)}, bf16[32,3072]{1,0:T(8,128)(2,1)S(1)}, u32[]{:S(2)}, u32[]{:S(2)}) collective-permute-start(bf16[32,3072]{1,0:T(8,128)(2,1)S(1)} %pad_maximum_fusion.1.lead), channel_id=1, source_target_pairs={{0,1},{1,0},{2,3},{3,2},{4,5},{5,4},{6,7},{7,6},{8,9},{9,8},{10,11... | collective-permute-start | bytes 589832 | tf_op jit(solution)/shard_map/ppermute | solution.py:236
  9.6 3.0 %collective-permute-start.5 = (bf16[32,1920]{1,0:T(8,128)(2,1)S(1)}, bf16[32,1920]{1,0:T(8,128)(2,1)S(1)}, u32[]{:S(2)}, u32[]{:S(2)}) collective-permute-start(bf16[32,1920]{1,0:T(8,128)(2,1)S(1)} %get-tuple-element.62), channel_id=1, source_target_pairs={{0,2},{1,3},{2,0},{3,1},{4,6},{5,7},{6,4},{7,5},{8,10},{9,11},{10,... | collective-permute-start | bytes 368648 | tf_op jit(solution)/shard_map/ppermute | solution.py:236
  12.9 2.4 %own.1 = (bf16[256,896]{1,0:T(8,128)(2,1)S(1)}, bf16[256,768]{1,0:T(8,128)(2,1)S(1)}) custom-call(s32[1]{0:T(128)S(6)} %copy.19.live, s32[1]{0:T(128)} %bitcast.index.index_in, bf16[8,256,128]{2,1,0:T(8,128)(2,1)} %bitcast.24, bf16[8,1024,128]{2,1,0:T(8,128)(2,1)} %left.7, bf16[8,1024,128]{2,1,0:T(8,128)(2,1)S(1)} %get-tuple-element.24.right, ...), custom_call_target="tpu_custom_call" | custom-call | flops 1500000000 | bytes 1000000 | tf_op jit(solution)/shard_map/own/pallas_call | solution.py:344
  15.2 0.6 collective-permute-done.1
  16.0 3.3 %collective-permute-start.2 = (bf16[32,128]{1,0:T(8,128)(2,1)S(1)}, bf16[32,128]{1,0:T(8,128)(2,1)S(1)}, u32[]{:S(2)}, u32[]{:S(2)}) collective-permute-start(bf16[32,128]{1,0:T(8,128)(2,1)S(1)} %slice.776), channel_id=1, source_target_pairs={{0,2},{1,3},{2,0},{3,1},{4,6},{5,7},{6,4},{7,5},{8,10},{9,11},{10,... | collective-permute-start | bytes 24584 | tf_op jit(solution)/shard_map/ppermute | solution.py:236
  19.3 0.7 collective-permute-start.4
  20.5 1.0 %collective-permute-done.6 = bf16[32,1920]{1,0:T(8,128)(2,1)S(1)} collective-permute-done((bf16[32,1920]{1,0:T(8,128)(2,1)S(1)}, bf16[32,1920]{1,0:T(8,128)(2,1)S(1)}, u32[]{:S(2)}, u32[]{:S(2)}) %collective-permute-start.6) | collective-permute-done | bytes 122912 | tf_op jit(solution)/shard_map/ppermute | solution.py:236
  21.7 2.8 %collective-permute-start.9 = (bf16[32,768]{1,0:T(8,128)(2,1)S(1)}, bf16[32,768]{1,0:T(8,128)(2,1)S(1)}, u32[]{:S(2)}, u32[]{:S(2)}) collective-permute-start(bf16[32,768]{1,0:T(8,128)(2,1)S(1)} %behind.4), channel_id=1, source_target_pairs={{0,24},{1,25},{2,26},{3,27},{4,28},{5,29},{6,30},{7,31},{8,16},{9,... | collective-permute-start | bytes 147464 | tf_op jit(solution)/shard_map/ppermute | solution.py:236
  24.5 0.8 %collective-permute-start.8 = (bf16[32,768]{1,0:T(8,128)(2,1)S(1)}, bf16[32,768]{1,0:T(8,128)(2,1)S(1)}, u32[]{:S(2)}, u32[]{:S(2)}) collective-permute-start(bf16[32,768]{1,0:T(8,128)(2,1)S(1)} %behind.4), channel_id=1, source_target_pairs={{0,16},{1,17},{2,18},{3,19},{4,20},{5,21},{6,22},{7,23},{8,24},{9,... | collective-permute-start | bytes 147464 | tf_op jit(solution)/shard_map/ppermute | solution.py:236
  26.1 3.7 %collective-permute-done.7 = bf16[32,1280]{1,0:T(8,128)(2,1)S(1)} collective-permute-done((bf16[32,1280]{1,0:T(8,128)(2,1)S(1)}, bf16[32,1280]{1,0:T(8,128)(2,1)S(1)}, u32[]{:S(2)}, u32[]{:S(2)}) %collective-permute-start.7) | collective-permute-done | bytes 81952 | tf_op jit(solution)/shard_map/ppermute | solution.py:236
  30.2 2.0 %collective-permute-start.12 = (bf16[32,2688]{1,0:T(8,128)(2,1)S(1)}, bf16[32,2688]{1,0:T(8,128)(2,1)S(1)}, u32[]{:S(2)}, u32[]{:S(2)}) collective-permute-start(bf16[32,2688]{1,0:T(8,128)(2,1)S(1)} %pad_maximum_fusion.2.lead), channel_id=1, source_target_pairs={{0,3},{1,2},{2,1},{3,0},{4,7},{5,6},{6,5},{7,4},{8,11},{9,10},{10,... | collective-permute-start | bytes 516104 | tf_op jit(solution)/shard_map/ppermute | solution.py:236
  32.2 0.6 collective-permute-start.11
  32.8 1.6 %collective-permute-start.10 = (bf16[32,2688]{1,0:T(8,128)(2,1)S(1)}, bf16[32,2688]{1,0:T(8,128)(2,1)S(1)}, u32[]{:S(2)}, u32[]{:S(2)}) collective-permute-start(bf16[32,2688]{1,0:T(8,128)(2,1)S(1)} %pad_maximum_fusion.2.lead), channel_id=1, source_target_pairs={{0,1},{1,0},{2,3},{3,2},{4,5},{5,4},{6,7},{7,6},{8,9},{9,8},{10,11... | collective-permute-start | bytes 516104 | tf_op jit(solution)/shard_map/ppermute | solution.py:236
  34.4 1.7 %direct.1 = (f32[32,1024]{1,0:T(8,128)S(1)}, bf16[1024,1024]{1,0:T(8,128)(2,1)S(1)}) custom-call(s32[1,1024]{1,0:T(1,128)S(1)} %copy-done.3, bf16[64,1024]{1,0:T(8,128)(2,1)S(1)} %get-tuple-element.23.tree, bf16[1024,1024]{1,0:T(8,128)(2,1)S(1)} %copy-done.2, bf16[32,2688]{1,0:T(8,128)(2,1)S(1)} %pad_maximum_fusion.2.lead), custom_call_target="tpu_custom_call" | custom-call | flops 2000000000 | bytes 2000000 | tf_op jit(solution)/shard_map/direct/pallas_call | solution.py:385
  36.0 1.5 %moved.1 = bf16[1024,384]{1,0:T(8,128)(2,1)S(1)} custom-call(s32[1]{0:T(128)S(6)} %copy.19.live, bf16[1024,1024]{1,0:T(8,128)(2,1)S(1)} %get-tuple-element.33.hot, bf16[8,1024,128]{2,1,0:T(8,128)(2,1)S(1)} %copy-done), custom_call_target="tpu_custom_call" | custom-call | flops 1500000000 | bytes 2000000 | tf_op jit(solution)/shard_map/moved/pallas_call | solution.py:394
  37.5 1.6 %collective-permute-done.11 = bf16[32,2688]{1,0:T(8,128)(2,1)S(1)} collective-permute-done((bf16[32,2688]{1,0:T(8,128)(2,1)S(1)}, bf16[32,2688]{1,0:T(8,128)(2,1)S(1)}, u32[]{:S(2)}, u32[]{:S(2)}) %collective-permute-start.11) | collective-permute-done | bytes 172064 | tf_op jit(solution)/shard_map/ppermute | solution.py:236
  39.1 0.5 collective-permute-done.10
  40.2 1.8 %collective-permute-done.13 = bf16[32,7680]{1,0:T(8,128)(2,1)S(1)} collective-permute-done((bf16[32,7680]{1,0:T(8,128)(2,1)S(1)}, bf16[32,7680]{1,0:T(8,128)(2,1)S(1)}, u32[]{:S(2)}, u32[]{:S(2)}) %collective-permute-start.13) | collective-permute-done | bytes 491552 | tf_op jit(solution)/shard_map/ppermute | solution.py:236
  42.7 0.8 %collective-permute-start.17 = (bf16[32,1536]{1,0:T(8,128)(2,1)S(1)}, bf16[32,1536]{1,0:T(8,128)(2,1)S(1)}, u32[]{:S(2)}, u32[]{:S(2)}) collective-permute-start(bf16[32,1536]{1,0:T(8,128)(2,1)S(1)} %behind.5.refs_0_), channel_id=1, source_target_pairs={{0,32},{1,33},{2,34},{3,35},{4,36},{5,37},{6,38},{7,39},{8,40},{9,... | collective-permute-start | bytes 294920 | tf_op jit(solution)/shard_map/ppermute | solution.py:236
  43.5 3.4 %collective-permute-done.14 = bf16[32,1280]{1,0:T(8,128)(2,1)S(1)} collective-permute-done((bf16[32,1280]{1,0:T(8,128)(2,1)S(1)}, bf16[32,1280]{1,0:T(8,128)(2,1)S(1)}, u32[]{:S(2)}, u32[]{:S(2)}) %collective-permute-start.14) | collective-permute-done | bytes 81952 | tf_op jit(solution)/shard_map/ppermute | solution.py:236
  47.1 1.9 %collective-permute-start.15 = (bf16[32,1024]{1,0:T(8,128)(2,1)S(1)}, bf16[32,1024]{1,0:T(8,128)(2,1)S(1)}, u32[]{:S(2)}, u32[]{:S(2)}) collective-permute-start(bf16[32,1024]{1,0:T(8,128)(2,1)S(1)} %pad_maximum_fusion.7.lead_in), channel_id=1, source_target_pairs={{0,24},{1,25},{2,26},{3,27},{4,28},{5,29},{6,30},{7,31},{8,16},{9,... | collective-permute-start | bytes 196616 | tf_op jit(solution)/shard_map/ppermute | solution.py:236
  49.1 3.3 %collective-permute-start.21 = (bf16[32,1536]{1,0:T(8,128)(2,1)S(1)}, bf16[32,1536]{1,0:T(8,128)(2,1)S(1)}, u32[]{:S(2)}, u32[]{:S(2)}) collective-permute-start(bf16[32,1536]{1,0:T(8,128)(2,1)S(1)} %behind.6), channel_id=1, source_target_pairs={{0,64},{1,65},{2,66},{3,67},{4,68},{5,69},{6,70},{7,71},{8,72},{9,... | collective-permute-start | bytes 294920 | tf_op jit(solution)/shard_map/ppermute | solution.py:236
  52.9 2.0 %collective-permute-start.20 = (bf16[32,768]{1,0:T(8,128)(2,1)S(1)}, bf16[32,768]{1,0:T(8,128)(2,1)S(1)}, u32[]{:S(2)}, u32[]{:S(2)}) collective-permute-start(bf16[32,768]{1,0:T(8,128)(2,1)S(1)} %pad_maximum_fusion.10.lead_in), channel_id=1, source_target_pairs={{0,96},{1,97},{2,98},{3,99},{4,100},{5,101},{6,102},{7,103},{8,104... | collective-permute-start | bytes 147464 | tf_op jit(solution)/shard_map/ppermute | solution.py:236
  54.9 1.5 %collective-permute-start.19 = (bf16[32,768]{1,0:T(8,128)(2,1)S(1)}, bf16[32,768]{1,0:T(8,128)(2,1)S(1)}, u32[]{:S(2)}, u32[]{:S(2)}) collective-permute-start(bf16[32,768]{1,0:T(8,128)(2,1)S(1)} %pad_maximum_fusion.10.lead_in), channel_id=1, source_target_pairs={{0,64},{1,65},{2,66},{3,67},{4,68},{5,69},{6,70},{7,71},{8,72},{9,... | collective-permute-start | bytes 147464 | tf_op jit(solution)/shard_map/ppermute | solution.py:236
  56.4 1.4 %collective-permute-start.16 = (bf16[32,768]{1,0:T(8,128)(2,1)S(1)}, bf16[32,768]{1,0:T(8,128)(2,1)S(1)}, u32[]{:S(2)}, u32[]{:S(2)}) collective-permute-start(bf16[32,768]{1,0:T(8,128)(2,1)S(1)} %pad_maximum_fusion.10.lead_in), channel_id=1, source_target_pairs={{0,32},{1,33},{2,34},{3,35},{4,36},{5,37},{6,38},{7,39},{8,40},{9,... | collective-permute-start | bytes 147464 | tf_op jit(solution)/shard_map/ppermute | solution.py:236
  57.7 1.7 %partial.1 = (f32[32,1024]{1,0:T(8,128)S(1)}, f32[32,1024]{1,0:T(8,128)S(1)}, bf16[768,128]{1,0:T(8,128)(2,1)S(1)}) custom-call(s32[1]{0:T(128)S(6)} %copy.19.live, s32[1]{0:T(128)} %bitcast.index.index_in, bf16[8,256,128]{2,1,0:T(8,128)(2,1)S(1)} %bitcast.25, bf16[8,1024,128]{2,1,0:T(8,128)(2,1)S(1)} %copy-done, ...), custom_call_target="tpu_custom_call" | custom-call | flops 2000000000 | bytes 3000000 | tf_op jit(solution)/shard_map/partial/pallas_call | solution.py:459
  59.9 1.0 %collective-permute-done.16 = bf16[32,768]{1,0:T(8,128)(2,1)S(1)} collective-permute-done((bf16[32,768]{1,0:T(8,128)(2,1)S(1)}, bf16[32,768]{1,0:T(8,128)(2,1)S(1)}, u32[]{:S(2)}, u32[]{:S(2)}) %collective-permute-start.16) | collective-permute-done | bytes 49184 | tf_op jit(solution)/shard_map/ppermute | solution.py:236
  61.5 5.0 %collective-permute-start.23 = (bf16[32,256]{1,0:T(8,128)(2,1)S(1)}, bf16[32,256]{1,0:T(8,128)(2,1)S(1)}, u32[]{:S(2)}, u32[]{:S(2)}) collective-permute-start(bf16[32,256]{1,0:T(8,128)(2,1)S(1)} %pad_maximum_fusion.18), channel_id=1, source_target_pairs={{0,192},{1,193},{2,194},{3,195},{4,196},{5,197},{6,198},{7,199},{8... | collective-permute-start | bytes 49160 | tf_op jit(solution)/shard_map/ppermute | solution.py:236
  66.5 1.7 %collective-permute-done.23 = bf16[32,256]{1,0:T(8,128)(2,1)S(1)} collective-permute-done((bf16[32,256]{1,0:T(8,128)(2,1)S(1)}, bf16[32,256]{1,0:T(8,128)(2,1)S(1)}, u32[]{:S(2)}, u32[]{:S(2)}) %collective-permute-start.23) | collective-permute-done | bytes 16416 | tf_op jit(solution)/shard_map/ppermute | solution.py:236
  68.2 1.1 %last.1 = (f32[32,1024]{1,0:T(8,128)}, f32[32,1024]{1,0:T(8,128)}) custom-call(bf16[768,128]{1,0:T(8,128)(2,1)S(1)} %get-tuple-element.37.coupling, bf16[1024,384]{1,0:T(8,128)(2,1)S(1)} %moved.1, f32[32,1024]{1,0:T(8,128)S(1)} %get-tuple-element.41.prod, f32[32,1024]{1,0:T(8,128)S(1)} %get-tuple-element.42.sol, ...), custom_call_target="tpu_custom_call" | custom-call | flops 30000000 | bytes 1000000 | tf_op jit(solution)/shard_map/last/pallas_call | solution.py:489
  (114 shorter events, 5.8 us)
Async XLA Ops:
  5.8 2.0 %collective-permute-start = (bf16[128,1920]{1,0:T(8,128)(2,1)S(1)}, bf16[128,1920]{1,0:T(8,128)(2,1)S(1)}, u32[]{:S(2)}, u32[]{:S(2)}) collective-permute-start(bf16[128,1920]{1,0:T(8,128)(2,1)S(1)} %get-tuple-element.29), channel_id=1, source_target_pairs={{0,4},{1,5},{2,6},{3,7},{4,0},{5,1},{6,2},{7,3},{8,12},{9,13},{10,... | collective-permute-start | bytes 1474568 | tf_op jit(solution)/shard_map/ppermute | solution.py:236
  8.0 7.8 %collective-permute-start.1 = (bf16[32,3072]{1,0:T(8,128)(2,1)S(1)}, bf16[32,3072]{1,0:T(8,128)(2,1)S(1)}, u32[]{:S(2)}, u32[]{:S(2)}) collective-permute-start(bf16[32,3072]{1,0:T(8,128)(2,1)S(1)} %pad_maximum_fusion.1.lead), channel_id=1, source_target_pairs={{0,1},{1,0},{2,3},{3,2},{4,5},{5,4},{6,7},{7,6},{8,9},{9,8},{10,11... | collective-permute-start | bytes 589832 | tf_op jit(solution)/shard_map/ppermute | solution.py:236
  9.6 10.9 %collective-permute-start.5 = (bf16[32,1920]{1,0:T(8,128)(2,1)S(1)}, bf16[32,1920]{1,0:T(8,128)(2,1)S(1)}, u32[]{:S(2)}, u32[]{:S(2)}) collective-permute-start(bf16[32,1920]{1,0:T(8,128)(2,1)S(1)} %get-tuple-element.62), channel_id=1, source_target_pairs={{0,2},{1,3},{2,0},{3,1},{4,6},{5,7},{6,4},{7,5},{8,10},{9,11},{10,... | collective-permute-start | bytes 368648 | tf_op jit(solution)/shard_map/ppermute | solution.py:236
  12.6 8.8 %collective-permute-start.6 = (bf16[32,1920]{1,0:T(8,128)(2,1)S(1)}, bf16[32,1920]{1,0:T(8,128)(2,1)S(1)}, u32[]{:S(2)}, u32[]{:S(2)}) collective-permute-start(bf16[32,1920]{1,0:T(8,128)(2,1)S(1)} %get-tuple-element.63), channel_id=1, source_target_pairs={{0,3},{1,2},{2,1},{3,0},{4,7},{5,6},{6,5},{7,4},{8,11},{9,10},{10,... | collective-permute-start | bytes 368648 | tf_op jit(solution)/shard_map/ppermute | solution.py:236
  15.8 18.5 %copy-start.2 = (bf16[1024,1024]{1,0:T(8,128)(2,1)S(1)}, bf16[1024,1024]{1,0:T(8,128)(2,1)}, u32[]{:S(2)}) copy-start(bf16[1024,1024]{1,0:T(8,128)(2,1)} %block.1) | copy-start | bytes 6291460
  15.8 18.5 %copy-start.3 = (s32[1,1024]{1,0:T(1,128)S(1)}, s32[1,1024]{1,0:T(1,128)}, u32[]{:S(2)}) copy-start(s32[1,1024]{1,0:T(1,128)} %order.3) | copy-start | bytes 12292
  16.0 9.3 %collective-permute-start.2 = (bf16[32,128]{1,0:T(8,128)(2,1)S(1)}, bf16[32,128]{1,0:T(8,128)(2,1)S(1)}, u32[]{:S(2)}, u32[]{:S(2)}) collective-permute-start(bf16[32,128]{1,0:T(8,128)(2,1)S(1)} %slice.776), channel_id=1, source_target_pairs={{0,2},{1,3},{2,0},{3,1},{4,6},{5,7},{6,4},{7,5},{8,10},{9,11},{10,... | collective-permute-start | bytes 24584 | tf_op jit(solution)/shard_map/ppermute | solution.py:236
  19.3 6.5 %collective-permute-start.4 = (bf16[32,128]{1,0:T(8,128)(2,1)S(1)}, bf16[32,128]{1,0:T(8,128)(2,1)S(1)}, u32[]{:S(2)}, u32[]{:S(2)}) collective-permute-start(bf16[32,128]{1,0:T(8,128)(2,1)S(1)} %slice.776), channel_id=1, source_target_pairs={{0,1},{1,0},{2,3},{3,2},{4,5},{5,4},{6,7},{7,6},{8,9},{9,8},{10,11... | collective-permute-start | bytes 24584 | tf_op jit(solution)/shard_map/ppermute | solution.py:236
  20.0 5.8 %collective-permute-start.3 = (bf16[32,1024]{1,0:T(8,128)(2,1)S(1)}, bf16[32,1024]{1,0:T(8,128)(2,1)S(1)}, u32[]{:S(2)}, u32[]{:S(2)}) collective-permute-start(bf16[32,1024]{1,0:T(8,128)(2,1)S(1)} %pad_maximum_fusion.6), channel_id=1, source_target_pairs={{0,3},{1,2},{2,1},{3,0},{4,7},{5,6},{6,5},{7,4},{8,11},{9,10},{10,... | collective-permute-start | bytes 196616 | tf_op jit(solution)/shard_map/ppermute | solution.py:236
  21.7 8.1 %collective-permute-start.9 = (bf16[32,768]{1,0:T(8,128)(2,1)S(1)}, bf16[32,768]{1,0:T(8,128)(2,1)S(1)}, u32[]{:S(2)}, u32[]{:S(2)}) collective-permute-start(bf16[32,768]{1,0:T(8,128)(2,1)S(1)} %behind.4), channel_id=1, source_target_pairs={{0,24},{1,25},{2,26},{3,27},{4,28},{5,29},{6,30},{7,31},{8,16},{9,... | collective-permute-start | bytes 147464 | tf_op jit(solution)/shard_map/ppermute | solution.py:236
  24.5 5.6 %collective-permute-start.8 = (bf16[32,768]{1,0:T(8,128)(2,1)S(1)}, bf16[32,768]{1,0:T(8,128)(2,1)S(1)}, u32[]{:S(2)}, u32[]{:S(2)}) collective-permute-start(bf16[32,768]{1,0:T(8,128)(2,1)S(1)} %behind.4), channel_id=1, source_target_pairs={{0,16},{1,17},{2,18},{3,19},{4,20},{5,21},{6,22},{7,23},{8,24},{9,... | collective-permute-start | bytes 147464 | tf_op jit(solution)/shard_map/ppermute | solution.py:236
  25.3 4.4 %collective-permute-start.7 = (bf16[32,1280]{1,0:T(8,128)(2,1)S(1)}, bf16[32,1280]{1,0:T(8,128)(2,1)S(1)}, u32[]{:S(2)}, u32[]{:S(2)}) collective-permute-start(bf16[32,1280]{1,0:T(8,128)(2,1)S(1)} %slice.496.lead_in), channel_id=1, source_target_pairs={{0,8},{1,9},{2,10},{3,11},{4,12},{5,13},{6,14},{7,15},{8,0},{9,1},... | collective-permute-start | bytes 245768 | tf_op jit(solution)/shard_map/ppermute | solution.py:236
  30.2 5.9 %copy-start = (bf16[8,1024,128]{2,1,0:T(8,128)(2,1)S(1)}, bf16[8,1024,128]{2,1,0:T(8,128)(2,1)}, u32[]{:S(2)}) copy-start(bf16[8,1024,128]{2,1,0:T(8,128)(2,1)} %left.7) | copy-start | bytes 6291460
  30.2 7.3 %collective-permute-start.12 = (bf16[32,2688]{1,0:T(8,128)(2,1)S(1)}, bf16[32,2688]{1,0:T(8,128)(2,1)S(1)}, u32[]{:S(2)}, u32[]{:S(2)}) collective-permute-start(bf16[32,2688]{1,0:T(8,128)(2,1)S(1)} %pad_maximum_fusion.2.lead), channel_id=1, source_target_pairs={{0,3},{1,2},{2,1},{3,0},{4,7},{5,6},{6,5},{7,4},{8,11},{9,10},{10,... | collective-permute-start | bytes 516104 | tf_op jit(solution)/shard_map/ppermute | solution.py:236
  32.2 6.9 %collective-permute-start.11 = (bf16[32,2688]{1,0:T(8,128)(2,1)S(1)}, bf16[32,2688]{1,0:T(8,128)(2,1)S(1)}, u32[]{:S(2)}, u32[]{:S(2)}) collective-permute-start(bf16[32,2688]{1,0:T(8,128)(2,1)S(1)} %pad_maximum_fusion.2.lead), channel_id=1, source_target_pairs={{0,2},{1,3},{2,0},{3,1},{4,6},{5,7},{6,4},{7,5},{8,10},{9,11},{10,... | collective-permute-start | bytes 516104 | tf_op jit(solution)/shard_map/ppermute | solution.py:236
  32.8 6.8 %collective-permute-start.10 = (bf16[32,2688]{1,0:T(8,128)(2,1)S(1)}, bf16[32,2688]{1,0:T(8,128)(2,1)S(1)}, u32[]{:S(2)}, u32[]{:S(2)}) collective-permute-start(bf16[32,2688]{1,0:T(8,128)(2,1)S(1)} %pad_maximum_fusion.2.lead), channel_id=1, source_target_pairs={{0,1},{1,0},{2,3},{3,2},{4,5},{5,4},{6,7},{7,6},{8,9},{9,8},{10,11... | collective-permute-start | bytes 516104 | tf_op jit(solution)/shard_map/ppermute | solution.py:236
  40.1 2.0 %collective-permute-start.13 = (bf16[32,7680]{1,0:T(8,128)(2,1)S(1)}, bf16[32,7680]{1,0:T(8,128)(2,1)S(1)}, u32[]{:S(2)}, u32[]{:S(2)}) collective-permute-start(bf16[32,7680]{1,0:T(8,128)(2,1)S(1)} %get-tuple-element.80), channel_id=1, source_target_pairs={{0,4},{1,5},{2,6},{3,7},{4,0},{5,1},{6,2},{7,3},{8,12},{9,13},{10,... | collective-permute-start | bytes 1474568 | tf_op jit(solution)/shard_map/ppermute | solution.py:236
  42.1 15.6 %copy-start.1 = (bf16[1,8,256,128]{3,2,1,0:T(8,128)(2,1)S(1)}, bf16[1,8,256,128]{3,2,1,0:T(8,128)(2,1)}, u32[]{:S(2)}) copy-start(bf16[1,8,256,128]{3,2,1,0:T(8,128)(2,1)} %param.15) | copy-start | bytes 1572868
  42.4 4.6 %collective-permute-start.14 = (bf16[32,1280]{1,0:T(8,128)(2,1)S(1)}, bf16[32,1280]{1,0:T(8,128)(2,1)S(1)}, u32[]{:S(2)}, u32[]{:S(2)}) collective-permute-start(bf16[32,1280]{1,0:T(8,128)(2,1)S(1)} %pad_maximum_fusion.5.lead_in), channel_id=1, source_target_pairs={{0,8},{1,9},{2,10},{3,11},{4,12},{5,13},{6,14},{7,15},{8,0},{9,1},... | collective-permute-start | bytes 245768 | tf_op jit(solution)/shard_map/ppermute | solution.py:236
  42.7 6.3 %collective-permute-start.17 = (bf16[32,1536]{1,0:T(8,128)(2,1)S(1)}, bf16[32,1536]{1,0:T(8,128)(2,1)S(1)}, u32[]{:S(2)}, u32[]{:S(2)}) collective-permute-start(bf16[32,1536]{1,0:T(8,128)(2,1)S(1)} %behind.5.refs_0_), channel_id=1, source_target_pairs={{0,32},{1,33},{2,34},{3,35},{4,36},{5,37},{6,38},{7,39},{8,40},{9,... | collective-permute-start | bytes 294920 | tf_op jit(solution)/shard_map/ppermute | solution.py:236
  47.1 5.6 %collective-permute-start.15 = (bf16[32,1024]{1,0:T(8,128)(2,1)S(1)}, bf16[32,1024]{1,0:T(8,128)(2,1)S(1)}, u32[]{:S(2)}, u32[]{:S(2)}) collective-permute-start(bf16[32,1024]{1,0:T(8,128)(2,1)S(1)} %pad_maximum_fusion.7.lead_in), channel_id=1, source_target_pairs={{0,24},{1,25},{2,26},{3,27},{4,28},{5,29},{6,30},{7,31},{8,16},{9,... | collective-permute-start | bytes 196616 | tf_op jit(solution)/shard_map/ppermute | solution.py:236
  49.1 10.4 %collective-permute-start.21 = (bf16[32,1536]{1,0:T(8,128)(2,1)S(1)}, bf16[32,1536]{1,0:T(8,128)(2,1)S(1)}, u32[]{:S(2)}, u32[]{:S(2)}) collective-permute-start(bf16[32,1536]{1,0:T(8,128)(2,1)S(1)} %behind.6), channel_id=1, source_target_pairs={{0,64},{1,65},{2,66},{3,67},{4,68},{5,69},{6,70},{7,71},{8,72},{9,... | collective-permute-start | bytes 294920 | tf_op jit(solution)/shard_map/ppermute | solution.py:236
  52.5 7.0 %collective-permute-start.18 = (bf16[32,1024]{1,0:T(8,128)(2,1)S(1)}, bf16[32,1024]{1,0:T(8,128)(2,1)S(1)}, u32[]{:S(2)}, u32[]{:S(2)}) collective-permute-start(bf16[32,1024]{1,0:T(8,128)(2,1)S(1)} %pad_maximum_fusion.8.mine_in), channel_id=1, source_target_pairs={{0,4},{1,5},{2,6},{3,7},{4,0},{5,1},{6,2},{7,3},{8,12},{9,13},{10,... | collective-permute-start | bytes 196616 | tf_op jit(solution)/shard_map/ppermute | solution.py:236
  52.9 6.8 %collective-permute-start.20 = (bf16[32,768]{1,0:T(8,128)(2,1)S(1)}, bf16[32,768]{1,0:T(8,128)(2,1)S(1)}, u32[]{:S(2)}, u32[]{:S(2)}) collective-permute-start(bf16[32,768]{1,0:T(8,128)(2,1)S(1)} %pad_maximum_fusion.10.lead_in), channel_id=1, source_target_pairs={{0,96},{1,97},{2,98},{3,99},{4,100},{5,101},{6,102},{7,103},{8,104... | collective-permute-start | bytes 147464 | tf_op jit(solution)/shard_map/ppermute | solution.py:236
  54.9 5.0 %collective-permute-start.19 = (bf16[32,768]{1,0:T(8,128)(2,1)S(1)}, bf16[32,768]{1,0:T(8,128)(2,1)S(1)}, u32[]{:S(2)}, u32[]{:S(2)}) collective-permute-start(bf16[32,768]{1,0:T(8,128)(2,1)S(1)} %pad_maximum_fusion.10.lead_in), channel_id=1, source_target_pairs={{0,64},{1,65},{2,66},{3,67},{4,68},{5,69},{6,70},{7,71},{8,72},{9,... | collective-permute-start | bytes 147464 | tf_op jit(solution)/shard_map/ppermute | solution.py:236
  56.4 4.5 %collective-permute-start.16 = (bf16[32,768]{1,0:T(8,128)(2,1)S(1)}, bf16[32,768]{1,0:T(8,128)(2,1)S(1)}, u32[]{:S(2)}, u32[]{:S(2)}) collective-permute-start(bf16[32,768]{1,0:T(8,128)(2,1)S(1)} %pad_maximum_fusion.10.lead_in), channel_id=1, source_target_pairs={{0,32},{1,33},{2,34},{3,35},{4,36},{5,37},{6,38},{7,39},{8,40},{9,... | collective-permute-start | bytes 147464 | tf_op jit(solution)/shard_map/ppermute | solution.py:236
  59.6 1.5 %collective-permute-start.22 = (bf16[32,1536]{1,0:T(8,128)(2,1)S(1)}, bf16[32,1536]{1,0:T(8,128)(2,1)S(1)}, u32[]{:S(2)}, u32[]{:S(2)}) collective-permute-start(bf16[32,1536]{1,0:T(8,128)(2,1)S(1)} %get-tuple-element.46), channel_id=1, source_target_pairs={{0,4},{1,5},{2,6},{3,7},{4,0},{5,1},{6,2},{7,3},{8,12},{9,13},{10,... | collective-permute-start | bytes 294920 | tf_op jit(solution)/shard_map/ppermute | solution.py:236
  61.5 6.7 %collective-permute-start.23 = (bf16[32,256]{1,0:T(8,128)(2,1)S(1)}, bf16[32,256]{1,0:T(8,128)(2,1)S(1)}, u32[]{:S(2)}, u32[]{:S(2)}) collective-permute-start(bf16[32,256]{1,0:T(8,128)(2,1)S(1)} %pad_maximum_fusion.18), channel_id=1, source_target_pairs={{0,192},{1,193},{2,194},{3,195},{4,196},{5,197},{6,198},{7,199},{8... | collective-permute-start | bytes 49160 | tf_op jit(solution)/shard_map/ppermute | solution.py:236

commit v6 on v5

--- a/solution.py
+++ b/solution.py
@@ -57,7 +57,7 @@
 
 
 def summed_kernel(live, index, order, vec, rhs, coupling, left, right, *rest):
-    home, away, bits, tree, right_in, turned, order_in, fields, held, left_in, sems = rest
+    home, away, bits, order_in, fields, right_in, turned, held, left_in, sems = rest
     nvec, points = vec.shape
     small = [
         pltpu.make_async_copy(order, order_in, sems.at[0, LEVELS]),
@@ -71,23 +71,15 @@
     }
     kept = pl.ds(SUMMED, LEVELS - 1 - SUMMED)
     coupling_copy = pltpu.make_async_copy(coupling.at[kept], held.at[kept], sems.at[1, LEVELS])
-    for copy in small + [rights[LEVELS - 1]]:
-        copy.start()
+    rights[LEVELS - 1].start()
     coupling_copy.start()
     for level in range(LEVELS - 2, SUMMED - 1, -1):
         lefts[level].start()
         rights[level].start()
-    for level in range(SUMMED - 1, -1, -1):
-        rights[level].start()
+    for copy in small + rights[SUMMED - 1 :: -1]:
+        copy.start()
     levels = lax.broadcasted_iota(jnp.int32, bits.shape, 0)
     bits[...] = (lax.shift_right_logical(jnp.full(bits.shape, index[0], jnp.int32), levels) & 1).astype(F32)
-    for copy in small:
-        copy.wait()
-    chunk = 256
-    for low in range(0, points, chunk):
-        moved = dot(fields[...], one_hot(order_in[...], low, chunk))
-        slot = lax.broadcasted_iota(jnp.int32, moved.shape, 1) + low
-        tree[:, low : low + chunk] = jnp.where(slot < live[0], moved, 0.0).astype(BF)
 
     def turn(level):
         rights[level].wait()
@@ -113,8 +105,8 @@
         if low > SUMMED:
             turn(low)
             turn(low - 1)
-    for level in range(SUMMED, -1, -1):
-        rights[level].wait()
+    for copy in rights[SUMMED::-1] + small:
+        copy.wait()
 
 
 def own_kernel(live, index, coupling, left, right, turned, lead, update_0, update_1, held, left_in, low_turned, sems):
@@ -134,8 +126,14 @@
         out[...] = updates_of_level(gram, 0, level, canonical(held, index, level))
 
 
-def coefficient_kernel(tree, right, first_out, solve_out):
+def coefficient_kernel(live, order, fields, right, first_out, solve_out, tree):
     nvec = first_out.shape[0]
+    points = order.shape[1]
+    chunk = 256
+    for low in range(0, points, chunk):
+        moved = dot(fields[...], one_hot(order[...], low, chunk))
+        slot = lax.broadcasted_iota(jnp.int32, moved.shape, 1) + low
+        tree[:, low : low + chunk] = jnp.where(slot < live[0], moved, 0.0).astype(BF)
     for level in range(0, LEVELS, 2):
         pair = dot(tree[...], pair_of(right, level))
         for now in (level, level + 1):
@@ -302,16 +300,14 @@
         return [pick(1, even[i ^ 2], even[i]) for i in range(4)]
 
     summed = sum(LEVELS - 1 - level for level in range(SUMMED, LEVELS - 1))
-    home, away, bits, tree, right_in, turned = pl.pallas_call(
+    home, away, bits, order_in, fields, right_in, turned = pl.pallas_call(
         summed_kernel,
         out_shape=(pltpu.VMEM((LANE, summed * LANE), BF),) * 2
-        + (pltpu.VMEM((LEVELS, 2 * points), F32), pltpu.VMEM((2 * nvec, points), BF))
+        + (pltpu.VMEM((LEVELS, 2 * points), F32), pltpu.VMEM((1, points), jnp.int32), pltpu.VMEM((2 * nvec, points), BF))
         + (pltpu.VMEM(right_bases.shape, BF), pltpu.VMEM(((LEVELS - 1 - SUMMED) * LANE, points), BF)),
         in_specs=[SMEM, SMEM] + [HBM] * 6,
-        out_specs=(VMEM,) * 6,
+        out_specs=(VMEM,) * 7,
         scratch_shapes=[
-            pltpu.VMEM((1, points), jnp.int32),
-            pltpu.VMEM((2 * nvec, points), BF),
             pltpu.VMEM(coupling.shape, BF),
             pltpu.VMEM((LEVELS - 1 - SUMMED, points, LANE), BF),
             pltpu.SemaphoreType.DMA((2, LEVELS + 3)),
@@ -325,15 +321,19 @@
         *map(in_hbm, (tree_order, vectors, right_side, coupling, left_basis, right_bases)),
     )
     got = swap(away, 4)
-    first, coef = pl.pallas_call(
+    first, coef, tree = pl.pallas_call(
         coefficient_kernel,
-        out_shape=(pltpu.VMEM((nvec, 9 * LANE), BF), pltpu.VMEM((nvec, 7 * LANE), F32)),
-        in_specs=[VMEM, VMEM],
-        out_specs=(VMEM, VMEM),
+        out_shape=(
+            pltpu.VMEM((nvec, 9 * LANE), BF),
+            pltpu.VMEM((nvec, 7 * LANE), F32),
+            pltpu.VMEM((2 * nvec, points), BF),
+        ),
+        in_specs=[SMEM, VMEM, VMEM, VMEM],
+        out_specs=(VMEM,) * 3,
         compiler_params=params(12),
-        cost_estimate=pl.CostEstimate(flops=150_000_000, bytes_accessed=2_500_000, transcendentals=0),
+        cost_estimate=pl.CostEstimate(flops=300_000_000, bytes_accessed=2_500_000, transcendentals=0),
         name="coefficients",
-    )(tree, right_in)
+    )(live_counts, order_in, fields, right_in)
     halves = (home.astype(F32) + got.astype(F32)).astype(BF)
     piece = halves.shape[0] // 4
     rows_of = by_sub([halves[i * piece : (i + 1) * piece] for i in range(4)])

time: 69.7 us -> 69.3 us (level)
  transfers between devices with their start and end apart: 24 -> 24, of which waited for: 13 -> 13; matrix products, arithmetic and copies ran while one was open for 2% -> 2% of each run, Pallas kernels for 11% -> 12%
where the time goes in v6:
time: 69.3 us; the launch traced here: 68.9 us
  starting transfers between devices  34.1 us (49%)
  waiting for transfers between devices  16.9 us (24%)
  Pallas kernels  13.5 us (19%)
  between operations  1.87 us (3%)
  matrix products  1.27 us (2%)
  other arithmetic  1.07 us (2%)
    ppermute x24, starting transfers between devices, swap(): lax.ppermute(block, ('leaf', 'sub'), [(i, i ^ mask) for i in range(count)])  34.1 us
    ppermute x24, waiting for transfers between devices, swap(): lax.ppermute(block, ('leaf', 'sub'), [(i, i ^ mask) for i in range(count)])  16.9 us
    pallas_call x1, Pallas kernels, per_device(): pl.pallas_call(summed_kernel, out_shape=(pltpu.VMEM((LANE, summed * LANE)...  4.1 us
    pallas_call x1, Pallas kernels, per_device(): pl.pallas_call(own_kernel, out_shape=(pltpu.VMEM((2 * LANE, 7 * LANE), BF...  2.37 us
    pallas_call x1, Pallas kernels, per_device(): pl.pallas_call(partial_kernel, out_shape=(pltpu.VMEM((nvec, points), F32)...  1.73 us
    pallas_call x1, Pallas kernels, per_device(): pl.pallas_call(direct_kernel, out_shape=(pltpu.VMEM((nvec, points), F32),...  1.66 us
    pallas_call x1, Pallas kernels, per_device(): pl.pallas_call(moved_kernel, out_shape=pltpu.VMEM((points, (LEVELS - BEFO...  1.47 us
  transfers between devices with their start and end apart: 24, of which 13 were waited for; matrix products, arithmetic and copies ran while one was open for 2% of the time, Pallas kernels for 12%

profile of v6, /device:TPU:32, one launch (start us, length us, event | category | flops | bytes accessed | tf_op | source)
XLA Modules:
  0.0 68.9 jit_solution(16631335505600176107)
XLA Ops:
  1.3 4.1 %summed.1 = (bf16[128,1920]{1,0:T(8,128)(2,1)S(1)}, bf16[128,1920]{1,0:T(8,128)(2,1)S(1)}, f32[8,2048]{1,0:T(8,128)S(1)}, s32[1,1024]{1,0:T(1,128)S(1)}, bf16[64...) custom-call(s32[1]{0:T(128)S(6)} %copy.19.live, s32[1]{0:T(128)} %bitcast.index.index_in, ...), custom_call_target="tpu_custom_call" | custom-call | flops 1500000000 | bytes 5000000 | tf_op jit(solution)/shard_map/summed/pallas_call | solution.py:303
  5.5 0.9 %coefficients.1 = (bf16[32,1152]{1,0:T(8,128)(2,1)S(1)}, f32[32,896]{1,0:T(8,128)S(1)}, bf16[64,1024]{1,0:T(8,128)(2,1)S(1)}) custom-call(s32[1]{0:T(128)S(6)} %copy.19.live, s32[1,1024]{1,0:T(1,128)S(1)} %get-tuple-element.25.order, bf16[64,1024]{1,0:T(8,128)(2,1)S(1)} %get-tuple-element.26.fields, bf16[8,1024,128]{2,1,0:T(8,128)(2,1)S(1)} %get-tuple-element.27.right), custom_call_target="tpu_custom_call" | custom-call | flops 300000000 | bytes 2500000 | tf_op jit(solution)/shard_map/coefficients/pallas_call | solution.py:324
  6.4 0.9 %collective-permute-done = bf16[128,1920]{1,0:T(8,128)(2,1)S(1)} collective-permute-done((bf16[128,1920]{1,0:T(8,128)(2,1)S(1)}, bf16[128,1920]{1,0:T(8,128)(2,1)S(1)}, u32[]{:S(2)}, u32[]{:S(2)}) %collective-permute-start) | collective-permute-done | bytes 491552 | tf_op jit(solution)/shard_map/ppermute | solution.py:234
  7.6 1.7 %collective-permute-start.1 = (bf16[32,3072]{1,0:T(8,128)(2,1)S(1)}, bf16[32,3072]{1,0:T(8,128)(2,1)S(1)}, u32[]{:S(2)}, u32[]{:S(2)}) collective-permute-start(bf16[32,3072]{1,0:T(8,128)(2,1)S(1)} %pad_maximum_fusion.1.lead), channel_id=1, source_target_pairs={{0,1},{1,0},{2,3},{3,2},{4,5},{5,4},{6,7},{7,6},{8,9},{9,8},{10,11... | collective-permute-start | bytes 589832 | tf_op jit(solution)/shard_map/ppermute | solution.py:234
  9.3 3.0 %collective-permute-start.5 = (bf16[32,1920]{1,0:T(8,128)(2,1)S(1)}, bf16[32,1920]{1,0:T(8,128)(2,1)S(1)}, u32[]{:S(2)}, u32[]{:S(2)}) collective-permute-start(bf16[32,1920]{1,0:T(8,128)(2,1)S(1)} %get-tuple-element.66), channel_id=1, source_target_pairs={{0,2},{1,3},{2,0},{3,1},{4,6},{5,7},{6,4},{7,5},{8,10},{9,11},{10,... | collective-permute-start | bytes 368648 | tf_op jit(solution)/shard_map/ppermute | solution.py:234
  12.5 2.4 %own.1 = (bf16[256,896]{1,0:T(8,128)(2,1)S(1)}, bf16[256,768]{1,0:T(8,128)(2,1)S(1)}) custom-call(s32[1]{0:T(128)S(6)} %copy.19.live, s32[1]{0:T(128)} %bitcast.index.index_in, bf16[8,256,128]{2,1,0:T(8,128)(2,1)} %bitcast.24, bf16[8,1024,128]{2,1,0:T(8,128)(2,1)} %left.7, bf16[8,1024,128]{2,1,0:T(8,128)(2,1)S(1)} %get-tuple-element.27.right, ...), custom_call_target="tpu_custom_call" | custom-call | flops 1500000000 | bytes 1000000 | tf_op jit(solution)/shard_map/own/pallas_call | solution.py:344
  14.9 0.6 collective-permute-done.1
  15.7 3.3 %collective-permute-start.2 = (bf16[32,128]{1,0:T(8,128)(2,1)S(1)}, bf16[32,128]{1,0:T(8,128)(2,1)S(1)}, u32[]{:S(2)}, u32[]{:S(2)}) collective-permute-start(bf16[32,128]{1,0:T(8,128)(2,1)S(1)} %slice.776), channel_id=1, source_target_pairs={{0,2},{1,3},{2,0},{3,1},{4,6},{5,7},{6,4},{7,5},{8,10},{9,11},{10,... | collective-permute-start | bytes 24584 | tf_op jit(solution)/shard_map/ppermute | solution.py:234
  19.0 0.7 collective-permute-start.4
  20.1 1.0 %collective-permute-done.6 = bf16[32,1920]{1,0:T(8,128)(2,1)S(1)} collective-permute-done((bf16[32,1920]{1,0:T(8,128)(2,1)S(1)}, bf16[32,1920]{1,0:T(8,128)(2,1)S(1)}, u32[]{:S(2)}, u32[]{:S(2)}) %collective-permute-start.6) | collective-permute-done | bytes 122912 | tf_op jit(solution)/shard_map/ppermute | solution.py:234
  21.3 2.8 %collective-permute-start.9 = (bf16[32,768]{1,0:T(8,128)(2,1)S(1)}, bf16[32,768]{1,0:T(8,128)(2,1)S(1)}, u32[]{:S(2)}, u32[]{:S(2)}) collective-permute-start(bf16[32,768]{1,0:T(8,128)(2,1)S(1)} %behind.4), channel_id=1, source_target_pairs={{0,24},{1,25},{2,26},{3,27},{4,28},{5,29},{6,30},{7,31},{8,16},{9,... | collective-permute-start | bytes 147464 | tf_op jit(solution)/shard_map/ppermute | solution.py:234
  24.1 0.8 %collective-permute-start.8 = (bf16[32,768]{1,0:T(8,128)(2,1)S(1)}, bf16[32,768]{1,0:T(8,128)(2,1)S(1)}, u32[]{:S(2)}, u32[]{:S(2)}) collective-permute-start(bf16[32,768]{1,0:T(8,128)(2,1)S(1)} %behind.4), channel_id=1, source_target_pairs={{0,16},{1,17},{2,18},{3,19},{4,20},{5,21},{6,22},{7,23},{8,24},{9,... | collective-permute-start | bytes 147464 | tf_op jit(solution)/shard_map/ppermute | solution.py:234
  25.7 3.7 %collective-permute-done.7 = bf16[32,1280]{1,0:T(8,128)(2,1)S(1)} collective-permute-done((bf16[32,1280]{1,0:T(8,128)(2,1)S(1)}, bf16[32,1280]{1,0:T(8,128)(2,1)S(1)}, u32[]{:S(2)}, u32[]{:S(2)}) %collective-permute-start.7) | collective-permute-done | bytes 81952 | tf_op jit(solution)/shard_map/ppermute | solution.py:234
  29.8 2.0 %collective-permute-start.12 = (bf16[32,2688]{1,0:T(8,128)(2,1)S(1)}, bf16[32,2688]{1,0:T(8,128)(2,1)S(1)}, u32[]{:S(2)}, u32[]{:S(2)}) collective-permute-start(bf16[32,2688]{1,0:T(8,128)(2,1)S(1)} %pad_maximum_fusion.2.lead), channel_id=1, source_target_pairs={{0,3},{1,2},{2,1},{3,0},{4,7},{5,6},{6,5},{7,4},{8,11},{9,10},{10,... | collective-permute-start | bytes 516104 | tf_op jit(solution)/shard_map/ppermute | solution.py:234
  31.8 0.6 collective-permute-start.11
  32.4 1.6 %collective-permute-start.10 = (bf16[32,2688]{1,0:T(8,128)(2,1)S(1)}, bf16[32,2688]{1,0:T(8,128)(2,1)S(1)}, u32[]{:S(2)}, u32[]{:S(2)}) collective-permute-start(bf16[32,2688]{1,0:T(8,128)(2,1)S(1)} %pad_maximum_fusion.2.lead), channel_id=1, source_target_pairs={{0,1},{1,0},{2,3},{3,2},{4,5},{5,4},{6,7},{7,6},{8,9},{9,8},{10,11... | collective-permute-start | bytes 516104 | tf_op jit(solution)/shard_map/ppermute | solution.py:234
  34.0 1.7 %direct.1 = (f32[32,1024]{1,0:T(8,128)S(1)}, bf16[1024,1024]{1,0:T(8,128)(2,1)S(1)}) custom-call(s32[1,1024]{1,0:T(1,128)S(1)} %copy-done.3, bf16[64,1024]{1,0:T(8,128)(2,1)S(1)} %get-tuple-element.28.tree, bf16[1024,1024]{1,0:T(8,128)(2,1)S(1)} %copy-done.2, bf16[32,2688]{1,0:T(8,128)(2,1)S(1)} %pad_maximum_fusion.2.lead), custom_call_target="tpu_custom_call" | custom-call | flops 2000000000 | bytes 2000000 | tf_op jit(solution)/shard_map/direct/pallas_call | solution.py:385
  35.6 1.5 %moved.1 = bf16[1024,384]{1,0:T(8,128)(2,1)S(1)} custom-call(s32[1]{0:T(128)S(6)} %copy.19.live, bf16[1024,1024]{1,0:T(8,128)(2,1)S(1)} %get-tuple-element.37.hot, bf16[8,1024,128]{2,1,0:T(8,128)(2,1)S(1)} %copy-done), custom_call_target="tpu_custom_call" | custom-call | flops 1500000000 | bytes 2000000 | tf_op jit(solution)/shard_map/moved/pallas_call | solution.py:394
  37.1 1.6 %collective-permute-done.11 = bf16[32,2688]{1,0:T(8,128)(2,1)S(1)} collective-permute-done((bf16[32,2688]{1,0:T(8,128)(2,1)S(1)}, bf16[32,2688]{1,0:T(8,128)(2,1)S(1)}, u32[]{:S(2)}, u32[]{:S(2)}) %collective-permute-start.11) | collective-permute-done | bytes 172064 | tf_op jit(solution)/shard_map/ppermute | solution.py:234
  39.8 1.8 %collective-permute-done.13 = bf16[32,7680]{1,0:T(8,128)(2,1)S(1)} collective-permute-done((bf16[32,7680]{1,0:T(8,128)(2,1)S(1)}, bf16[32,7680]{1,0:T(8,128)(2,1)S(1)}, u32[]{:S(2)}, u32[]{:S(2)}) %collective-permute-start.13) | collective-permute-done | bytes 491552 | tf_op jit(solution)/shard_map/ppermute | solution.py:234
  42.3 0.8 %collective-permute-start.17 = (bf16[32,1536]{1,0:T(8,128)(2,1)S(1)}, bf16[32,1536]{1,0:T(8,128)(2,1)S(1)}, u32[]{:S(2)}, u32[]{:S(2)}) collective-permute-start(bf16[32,1536]{1,0:T(8,128)(2,1)S(1)} %behind.5.refs_0_), channel_id=1, source_target_pairs={{0,32},{1,33},{2,34},{3,35},{4,36},{5,37},{6,38},{7,39},{8,40},{9,... | collective-permute-start | bytes 294920 | tf_op jit(solution)/shard_map/ppermute | solution.py:234
  43.1 3.4 %collective-permute-done.14 = bf16[32,1280]{1,0:T(8,128)(2,1)S(1)} collective-permute-done((bf16[32,1280]{1,0:T(8,128)(2,1)S(1)}, bf16[32,1280]{1,0:T(8,128)(2,1)S(1)}, u32[]{:S(2)}, u32[]{:S(2)}) %collective-permute-start.14) | collective-permute-done | bytes 81952 | tf_op jit(solution)/shard_map/ppermute | solution.py:234
  46.8 1.9 %collective-permute-start.15 = (bf16[32,1024]{1,0:T(8,128)(2,1)S(1)}, bf16[32,1024]{1,0:T(8,128)(2,1)S(1)}, u32[]{:S(2)}, u32[]{:S(2)}) collective-permute-start(bf16[32,1024]{1,0:T(8,128)(2,1)S(1)} %pad_maximum_fusion.7.lead_in), channel_id=1, source_target_pairs={{0,24},{1,25},{2,26},{3,27},{4,28},{5,29},{6,30},{7,31},{8,16},{9,... | collective-permute-start | bytes 196616 | tf_op jit(solution)/shard_map/ppermute | solution.py:234
  48.7 3.3 %collective-permute-start.21 = (bf16[32,1536]{1,0:T(8,128)(2,1)S(1)}, bf16[32,1536]{1,0:T(8,128)(2,1)S(1)}, u32[]{:S(2)}, u32[]{:S(2)}) collective-permute-start(bf16[32,1536]{1,0:T(8,128)(2,1)S(1)} %behind.6), channel_id=1, source_target_pairs={{0,64},{1,65},{2,66},{3,67},{4,68},{5,69},{6,70},{7,71},{8,72},{9,... | collective-permute-start | bytes 294920 | tf_op jit(solution)/shard_map/ppermute | solution.py:234
  52.5 2.0 %collective-permute-start.20 = (bf16[32,768]{1,0:T(8,128)(2,1)S(1)}, bf16[32,768]{1,0:T(8,128)(2,1)S(1)}, u32[]{:S(2)}, u32[]{:S(2)}) collective-permute-start(bf16[32,768]{1,0:T(8,128)(2,1)S(1)} %pad_maximum_fusion.10.lead_in), channel_id=1, source_target_pairs={{0,96},{1,97},{2,98},{3,99},{4,100},{5,101},{6,102},{7,103},{8,104... | collective-permute-start | bytes 147464 | tf_op jit(solution)/shard_map/ppermute | solution.py:234
  54.5 1.5 %collective-permute-start.19 = (bf16[32,768]{1,0:T(8,128)(2,1)S(1)}, bf16[32,768]{1,0:T(8,128)(2,1)S(1)}, u32[]{:S(2)}, u32[]{:S(2)}) collective-permute-start(bf16[32,768]{1,0:T(8,128)(2,1)S(1)} %pad_maximum_fusion.10.lead_in), channel_id=1, source_target_pairs={{0,64},{1,65},{2,66},{3,67},{4,68},{5,69},{6,70},{7,71},{8,72},{9,... | collective-permute-start | bytes 147464 | tf_op jit(solution)/shard_map/ppermute | solution.py:234
  56.0 1.4 %collective-permute-start.16 = (bf16[32,768]{1,0:T(8,128)(2,1)S(1)}, bf16[32,768]{1,0:T(8,128)(2,1)S(1)}, u32[]{:S(2)}, u32[]{:S(2)}) collective-permute-start(bf16[32,768]{1,0:T(8,128)(2,1)S(1)} %pad_maximum_fusion.10.lead_in), channel_id=1, source_target_pairs={{0,32},{1,33},{2,34},{3,35},{4,36},{5,37},{6,38},{7,39},{8,40},{9,... | collective-permute-start | bytes 147464 | tf_op jit(solution)/shard_map/ppermute | solution.py:234
  57.3 1.7 %partial.1 = (f32[32,1024]{1,0:T(8,128)S(1)}, f32[32,1024]{1,0:T(8,128)S(1)}, bf16[768,128]{1,0:T(8,128)(2,1)S(1)}) custom-call(s32[1]{0:T(128)S(6)} %copy.19.live, s32[1]{0:T(128)} %bitcast.index.index_in, bf16[8,256,128]{2,1,0:T(8,128)(2,1)S(1)} %bitcast.25, bf16[8,1024,128]{2,1,0:T(8,128)(2,1)S(1)} %copy-done, ...), custom_call_target="tpu_custom_call" | custom-call | flops 2000000000 | bytes 3000000 | tf_op jit(solution)/shard_map/partial/pallas_call | solution.py:459
  59.5 1.0 %collective-permute-done.16 = bf16[32,768]{1,0:T(8,128)(2,1)S(1)} collective-permute-done((bf16[32,768]{1,0:T(8,128)(2,1)S(1)}, bf16[32,768]{1,0:T(8,128)(2,1)S(1)}, u32[]{:S(2)}, u32[]{:S(2)}) %collective-permute-start.16) | collective-permute-done | bytes 49184 | tf_op jit(solution)/shard_map/ppermute | solution.py:234
  61.1 5.0 %collective-permute-start.23 = (bf16[32,256]{1,0:T(8,128)(2,1)S(1)}, bf16[32,256]{1,0:T(8,128)(2,1)S(1)}, u32[]{:S(2)}, u32[]{:S(2)}) collective-permute-start(bf16[32,256]{1,0:T(8,128)(2,1)S(1)} %pad_maximum_fusion.18), channel_id=1, source_target_pairs={{0,192},{1,193},{2,194},{3,195},{4,196},{5,197},{6,198},{7,199},{8... | collective-permute-start | bytes 49160 | tf_op jit(solution)/shard_map/ppermute | solution.py:234
  66.1 1.7 %collective-permute-done.23 = bf16[32,256]{1,0:T(8,128)(2,1)S(1)} collective-permute-done((bf16[32,256]{1,0:T(8,128)(2,1)S(1)}, bf16[32,256]{1,0:T(8,128)(2,1)S(1)}, u32[]{:S(2)}, u32[]{:S(2)}) %collective-permute-start.23) | collective-permute-done | bytes 16416 | tf_op jit(solution)/shard_map/ppermute | solution.py:234
  67.8 1.1 %last.1 = (f32[32,1024]{1,0:T(8,128)}, f32[32,1024]{1,0:T(8,128)}) custom-call(bf16[768,128]{1,0:T(8,128)(2,1)S(1)} %get-tuple-element.41.coupling, bf16[1024,384]{1,0:T(8,128)(2,1)S(1)} %moved.1, f32[32,1024]{1,0:T(8,128)S(1)} %get-tuple-element.45.prod, f32[32,1024]{1,0:T(8,128)S(1)} %get-tuple-element.46.sol, ...), custom_call_target="tpu_custom_call" | custom-call | flops 30000000 | bytes 1000000 | tf_op jit(solution)/shard_map/last/pallas_call | solution.py:489
  (114 shorter events, 5.9 us)
Async XLA Ops:
  5.4 2.0 %collective-permute-start = (bf16[128,1920]{1,0:T(8,128)(2,1)S(1)}, bf16[128,1920]{1,0:T(8,128)(2,1)S(1)}, u32[]{:S(2)}, u32[]{:S(2)}) collective-permute-start(bf16[128,1920]{1,0:T(8,128)(2,1)S(1)} %get-tuple-element.33), channel_id=1, source_target_pairs={{0,4},{1,5},{2,6},{3,7},{4,0},{5,1},{6,2},{7,3},{8,12},{9,13},{10,... | collective-permute-start | bytes 1474568 | tf_op jit(solution)/shard_map/ppermute | solution.py:234
  7.6 7.8 %collective-permute-start.1 = (bf16[32,3072]{1,0:T(8,128)(2,1)S(1)}, bf16[32,3072]{1,0:T(8,128)(2,1)S(1)}, u32[]{:S(2)}, u32[]{:S(2)}) collective-permute-start(bf16[32,3072]{1,0:T(8,128)(2,1)S(1)} %pad_maximum_fusion.1.lead), channel_id=1, source_target_pairs={{0,1},{1,0},{2,3},{3,2},{4,5},{5,4},{6,7},{7,6},{8,9},{9,8},{10,11... | collective-permute-start | bytes 589832 | tf_op jit(solution)/shard_map/ppermute | solution.py:234
  9.3 10.9 %collective-permute-start.5 = (bf16[32,1920]{1,0:T(8,128)(2,1)S(1)}, bf16[32,1920]{1,0:T(8,128)(2,1)S(1)}, u32[]{:S(2)}, u32[]{:S(2)}) collective-permute-start(bf16[32,1920]{1,0:T(8,128)(2,1)S(1)} %get-tuple-element.66), channel_id=1, source_target_pairs={{0,2},{1,3},{2,0},{3,1},{4,6},{5,7},{6,4},{7,5},{8,10},{9,11},{10,... | collective-permute-start | bytes 368648 | tf_op jit(solution)/shard_map/ppermute | solution.py:234
  12.3 8.8 %collective-permute-start.6 = (bf16[32,1920]{1,0:T(8,128)(2,1)S(1)}, bf16[32,1920]{1,0:T(8,128)(2,1)S(1)}, u32[]{:S(2)}, u32[]{:S(2)}) collective-permute-start(bf16[32,1920]{1,0:T(8,128)(2,1)S(1)} %get-tuple-element.67), channel_id=1, source_target_pairs={{0,3},{1,2},{2,1},{3,0},{4,7},{5,6},{6,5},{7,4},{8,11},{9,10},{10,... | collective-permute-start | bytes 368648 | tf_op jit(solution)/shard_map/ppermute | solution.py:234
  15.4 18.5 %copy-start.2 = (bf16[1024,1024]{1,0:T(8,128)(2,1)S(1)}, bf16[1024,1024]{1,0:T(8,128)(2,1)}, u32[]{:S(2)}) copy-start(bf16[1024,1024]{1,0:T(8,128)(2,1)} %block.1) | copy-start | bytes 6291460
  15.4 18.5 %copy-start.3 = (s32[1,1024]{1,0:T(1,128)S(1)}, s32[1,1024]{1,0:T(1,128)}, u32[]{:S(2)}) copy-start(s32[1,1024]{1,0:T(1,128)} %order.3) | copy-start | bytes 12292
  15.7 9.3 %collective-permute-start.2 = (bf16[32,128]{1,0:T(8,128)(2,1)S(1)}, bf16[32,128]{1,0:T(8,128)(2,1)S(1)}, u32[]{:S(2)}, u32[]{:S(2)}) collective-permute-start(bf16[32,128]{1,0:T(8,128)(2,1)S(1)} %slice.776), channel_id=1, source_target_pairs={{0,2},{1,3},{2,0},{3,1},{4,6},{5,7},{6,4},{7,5},{8,10},{9,11},{10,... | collective-permute-start | bytes 24584 | tf_op jit(solution)/shard_map/ppermute | solution.py:234
  19.0 6.5 %collective-permute-start.4 = (bf16[32,128]{1,0:T(8,128)(2,1)S(1)}, bf16[32,128]{1,0:T(8,128)(2,1)S(1)}, u32[]{:S(2)}, u32[]{:S(2)}) collective-permute-start(bf16[32,128]{1,0:T(8,128)(2,1)S(1)} %slice.776), channel_id=1, source_target_pairs={{0,1},{1,0},{2,3},{3,2},{4,5},{5,4},{6,7},{7,6},{8,9},{9,8},{10,11... | collective-permute-start | bytes 24584 | tf_op jit(solution)/shard_map/ppermute | solution.py:234
  19.7 5.8 %collective-permute-start.3 = (bf16[32,1024]{1,0:T(8,128)(2,1)S(1)}, bf16[32,1024]{1,0:T(8,128)(2,1)S(1)}, u32[]{:S(2)}, u32[]{:S(2)}) collective-permute-start(bf16[32,1024]{1,0:T(8,128)(2,1)S(1)} %pad_maximum_fusion.6), channel_id=1, source_target_pairs={{0,3},{1,2},{2,1},{3,0},{4,7},{5,6},{6,5},{7,4},{8,11},{9,10},{10,... | collective-permute-start | bytes 196616 | tf_op jit(solution)/shard_map/ppermute | solution.py:234
  21.3 8.1 %collective-permute-start.9 = (bf16[32,768]{1,0:T(8,128)(2,1)S(1)}, bf16[32,768]{1,0:T(8,128)(2,1)S(1)}, u32[]{:S(2)}, u32[]{:S(2)}) collective-permute-start(bf16[32,768]{1,0:T(8,128)(2,1)S(1)} %behind.4), channel_id=1, source_target_pairs={{0,24},{1,25},{2,26},{3,27},{4,28},{5,29},{6,30},{7,31},{8,16},{9,... | collective-permute-start | bytes 147464 | tf_op jit(solution)/shard_map/ppermute | solution.py:234
  24.1 5.6 %collective-permute-start.8 = (bf16[32,768]{1,0:T(8,128)(2,1)S(1)}, bf16[32,768]{1,0:T(8,128)(2,1)S(1)}, u32[]{:S(2)}, u32[]{:S(2)}) collective-permute-start(bf16[32,768]{1,0:T(8,128)(2,1)S(1)} %behind.4), channel_id=1, source_target_pairs={{0,16},{1,17},{2,18},{3,19},{4,20},{5,21},{6,22},{7,23},{8,24},{9,... | collective-permute-start | bytes 147464 | tf_op jit(solution)/shard_map/ppermute | solution.py:234
  24.9 4.4 %collective-permute-start.7 = (bf16[32,1280]{1,0:T(8,128)(2,1)S(1)}, bf16[32,1280]{1,0:T(8,128)(2,1)S(1)}, u32[]{:S(2)}, u32[]{:S(2)}) collective-permute-start(bf16[32,1280]{1,0:T(8,128)(2,1)S(1)} %slice.496.lead_in), channel_id=1, source_target_pairs={{0,8},{1,9},{2,10},{3,11},{4,12},{5,13},{6,14},{7,15},{8,0},{9,1},... | collective-permute-start | bytes 245768 | tf_op jit(solution)/shard_map/ppermute | solution.py:234
  29.8 7.3 %collective-permute-start.12 = (bf16[32,2688]{1,0:T(8,128)(2,1)S(1)}, bf16[32,2688]{1,0:T(8,128)(2,1)S(1)}, u32[]{:S(2)}, u32[]{:S(2)}) collective-permute-start(bf16[32,2688]{1,0:T(8,128)(2,1)S(1)} %pad_maximum_fusion.2.lead), channel_id=1, source_target_pairs={{0,3},{1,2},{2,1},{3,0},{4,7},{5,6},{6,5},{7,4},{8,11},{9,10},{10,... | collective-permute-start | bytes 516104 | tf_op jit(solution)/shard_map/ppermute | solution.py:234
  31.8 6.9 %collective-permute-start.11 = (bf16[32,2688]{1,0:T(8,128)(2,1)S(1)}, bf16[32,2688]{1,0:T(8,128)(2,1)S(1)}, u32[]{:S(2)}, u32[]{:S(2)}) collective-permute-start(bf16[32,2688]{1,0:T(8,128)(2,1)S(1)} %pad_maximum_fusion.2.lead), channel_id=1, source_target_pairs={{0,2},{1,3},{2,0},{3,1},{4,6},{5,7},{6,4},{7,5},{8,10},{9,11},{10,... | collective-permute-start | bytes 516104 | tf_op jit(solution)/shard_map/ppermute | solution.py:234
  32.4 6.8 %collective-permute-start.10 = (bf16[32,2688]{1,0:T(8,128)(2,1)S(1)}, bf16[32,2688]{1,0:T(8,128)(2,1)S(1)}, u32[]{:S(2)}, u32[]{:S(2)}) collective-permute-start(bf16[32,2688]{1,0:T(8,128)(2,1)S(1)} %pad_maximum_fusion.2.lead), channel_id=1, source_target_pairs={{0,1},{1,0},{2,3},{3,2},{4,5},{5,4},{6,7},{7,6},{8,9},{9,8},{10,11... | collective-permute-start | bytes 516104 | tf_op jit(solution)/shard_map/ppermute | solution.py:234
  34.0 1.7 %copy-start = (bf16[8,1024,128]{2,1,0:T(8,128)(2,1)S(1)}, bf16[8,1024,128]{2,1,0:T(8,128)(2,1)}, u32[]{:S(2)}) copy-start(bf16[8,1024,128]{2,1,0:T(8,128)(2,1)} %left.7) | copy-start | bytes 6291460
  39.7 2.0 %collective-permute-start.13 = (bf16[32,7680]{1,0:T(8,128)(2,1)S(1)}, bf16[32,7680]{1,0:T(8,128)(2,1)S(1)}, u32[]{:S(2)}, u32[]{:S(2)}) collective-permute-start(bf16[32,7680]{1,0:T(8,128)(2,1)S(1)} %get-tuple-element.84), channel_id=1, source_target_pairs={{0,4},{1,5},{2,6},{3,7},{4,0},{5,1},{6,2},{7,3},{8,12},{9,13},{10,... | collective-permute-start | bytes 1474568 | tf_op jit(solution)/shard_map/ppermute | solution.py:234
  41.8 15.6 %copy-start.1 = (bf16[1,8,256,128]{3,2,1,0:T(8,128)(2,1)S(1)}, bf16[1,8,256,128]{3,2,1,0:T(8,128)(2,1)}, u32[]{:S(2)}) copy-start(bf16[1,8,256,128]{3,2,1,0:T(8,128)(2,1)} %param.15) | copy-start | bytes 1572868
  42.0 4.6 %collective-permute-start.14 = (bf16[32,1280]{1,0:T(8,128)(2,1)S(1)}, bf16[32,1280]{1,0:T(8,128)(2,1)S(1)}, u32[]{:S(2)}, u32[]{:S(2)}) collective-permute-start(bf16[32,1280]{1,0:T(8,128)(2,1)S(1)} %pad_maximum_fusion.5.lead_in), channel_id=1, source_target_pairs={{0,8},{1,9},{2,10},{3,11},{4,12},{5,13},{6,14},{7,15},{8,0},{9,1},... | collective-permute-start | bytes 245768 | tf_op jit(solution)/shard_map/ppermute | solution.py:234
  42.3 6.3 %collective-permute-start.17 = (bf16[32,1536]{1,0:T(8,128)(2,1)S(1)}, bf16[32,1536]{1,0:T(8,128)(2,1)S(1)}, u32[]{:S(2)}, u32[]{:S(2)}) collective-permute-start(bf16[32,1536]{1,0:T(8,128)(2,1)S(1)} %behind.5.refs_0_), channel_id=1, source_target_pairs={{0,32},{1,33},{2,34},{3,35},{4,36},{5,37},{6,38},{7,39},{8,40},{9,... | collective-permute-start | bytes 294920 | tf_op jit(solution)/shard_map/ppermute | solution.py:234
  46.8 5.6 %collective-permute-start.15 = (bf16[32,1024]{1,0:T(8,128)(2,1)S(1)}, bf16[32,1024]{1,0:T(8,128)(2,1)S(1)}, u32[]{:S(2)}, u32[]{:S(2)}) collective-permute-start(bf16[32,1024]{1,0:T(8,128)(2,1)S(1)} %pad_maximum_fusion.7.lead_in), channel_id=1, source_target_pairs={{0,24},{1,25},{2,26},{3,27},{4,28},{5,29},{6,30},{7,31},{8,16},{9,... | collective-permute-start | bytes 196616 | tf_op jit(solution)/shard_map/ppermute | solution.py:234
  48.7 10.4 %collective-permute-start.21 = (bf16[32,1536]{1,0:T(8,128)(2,1)S(1)}, bf16[32,1536]{1,0:T(8,128)(2,1)S(1)}, u32[]{:S(2)}, u32[]{:S(2)}) collective-permute-start(bf16[32,1536]{1,0:T(8,128)(2,1)S(1)} %behind.6), channel_id=1, source_target_pairs={{0,64},{1,65},{2,66},{3,67},{4,68},{5,69},{6,70},{7,71},{8,72},{9,... | collective-permute-start | bytes 294920 | tf_op jit(solution)/shard_map/ppermute | solution.py:234
  52.1 7.0 %collective-permute-start.18 = (bf16[32,1024]{1,0:T(8,128)(2,1)S(1)}, bf16[32,1024]{1,0:T(8,128)(2,1)S(1)}, u32[]{:S(2)}, u32[]{:S(2)}) collective-permute-start(bf16[32,1024]{1,0:T(8,128)(2,1)S(1)} %pad_maximum_fusion.8.mine_in), channel_id=1, source_target_pairs={{0,4},{1,5},{2,6},{3,7},{4,0},{5,1},{6,2},{7,3},{8,12},{9,13},{10,... | collective-permute-start | bytes 196616 | tf_op jit(solution)/shard_map/ppermute | solution.py:234
  52.5 6.8 %collective-permute-start.20 = (bf16[32,768]{1,0:T(8,128)(2,1)S(1)}, bf16[32,768]{1,0:T(8,128)(2,1)S(1)}, u32[]{:S(2)}, u32[]{:S(2)}) collective-permute-start(bf16[32,768]{1,0:T(8,128)(2,1)S(1)} %pad_maximum_fusion.10.lead_in), channel_id=1, source_target_pairs={{0,96},{1,97},{2,98},{3,99},{4,100},{5,101},{6,102},{7,103},{8,104... | collective-permute-start | bytes 147464 | tf_op jit(solution)/shard_map/ppermute | solution.py:234
  54.5 5.0 %collective-permute-start.19 = (bf16[32,768]{1,0:T(8,128)(2,1)S(1)}, bf16[32,768]{1,0:T(8,128)(2,1)S(1)}, u32[]{:S(2)}, u32[]{:S(2)}) collective-permute-start(bf16[32,768]{1,0:T(8,128)(2,1)S(1)} %pad_maximum_fusion.10.lead_in), channel_id=1, source_target_pairs={{0,64},{1,65},{2,66},{3,67},{4,68},{5,69},{6,70},{7,71},{8,72},{9,... | collective-permute-start | bytes 147464 | tf_op jit(solution)/shard_map/ppermute | solution.py:234
  56.0 4.5 %collective-permute-start.16 = (bf16[32,768]{1,0:T(8,128)(2,1)S(1)}, bf16[32,768]{1,0:T(8,128)(2,1)S(1)}, u32[]{:S(2)}, u32[]{:S(2)}) collective-permute-start(bf16[32,768]{1,0:T(8,128)(2,1)S(1)} %pad_maximum_fusion.10.lead_in), channel_id=1, source_target_pairs={{0,32},{1,33},{2,34},{3,35},{4,36},{5,37},{6,38},{7,39},{8,40},{9,... | collective-permute-start | bytes 147464 | tf_op jit(solution)/shard_map/ppermute | solution.py:234
  59.2 1.5 %collective-permute-start.22 = (bf16[32,1536]{1,0:T(8,128)(2,1)S(1)}, bf16[32,1536]{1,0:T(8,128)(2,1)S(1)}, u32[]{:S(2)}, u32[]{:S(2)}) collective-permute-start(bf16[32,1536]{1,0:T(8,128)(2,1)S(1)} %get-tuple-element.50), channel_id=1, source_target_pairs={{0,4},{1,5},{2,6},{3,7},{4,0},{5,1},{6,2},{7,3},{8,12},{9,13},{10,... | collective-permute-start | bytes 294920 | tf_op jit(solution)/shard_map/ppermute | solution.py:234
  61.1 6.7 %collective-permute-start.23 = (bf16[32,256]{1,0:T(8,128)(2,1)S(1)}, bf16[32,256]{1,0:T(8,128)(2,1)S(1)}, u32[]{:S(2)}, u32[]{:S(2)}) collective-permute-start(bf16[32,256]{1,0:T(8,128)(2,1)S(1)} %pad_maximum_fusion.18), channel_id=1, source_target_pairs={{0,192},{1,193},{2,194},{3,195},{4,196},{5,197},{6,198},{7,199},{8... | collective-permute-start | bytes 49160 | tf_op jit(solution)/shard_map/ppermute | solution.py:234

commit v7 on v6

--- a/solution.py
+++ b/solution.py
@@ -404,10 +404,10 @@
         cost_estimate=pl.CostEstimate(flops=1_500_000_000, bytes_accessed=2_000_000, transcendentals=0),
         name="moved",
     )(live_counts, hot, left_basis)
-    got = {mask: swap(sent, mask) for mask in (1, 2, 3)}
+    got = {mask: swap(sent, mask) for mask in (1, 3, 2)}
     got[0] = sent
     lead = LEVELS - SUMMED
-    total = sum(cols(got[mask], 0, lead).astype(F32) for mask in range(4))
+    total = sum(cols(got[mask], 0, lead).astype(F32) for mask in (0, 1, 3, 2))
     quarters = by_sub([cols(got[mask], lead) for mask in range(4)])
     total, moved, direct = lax.optimization_barrier((total, moved, direct))
 

time: 69.3 us -> 69 us (level)
  starting transfers between devices: 34.1 us -> 33.4 us
    ppermute x24, starting transfers between devices: 34.1 us -> 33.4 us  [swap(): lax.ppermute(block, ('leaf', 'sub'), [(i, i ^ mask) for i in range(count)])]
where the time goes in v7:
time: 69 us; the launch traced here: 68.6 us
  starting transfers between devices  33.4 us (48%)
  waiting for transfers between devices  17.3 us (25%)
  Pallas kernels  13.5 us (20%)
  between operations  1.86 us (3%)
  matrix products  1.27 us (2%)
  other arithmetic  1.07 us (2%)
    ppermute x24, starting transfers between devices, swap(): lax.ppermute(block, ('leaf', 'sub'), [(i, i ^ mask) for i in range(count)])  33.4 us
    ppermute x24, waiting for transfers between devices, swap(): lax.ppermute(block, ('leaf', 'sub'), [(i, i ^ mask) for i in range(count)])  17.3 us
    pallas_call x1, Pallas kernels, per_device(): pl.pallas_call(summed_kernel, out_shape=(pltpu.VMEM((LANE, summed * LANE)...  4.1 us
    pallas_call x1, Pallas kernels, per_device(): pl.pallas_call(own_kernel, out_shape=(pltpu.VMEM((2 * LANE, 7 * LANE), BF...  2.37 us
    pallas_call x1, Pallas kernels, per_device(): pl.pallas_call(partial_kernel, out_shape=(pltpu.VMEM((nvec, points), F32)...  1.73 us
    pallas_call x1, Pallas kernels, per_device(): pl.pallas_call(direct_kernel, out_shape=(pltpu.VMEM((nvec, points), F32),...  1.67 us
    pallas_call x1, Pallas kernels, per_device(): pl.pallas_call(moved_kernel, out_shape=pltpu.VMEM((points, (LEVELS - BEFO...  1.46 us
  transfers between devices with their start and end apart: 24, of which 13 were waited for; matrix products, arithmetic and copies ran while one was open for 2% of the time, Pallas kernels for 12%

profile of v7, /device:TPU:32, one launch (start us, length us, event | category | flops | bytes accessed | tf_op | source)
XLA Modules:
  0.0 68.6 jit_solution(4752932020645356243)
XLA Ops:
  1.3 4.1 %summed.1 = (bf16[128,1920]{1,0:T(8,128)(2,1)S(1)}, bf16[128,1920]{1,0:T(8,128)(2,1)S(1)}, f32[8,2048]{1,0:T(8,128)S(1)}, s32[1,1024]{1,0:T(1,128)S(1)}, bf16[64...) custom-call(s32[1]{0:T(128)S(6)} %copy.19.live, s32[1]{0:T(128)} %bitcast.index.index_in, ...), custom_call_target="tpu_custom_call" | custom-call | flops 1500000000 | bytes 5000000 | tf_op jit(solution)/shard_map/summed/pallas_call | solution.py:303
  5.5 0.9 %coefficients.1 = (bf16[32,1152]{1,0:T(8,128)(2,1)S(1)}, f32[32,896]{1,0:T(8,128)S(1)}, bf16[64,1024]{1,0:T(8,128)(2,1)S(1)}) custom-call(s32[1]{0:T(128)S(6)} %copy.19.live, s32[1,1024]{1,0:T(1,128)S(1)} %get-tuple-element.25.order, bf16[64,1024]{1,0:T(8,128)(2,1)S(1)} %get-tuple-element.26.fields, bf16[8,1024,128]{2,1,0:T(8,128)(2,1)S(1)} %get-tuple-element.27.right), custom_call_target="tpu_custom_call" | custom-call | flops 300000000 | bytes 2500000 | tf_op jit(solution)/shard_map/coefficients/pallas_call | solution.py:324
  6.4 0.9 %collective-permute-done = bf16[128,1920]{1,0:T(8,128)(2,1)S(1)} collective-permute-done((bf16[128,1920]{1,0:T(8,128)(2,1)S(1)}, bf16[128,1920]{1,0:T(8,128)(2,1)S(1)}, u32[]{:S(2)}, u32[]{:S(2)}) %collective-permute-start) | collective-permute-done | bytes 491552 | tf_op jit(solution)/shard_map/ppermute | solution.py:234
  7.6 1.7 %collective-permute-start.1 = (bf16[32,3072]{1,0:T(8,128)(2,1)S(1)}, bf16[32,3072]{1,0:T(8,128)(2,1)S(1)}, u32[]{:S(2)}, u32[]{:S(2)}) collective-permute-start(bf16[32,3072]{1,0:T(8,128)(2,1)S(1)} %pad_maximum_fusion.1.lead), channel_id=1, source_target_pairs={{0,1},{1,0},{2,3},{3,2},{4,5},{5,4},{6,7},{7,6},{8,9},{9,8},{10,11... | collective-permute-start | bytes 589832 | tf_op jit(solution)/shard_map/ppermute | solution.py:234
  9.3 3.0 %collective-permute-start.5 = (bf16[32,1920]{1,0:T(8,128)(2,1)S(1)}, bf16[32,1920]{1,0:T(8,128)(2,1)S(1)}, u32[]{:S(2)}, u32[]{:S(2)}) collective-permute-start(bf16[32,1920]{1,0:T(8,128)(2,1)S(1)} %get-tuple-element.66), channel_id=1, source_target_pairs={{0,2},{1,3},{2,0},{3,1},{4,6},{5,7},{6,4},{7,5},{8,10},{9,11},{10,... | collective-permute-start | bytes 368648 | tf_op jit(solution)/shard_map/ppermute | solution.py:234
  12.5 2.4 %own.1 = (bf16[256,896]{1,0:T(8,128)(2,1)S(1)}, bf16[256,768]{1,0:T(8,128)(2,1)S(1)}) custom-call(s32[1]{0:T(128)S(6)} %copy.19.live, s32[1]{0:T(128)} %bitcast.index.index_in, bf16[8,256,128]{2,1,0:T(8,128)(2,1)} %bitcast.24, bf16[8,1024,128]{2,1,0:T(8,128)(2,1)} %left.7, bf16[8,1024,128]{2,1,0:T(8,128)(2,1)S(1)} %get-tuple-element.27.right, ...), custom_call_target="tpu_custom_call" | custom-call | flops 1500000000 | bytes 1000000 | tf_op jit(solution)/shard_map/own/pallas_call | solution.py:344
  14.9 0.6 collective-permute-done.1
  15.7 3.3 %collective-permute-start.2 = (bf16[32,128]{1,0:T(8,128)(2,1)S(1)}, bf16[32,128]{1,0:T(8,128)(2,1)S(1)}, u32[]{:S(2)}, u32[]{:S(2)}) collective-permute-start(bf16[32,128]{1,0:T(8,128)(2,1)S(1)} %slice.776), channel_id=1, source_target_pairs={{0,2},{1,3},{2,0},{3,1},{4,6},{5,7},{6,4},{7,5},{8,10},{9,11},{10,... | collective-permute-start | bytes 24584 | tf_op jit(solution)/shard_map/ppermute | solution.py:234
  19.0 0.7 collective-permute-start.4
  20.1 1.0 %collective-permute-done.6 = bf16[32,1920]{1,0:T(8,128)(2,1)S(1)} collective-permute-done((bf16[32,1920]{1,0:T(8,128)(2,1)S(1)}, bf16[32,1920]{1,0:T(8,128)(2,1)S(1)}, u32[]{:S(2)}, u32[]{:S(2)}) %collective-permute-start.6) | collective-permute-done | bytes 122912 | tf_op jit(solution)/shard_map/ppermute | solution.py:234
  21.3 2.8 %collective-permute-start.9 = (bf16[32,768]{1,0:T(8,128)(2,1)S(1)}, bf16[32,768]{1,0:T(8,128)(2,1)S(1)}, u32[]{:S(2)}, u32[]{:S(2)}) collective-permute-start(bf16[32,768]{1,0:T(8,128)(2,1)S(1)} %behind.4), channel_id=1, source_target_pairs={{0,24},{1,25},{2,26},{3,27},{4,28},{5,29},{6,30},{7,31},{8,16},{9,... | collective-permute-start | bytes 147464 | tf_op jit(solution)/shard_map/ppermute | solution.py:234
  24.1 0.8 %collective-permute-start.8 = (bf16[32,768]{1,0:T(8,128)(2,1)S(1)}, bf16[32,768]{1,0:T(8,128)(2,1)S(1)}, u32[]{:S(2)}, u32[]{:S(2)}) collective-permute-start(bf16[32,768]{1,0:T(8,128)(2,1)S(1)} %behind.4), channel_id=1, source_target_pairs={{0,16},{1,17},{2,18},{3,19},{4,20},{5,21},{6,22},{7,23},{8,24},{9,... | collective-permute-start | bytes 147464 | tf_op jit(solution)/shard_map/ppermute | solution.py:234
  25.7 3.7 %collective-permute-done.7 = bf16[32,1280]{1,0:T(8,128)(2,1)S(1)} collective-permute-done((bf16[32,1280]{1,0:T(8,128)(2,1)S(1)}, bf16[32,1280]{1,0:T(8,128)(2,1)S(1)}, u32[]{:S(2)}, u32[]{:S(2)}) %collective-permute-start.7) | collective-permute-done | bytes 81952 | tf_op jit(solution)/shard_map/ppermute | solution.py:234
  29.8 2.2 %collective-permute-start.12 = (bf16[32,2688]{1,0:T(8,128)(2,1)S(1)}, bf16[32,2688]{1,0:T(8,128)(2,1)S(1)}, u32[]{:S(2)}, u32[]{:S(2)}) collective-permute-start(bf16[32,2688]{1,0:T(8,128)(2,1)S(1)} %pad_maximum_fusion.2.lead), channel_id=1, source_target_pairs={{0,2},{1,3},{2,0},{3,1},{4,6},{5,7},{6,4},{7,5},{8,10},{9,11},{10,... | collective-permute-start | bytes 516104 | tf_op jit(solution)/shard_map/ppermute | solution.py:234
  32.0 1.1 %collective-permute-start.11 = (bf16[32,2688]{1,0:T(8,128)(2,1)S(1)}, bf16[32,2688]{1,0:T(8,128)(2,1)S(1)}, u32[]{:S(2)}, u32[]{:S(2)}) collective-permute-start(bf16[32,2688]{1,0:T(8,128)(2,1)S(1)} %pad_maximum_fusion.2.lead), channel_id=1, source_target_pairs={{0,3},{1,2},{2,1},{3,0},{4,7},{5,6},{6,5},{7,4},{8,11},{9,10},{10,... | collective-permute-start | bytes 516104 | tf_op jit(solution)/shard_map/ppermute | solution.py:234
  33.4 1.7 %direct.1 = (f32[32,1024]{1,0:T(8,128)S(1)}, bf16[1024,1024]{1,0:T(8,128)(2,1)S(1)}) custom-call(s32[1,1024]{1,0:T(1,128)S(1)} %copy-done.3, bf16[64,1024]{1,0:T(8,128)(2,1)S(1)} %get-tuple-element.28.tree, bf16[1024,1024]{1,0:T(8,128)(2,1)S(1)} %copy-done.2, bf16[32,2688]{1,0:T(8,128)(2,1)S(1)} %pad_maximum_fusion.2.lead), custom_call_target="tpu_custom_call" | custom-call | flops 2000000000 | bytes 2000000 | tf_op jit(solution)/shard_map/direct/pallas_call | solution.py:385
  35.0 1.5 %moved.1 = bf16[1024,384]{1,0:T(8,128)(2,1)S(1)} custom-call(s32[1]{0:T(128)S(6)} %copy.19.live, bf16[1024,1024]{1,0:T(8,128)(2,1)S(1)} %get-tuple-element.37.hot, bf16[8,1024,128]{2,1,0:T(8,128)(2,1)S(1)} %copy-done), custom_call_target="tpu_custom_call" | custom-call | flops 1500000000 | bytes 2000000 | tf_op jit(solution)/shard_map/moved/pallas_call | solution.py:394
  36.5 0.6 collective-permute-done.12
  37.1 1.8 %collective-permute-done.11 = bf16[32,2688]{1,0:T(8,128)(2,1)S(1)} collective-permute-done((bf16[32,2688]{1,0:T(8,128)(2,1)S(1)}, bf16[32,2688]{1,0:T(8,128)(2,1)S(1)}, u32[]{:S(2)}, u32[]{:S(2)}) %collective-permute-start.11) | collective-permute-done | bytes 172064 | tf_op jit(solution)/shard_map/ppermute | solution.py:234
  39.5 1.8 %collective-permute-done.13 = bf16[32,7680]{1,0:T(8,128)(2,1)S(1)} collective-permute-done((bf16[32,7680]{1,0:T(8,128)(2,1)S(1)}, bf16[32,7680]{1,0:T(8,128)(2,1)S(1)}, u32[]{:S(2)}, u32[]{:S(2)}) %collective-permute-start.13) | collective-permute-done | bytes 491552 | tf_op jit(solution)/shard_map/ppermute | solution.py:234
  42.0 0.6 collective-permute-start.17
  42.6 3.7 %collective-permute-done.14 = bf16[32,1280]{1,0:T(8,128)(2,1)S(1)} collective-permute-done((bf16[32,1280]{1,0:T(8,128)(2,1)S(1)}, bf16[32,1280]{1,0:T(8,128)(2,1)S(1)}, u32[]{:S(2)}, u32[]{:S(2)}) %collective-permute-start.14) | collective-permute-done | bytes 81952 | tf_op jit(solution)/shard_map/ppermute | solution.py:234
  46.4 1.9 %collective-permute-start.15 = (bf16[32,1024]{1,0:T(8,128)(2,1)S(1)}, bf16[32,1024]{1,0:T(8,128)(2,1)S(1)}, u32[]{:S(2)}, u32[]{:S(2)}) collective-permute-start(bf16[32,1024]{1,0:T(8,128)(2,1)S(1)} %pad_maximum_fusion.7.lead_in), channel_id=1, source_target_pairs={{0,24},{1,25},{2,26},{3,27},{4,28},{5,29},{6,30},{7,31},{8,16},{9,... | collective-permute-start | bytes 196616 | tf_op jit(solution)/shard_map/ppermute | solution.py:234
  48.4 3.3 %collective-permute-start.21 = (bf16[32,1536]{1,0:T(8,128)(2,1)S(1)}, bf16[32,1536]{1,0:T(8,128)(2,1)S(1)}, u32[]{:S(2)}, u32[]{:S(2)}) collective-permute-start(bf16[32,1536]{1,0:T(8,128)(2,1)S(1)} %behind.6), channel_id=1, source_target_pairs={{0,64},{1,65},{2,66},{3,67},{4,68},{5,69},{6,70},{7,71},{8,72},{9,... | collective-permute-start | bytes 294920 | tf_op jit(solution)/shard_map/ppermute | solution.py:234
  52.2 2.0 %collective-permute-start.20 = (bf16[32,768]{1,0:T(8,128)(2,1)S(1)}, bf16[32,768]{1,0:T(8,128)(2,1)S(1)}, u32[]{:S(2)}, u32[]{:S(2)}) collective-permute-start(bf16[32,768]{1,0:T(8,128)(2,1)S(1)} %pad_maximum_fusion.10.lead_in), channel_id=1, source_target_pairs={{0,96},{1,97},{2,98},{3,99},{4,100},{5,101},{6,102},{7,103},{8,104... | collective-permute-start | bytes 147464 | tf_op jit(solution)/shard_map/ppermute | solution.py:234
  54.2 1.5 %collective-permute-start.19 = (bf16[32,768]{1,0:T(8,128)(2,1)S(1)}, bf16[32,768]{1,0:T(8,128)(2,1)S(1)}, u32[]{:S(2)}, u32[]{:S(2)}) collective-permute-start(bf16[32,768]{1,0:T(8,128)(2,1)S(1)} %pad_maximum_fusion.10.lead_in), channel_id=1, source_target_pairs={{0,64},{1,65},{2,66},{3,67},{4,68},{5,69},{6,70},{7,71},{8,72},{9,... | collective-permute-start | bytes 147464 | tf_op jit(solution)/shard_map/ppermute | solution.py:234
  55.6 1.4 %collective-permute-start.16 = (bf16[32,768]{1,0:T(8,128)(2,1)S(1)}, bf16[32,768]{1,0:T(8,128)(2,1)S(1)}, u32[]{:S(2)}, u32[]{:S(2)}) collective-permute-start(bf16[32,768]{1,0:T(8,128)(2,1)S(1)} %pad_maximum_fusion.10.lead_in), channel_id=1, source_target_pairs={{0,32},{1,33},{2,34},{3,35},{4,36},{5,37},{6,38},{7,39},{8,40},{9,... | collective-permute-start | bytes 147464 | tf_op jit(solution)/shard_map/ppermute | solution.py:234
  57.0 1.7 %partial.1 = (f32[32,1024]{1,0:T(8,128)S(1)}, f32[32,1024]{1,0:T(8,128)S(1)}, bf16[768,128]{1,0:T(8,128)(2,1)S(1)}) custom-call(s32[1]{0:T(128)S(6)} %copy.19.live, s32[1]{0:T(128)} %bitcast.index.index_in, bf16[8,256,128]{2,1,0:T(8,128)(2,1)S(1)} %bitcast.25, bf16[8,1024,128]{2,1,0:T(8,128)(2,1)S(1)} %copy-done, ...), custom_call_target="tpu_custom_call" | custom-call | flops 2000000000 | bytes 3000000 | tf_op jit(solution)/shard_map/partial/pallas_call | solution.py:459
  59.2 1.0 %collective-permute-done.16 = bf16[32,768]{1,0:T(8,128)(2,1)S(1)} collective-permute-done((bf16[32,768]{1,0:T(8,128)(2,1)S(1)}, bf16[32,768]{1,0:T(8,128)(2,1)S(1)}, u32[]{:S(2)}, u32[]{:S(2)}) %collective-permute-start.16) | collective-permute-done | bytes 49184 | tf_op jit(solution)/shard_map/ppermute | solution.py:234
  60.7 5.0 %collective-permute-start.23 = (bf16[32,256]{1,0:T(8,128)(2,1)S(1)}, bf16[32,256]{1,0:T(8,128)(2,1)S(1)}, u32[]{:S(2)}, u32[]{:S(2)}) collective-permute-start(bf16[32,256]{1,0:T(8,128)(2,1)S(1)} %pad_maximum_fusion.18), channel_id=1, source_target_pairs={{0,192},{1,193},{2,194},{3,195},{4,196},{5,197},{6,198},{7,199},{8... | collective-permute-start | bytes 49160 | tf_op jit(solution)/shard_map/ppermute | solution.py:234
  65.8 1.7 %collective-permute-done.23 = bf16[32,256]{1,0:T(8,128)(2,1)S(1)} collective-permute-done((bf16[32,256]{1,0:T(8,128)(2,1)S(1)}, bf16[32,256]{1,0:T(8,128)(2,1)S(1)}, u32[]{:S(2)}, u32[]{:S(2)}) %collective-permute-start.23) | collective-permute-done | bytes 16416 | tf_op jit(solution)/shard_map/ppermute | solution.py:234
  67.5 1.1 %last.1 = (f32[32,1024]{1,0:T(8,128)}, f32[32,1024]{1,0:T(8,128)}) custom-call(bf16[768,128]{1,0:T(8,128)(2,1)S(1)} %get-tuple-element.41.coupling, bf16[1024,384]{1,0:T(8,128)(2,1)S(1)} %moved.1, f32[32,1024]{1,0:T(8,128)S(1)} %get-tuple-element.45.prod, f32[32,1024]{1,0:T(8,128)S(1)} %get-tuple-element.46.sol, ...), custom_call_target="tpu_custom_call" | custom-call | flops 30000000 | bytes 1000000 | tf_op jit(solution)/shard_map/last/pallas_call | solution.py:489
  (114 shorter events, 5.6 us)
Async XLA Ops:
  5.4 2.0 %collective-permute-start = (bf16[128,1920]{1,0:T(8,128)(2,1)S(1)}, bf16[128,1920]{1,0:T(8,128)(2,1)S(1)}, u32[]{:S(2)}, u32[]{:S(2)}) collective-permute-start(bf16[128,1920]{1,0:T(8,128)(2,1)S(1)} %get-tuple-element.33), channel_id=1, source_target_pairs={{0,4},{1,5},{2,6},{3,7},{4,0},{5,1},{6,2},{7,3},{8,12},{9,13},{10,... | collective-permute-start | bytes 1474568 | tf_op jit(solution)/shard_map/ppermute | solution.py:234
  7.6 7.8 %collective-permute-start.1 = (bf16[32,3072]{1,0:T(8,128)(2,1)S(1)}, bf16[32,3072]{1,0:T(8,128)(2,1)S(1)}, u32[]{:S(2)}, u32[]{:S(2)}) collective-permute-start(bf16[32,3072]{1,0:T(8,128)(2,1)S(1)} %pad_maximum_fusion.1.lead), channel_id=1, source_target_pairs={{0,1},{1,0},{2,3},{3,2},{4,5},{5,4},{6,7},{7,6},{8,9},{9,8},{10,11... | collective-permute-start | bytes 589832 | tf_op jit(solution)/shard_map/ppermute | solution.py:234
  9.3 10.9 %collective-permute-start.5 = (bf16[32,1920]{1,0:T(8,128)(2,1)S(1)}, bf16[32,1920]{1,0:T(8,128)(2,1)S(1)}, u32[]{:S(2)}, u32[]{:S(2)}) collective-permute-start(bf16[32,1920]{1,0:T(8,128)(2,1)S(1)} %get-tuple-element.66), channel_id=1, source_target_pairs={{0,2},{1,3},{2,0},{3,1},{4,6},{5,7},{6,4},{7,5},{8,10},{9,11},{10,... | collective-permute-start | bytes 368648 | tf_op jit(solution)/shard_map/ppermute | solution.py:234
  12.3 8.8 %collective-permute-start.6 = (bf16[32,1920]{1,0:T(8,128)(2,1)S(1)}, bf16[32,1920]{1,0:T(8,128)(2,1)S(1)}, u32[]{:S(2)}, u32[]{:S(2)}) collective-permute-start(bf16[32,1920]{1,0:T(8,128)(2,1)S(1)} %get-tuple-element.67), channel_id=1, source_target_pairs={{0,3},{1,2},{2,1},{3,0},{4,7},{5,6},{6,5},{7,4},{8,11},{9,10},{10,... | collective-permute-start | bytes 368648 | tf_op jit(solution)/shard_map/ppermute | solution.py:234
  15.4 17.9 %copy-start.2 = (bf16[1024,1024]{1,0:T(8,128)(2,1)S(1)}, bf16[1024,1024]{1,0:T(8,128)(2,1)}, u32[]{:S(2)}) copy-start(bf16[1024,1024]{1,0:T(8,128)(2,1)} %block.1) | copy-start | bytes 6291460
  15.4 17.9 %copy-start.3 = (s32[1,1024]{1,0:T(1,128)S(1)}, s32[1,1024]{1,0:T(1,128)}, u32[]{:S(2)}) copy-start(s32[1,1024]{1,0:T(1,128)} %order.3) | copy-start | bytes 12292
  15.7 9.3 %collective-permute-start.2 = (bf16[32,128]{1,0:T(8,128)(2,1)S(1)}, bf16[32,128]{1,0:T(8,128)(2,1)S(1)}, u32[]{:S(2)}, u32[]{:S(2)}) collective-permute-start(bf16[32,128]{1,0:T(8,128)(2,1)S(1)} %slice.776), channel_id=1, source_target_pairs={{0,2},{1,3},{2,0},{3,1},{4,6},{5,7},{6,4},{7,5},{8,10},{9,11},{10,... | collective-permute-start | bytes 24584 | tf_op jit(solution)/shard_map/ppermute | solution.py:234
  19.0 6.5 %collective-permute-start.4 = (bf16[32,128]{1,0:T(8,128)(2,1)S(1)}, bf16[32,128]{1,0:T(8,128)(2,1)S(1)}, u32[]{:S(2)}, u32[]{:S(2)}) collective-permute-start(bf16[32,128]{1,0:T(8,128)(2,1)S(1)} %slice.776), channel_id=1, source_target_pairs={{0,1},{1,0},{2,3},{3,2},{4,5},{5,4},{6,7},{7,6},{8,9},{9,8},{10,11... | collective-permute-start | bytes 24584 | tf_op jit(solution)/shard_map/ppermute | solution.py:234
  19.7 5.8 %collective-permute-start.3 = (bf16[32,1024]{1,0:T(8,128)(2,1)S(1)}, bf16[32,1024]{1,0:T(8,128)(2,1)S(1)}, u32[]{:S(2)}, u32[]{:S(2)}) collective-permute-start(bf16[32,1024]{1,0:T(8,128)(2,1)S(1)} %pad_maximum_fusion.6), channel_id=1, source_target_pairs={{0,3},{1,2},{2,1},{3,0},{4,7},{5,6},{6,5},{7,4},{8,11},{9,10},{10,... | collective-permute-start | bytes 196616 | tf_op jit(solution)/shard_map/ppermute | solution.py:234
  21.3 8.1 %collective-permute-start.9 = (bf16[32,768]{1,0:T(8,128)(2,1)S(1)}, bf16[32,768]{1,0:T(8,128)(2,1)S(1)}, u32[]{:S(2)}, u32[]{:S(2)}) collective-permute-start(bf16[32,768]{1,0:T(8,128)(2,1)S(1)} %behind.4), channel_id=1, source_target_pairs={{0,24},{1,25},{2,26},{3,27},{4,28},{5,29},{6,30},{7,31},{8,16},{9,... | collective-permute-start | bytes 147464 | tf_op jit(solution)/shard_map/ppermute | solution.py:234
  24.1 5.6 %collective-permute-start.8 = (bf16[32,768]{1,0:T(8,128)(2,1)S(1)}, bf16[32,768]{1,0:T(8,128)(2,1)S(1)}, u32[]{:S(2)}, u32[]{:S(2)}) collective-permute-start(bf16[32,768]{1,0:T(8,128)(2,1)S(1)} %behind.4), channel_id=1, source_target_pairs={{0,16},{1,17},{2,18},{3,19},{4,20},{5,21},{6,22},{7,23},{8,24},{9,... | collective-permute-start | bytes 147464 | tf_op jit(solution)/shard_map/ppermute | solution.py:234
  24.9 4.4 %collective-permute-start.7 = (bf16[32,1280]{1,0:T(8,128)(2,1)S(1)}, bf16[32,1280]{1,0:T(8,128)(2,1)S(1)}, u32[]{:S(2)}, u32[]{:S(2)}) collective-permute-start(bf16[32,1280]{1,0:T(8,128)(2,1)S(1)} %slice.496.lead_in), channel_id=1, source_target_pairs={{0,8},{1,9},{2,10},{3,11},{4,12},{5,13},{6,14},{7,15},{8,0},{9,1},... | collective-permute-start | bytes 245768 | tf_op jit(solution)/shard_map/ppermute | solution.py:234
  29.8 7.3 %collective-permute-start.12 = (bf16[32,2688]{1,0:T(8,128)(2,1)S(1)}, bf16[32,2688]{1,0:T(8,128)(2,1)S(1)}, u32[]{:S(2)}, u32[]{:S(2)}) collective-permute-start(bf16[32,2688]{1,0:T(8,128)(2,1)S(1)} %pad_maximum_fusion.2.lead), channel_id=1, source_target_pairs={{0,2},{1,3},{2,0},{3,1},{4,6},{5,7},{6,4},{7,5},{8,10},{9,11},{10,... | collective-permute-start | bytes 516104 | tf_op jit(solution)/shard_map/ppermute | solution.py:234
  32.0 6.9 %collective-permute-start.11 = (bf16[32,2688]{1,0:T(8,128)(2,1)S(1)}, bf16[32,2688]{1,0:T(8,128)(2,1)S(1)}, u32[]{:S(2)}, u32[]{:S(2)}) collective-permute-start(bf16[32,2688]{1,0:T(8,128)(2,1)S(1)} %pad_maximum_fusion.2.lead), channel_id=1, source_target_pairs={{0,3},{1,2},{2,1},{3,0},{4,7},{5,6},{6,5},{7,4},{8,11},{9,10},{10,... | collective-permute-start | bytes 516104 | tf_op jit(solution)/shard_map/ppermute | solution.py:234
  33.0 5.9 %collective-permute-start.10 = (bf16[32,2688]{1,0:T(8,128)(2,1)S(1)}, bf16[32,2688]{1,0:T(8,128)(2,1)S(1)}, u32[]{:S(2)}, u32[]{:S(2)}) collective-permute-start(bf16[32,2688]{1,0:T(8,128)(2,1)S(1)} %pad_maximum_fusion.2.lead), channel_id=1, source_target_pairs={{0,1},{1,0},{2,3},{3,2},{4,5},{5,4},{6,7},{7,6},{8,9},{9,8},{10,11... | collective-permute-start | bytes 516104 | tf_op jit(solution)/shard_map/ppermute | solution.py:234
  33.4 1.7 %copy-start = (bf16[8,1024,128]{2,1,0:T(8,128)(2,1)S(1)}, bf16[8,1024,128]{2,1,0:T(8,128)(2,1)}, u32[]{:S(2)}) copy-start(bf16[8,1024,128]{2,1,0:T(8,128)(2,1)} %left.7) | copy-start | bytes 6291460
  39.3 2.0 %collective-permute-start.13 = (bf16[32,7680]{1,0:T(8,128)(2,1)S(1)}, bf16[32,7680]{1,0:T(8,128)(2,1)S(1)}, u32[]{:S(2)}, u32[]{:S(2)}) collective-permute-start(bf16[32,7680]{1,0:T(8,128)(2,1)S(1)} %get-tuple-element.84), channel_id=1, source_target_pairs={{0,4},{1,5},{2,6},{3,7},{4,0},{5,1},{6,2},{7,3},{8,12},{9,13},{10,... | collective-permute-start | bytes 1474568 | tf_op jit(solution)/shard_map/ppermute | solution.py:234
  41.4 15.6 %copy-start.1 = (bf16[1,8,256,128]{3,2,1,0:T(8,128)(2,1)S(1)}, bf16[1,8,256,128]{3,2,1,0:T(8,128)(2,1)}, u32[]{:S(2)}) copy-start(bf16[1,8,256,128]{3,2,1,0:T(8,128)(2,1)} %param.15) | copy-start | bytes 1572868
  41.7 4.6 %collective-permute-start.14 = (bf16[32,1280]{1,0:T(8,128)(2,1)S(1)}, bf16[32,1280]{1,0:T(8,128)(2,1)S(1)}, u32[]{:S(2)}, u32[]{:S(2)}) collective-permute-start(bf16[32,1280]{1,0:T(8,128)(2,1)S(1)} %pad_maximum_fusion.5.lead_in), channel_id=1, source_target_pairs={{0,8},{1,9},{2,10},{3,11},{4,12},{5,13},{6,14},{7,15},{8,0},{9,1},... | collective-permute-start | bytes 245768 | tf_op jit(solution)/shard_map/ppermute | solution.py:234
  42.0 6.4 %collective-permute-start.17 = (bf16[32,1536]{1,0:T(8,128)(2,1)S(1)}, bf16[32,1536]{1,0:T(8,128)(2,1)S(1)}, u32[]{:S(2)}, u32[]{:S(2)}) collective-permute-start(bf16[32,1536]{1,0:T(8,128)(2,1)S(1)} %behind.5.refs_0_), channel_id=1, source_target_pairs={{0,32},{1,33},{2,34},{3,35},{4,36},{5,37},{6,38},{7,39},{8,40},{9,... | collective-permute-start | bytes 294920 | tf_op jit(solution)/shard_map/ppermute | solution.py:234
  46.4 5.6 %collective-permute-start.15 = (bf16[32,1024]{1,0:T(8,128)(2,1)S(1)}, bf16[32,1024]{1,0:T(8,128)(2,1)S(1)}, u32[]{:S(2)}, u32[]{:S(2)}) collective-permute-start(bf16[32,1024]{1,0:T(8,128)(2,1)S(1)} %pad_maximum_fusion.7.lead_in), channel_id=1, source_target_pairs={{0,24},{1,25},{2,26},{3,27},{4,28},{5,29},{6,30},{7,31},{8,16},{9,... | collective-permute-start | bytes 196616 | tf_op jit(solution)/shard_map/ppermute | solution.py:234
  48.4 10.3 %collective-permute-start.21 = (bf16[32,1536]{1,0:T(8,128)(2,1)S(1)}, bf16[32,1536]{1,0:T(8,128)(2,1)S(1)}, u32[]{:S(2)}, u32[]{:S(2)}) collective-permute-start(bf16[32,1536]{1,0:T(8,128)(2,1)S(1)} %behind.6), channel_id=1, source_target_pairs={{0,64},{1,65},{2,66},{3,67},{4,68},{5,69},{6,70},{7,71},{8,72},{9,... | collective-permute-start | bytes 294920 | tf_op jit(solution)/shard_map/ppermute | solution.py:234
  51.8 7.0 %collective-permute-start.18 = (bf16[32,1024]{1,0:T(8,128)(2,1)S(1)}, bf16[32,1024]{1,0:T(8,128)(2,1)S(1)}, u32[]{:S(2)}, u32[]{:S(2)}) collective-permute-start(bf16[32,1024]{1,0:T(8,128)(2,1)S(1)} %pad_maximum_fusion.8.mine_in), channel_id=1, source_target_pairs={{0,4},{1,5},{2,6},{3,7},{4,0},{5,1},{6,2},{7,3},{8,12},{9,13},{10,... | collective-permute-start | bytes 196616 | tf_op jit(solution)/shard_map/ppermute | solution.py:234
  52.2 6.8 %collective-permute-start.20 = (bf16[32,768]{1,0:T(8,128)(2,1)S(1)}, bf16[32,768]{1,0:T(8,128)(2,1)S(1)}, u32[]{:S(2)}, u32[]{:S(2)}) collective-permute-start(bf16[32,768]{1,0:T(8,128)(2,1)S(1)} %pad_maximum_fusion.10.lead_in), channel_id=1, source_target_pairs={{0,96},{1,97},{2,98},{3,99},{4,100},{5,101},{6,102},{7,103},{8,104... | collective-permute-start | bytes 147464 | tf_op jit(solution)/shard_map/ppermute | solution.py:234
  54.2 5.0 %collective-permute-start.19 = (bf16[32,768]{1,0:T(8,128)(2,1)S(1)}, bf16[32,768]{1,0:T(8,128)(2,1)S(1)}, u32[]{:S(2)}, u32[]{:S(2)}) collective-permute-start(bf16[32,768]{1,0:T(8,128)(2,1)S(1)} %pad_maximum_fusion.10.lead_in), channel_id=1, source_target_pairs={{0,64},{1,65},{2,66},{3,67},{4,68},{5,69},{6,70},{7,71},{8,72},{9,... | collective-permute-start | bytes 147464 | tf_op jit(solution)/shard_map/ppermute | solution.py:234
  55.6 4.5 %collective-permute-start.16 = (bf16[32,768]{1,0:T(8,128)(2,1)S(1)}, bf16[32,768]{1,0:T(8,128)(2,1)S(1)}, u32[]{:S(2)}, u32[]{:S(2)}) collective-permute-start(bf16[32,768]{1,0:T(8,128)(2,1)S(1)} %pad_maximum_fusion.10.lead_in), channel_id=1, source_target_pairs={{0,32},{1,33},{2,34},{3,35},{4,36},{5,37},{6,38},{7,39},{8,40},{9,... | collective-permute-start | bytes 147464 | tf_op jit(solution)/shard_map/ppermute | solution.py:234
  58.9 1.5 %collective-permute-start.22 = (bf16[32,1536]{1,0:T(8,128)(2,1)S(1)}, bf16[32,1536]{1,0:T(8,128)(2,1)S(1)}, u32[]{:S(2)}, u32[]{:S(2)}) collective-permute-start(bf16[32,1536]{1,0:T(8,128)(2,1)S(1)} %get-tuple-element.50), channel_id=1, source_target_pairs={{0,4},{1,5},{2,6},{3,7},{4,0},{5,1},{6,2},{7,3},{8,12},{9,13},{10,... | collective-permute-start | bytes 294920 | tf_op jit(solution)/shard_map/ppermute | solution.py:234
  60.7 6.7 %collective-permute-start.23 = (bf16[32,256]{1,0:T(8,128)(2,1)S(1)}, bf16[32,256]{1,0:T(8,128)(2,1)S(1)}, u32[]{:S(2)}, u32[]{:S(2)}) collective-permute-start(bf16[32,256]{1,0:T(8,128)(2,1)S(1)} %pad_maximum_fusion.18), channel_id=1, source_target_pairs={{0,192},{1,193},{2,194},{3,195},{4,196},{5,197},{6,198},{7,199},{8... | collective-permute-start | bytes 49160 | tf_op jit(solution)/shard_map/ppermute | solution.py:234
